TPU v7x, 32 devices: a whole 2x2x4 slice. The times are simulated.
32 devices in a mesh: section: 2 (over x), dp: 16 (over z, y, core).
Axes of the slice: x: 2, y: 2, z: 4, core: 2. Of those that a mesh axis runs over, the one named last changes fastest.
Arguments:
- tokens: bfloat16 [2, 6144, 768], P(None, 'dp'), may hold values from -6 to 6
- cotangent: bfloat16 [2, 6144, 768], P(None, 'dp'), may hold values from -6 to 6
- bucket: int32 [2, 16], P(None, 'dp'), may hold values from 0 to 2
- lengths: int32 [2, 96], P(None, 'dp'), may hold values from 16 to 192, as said below
- w_qkv: float32 [2, 768, 2304], P('section', 'dp'), may hold values from -0.21875 to 0.21875
- bias_q: float32 [2, 768], P('section', 'dp'), may hold values from -3 to 3
- bias_v: float32 [2, 768], P('section', 'dp'), may hold values from -3 to 3
- w_out: float32 [2, 768, 768], P('section', 'dp'), may hold values from -0.625 to 0.625
- bias_out: float32 [2, 768], P('section', 'dp'), may hold values from -3 to 3
- gain_attn: float32 [2, 768], P('section', 'dp'), may hold values from 0.25 to 1.75
- shift_attn: float32 [2, 768], P('section', 'dp'), may hold values from -3 to 3
- w_up: float32 [2, 768, 3072], P('section', 'dp'), may hold values from -0.21875 to 0.21875
- bias_up: float32 [2, 3072], P('section', 'dp'), may hold values from -3 to 3
- w_down: float32 [2, 3072, 768], P('section', 'dp'), may hold values from -0.15625 to 0.15625
- bias_down: float32 [2, 768], P('section', 'dp'), may hold values from -3 to 3
- gain_ffn: float32 [2, 768], P('section', 'dp'), may hold values from 0.25 to 1.75
- shift_ffn: float32 [2, 768], P('section', 'dp'), may hold values from -3 to 3
Outputs:
- hidden_states: bfloat16 [2, 2, 6144, 768], P('section', None, 'dp')
- input_grads: bfloat16 [2, 2, 6144, 768], P('section', None, 'dp')
- grad_w_qkv: float32 [2, 768, 2304], P('section', 'dp')
- grad_bias_q: float32 [2, 768], P('section', 'dp')
- grad_bias_v: float32 [2, 768], P('section', 'dp')
- grad_w_out: float32 [2, 768, 768], P('section', 'dp')
- grad_bias_out: float32 [2, 768], P('section', 'dp')
- grad_gain_attn: float32 [2, 768], P('section', 'dp')
- grad_shift_attn: float32 [2, 768], P('section', 'dp')
- grad_w_up: float32 [2, 768, 3072], P('section', 'dp')
- grad_bias_up: float32 [2, 3072], P('section', 'dp')
- grad_w_down: float32 [2, 3072, 768], P('section', 'dp')
- grad_bias_down: float32 [2, 768], P('section', 'dp')
- grad_gain_ffn: float32 [2, 768], P('section', 'dp')
- grad_shift_ffn: float32 [2, 768], P('section', 'dp')
Inputs may be any that keep to these rules, and one draw needn't show every extreme that they name: `lengths`: valid length of each pair slot before it is clipped to its segment length; slots past a bucket's pair count are unused.
All inputs are finite; a program needn't handle non-finite values.
Results may differ from a plain program's by a relative error of at most 0.02.
Values may be sent and summed in bfloat16 or wider, within the bound.
No kernel may reach another device: no remote copies, remote signals or barrier semaphores. Data moves between devices by JAX's collectives and lax.ppermute only.
A program may use at most 320 MiB of HBM per device.

v0:
```python
import math

import jax
import jax.numpy as jnp
from jax import lax
from jax.sharding import PartitionSpec as P

HEADS = 12
SEGMENT = 64
PAIRS = 6
ROWS = 384


epsilon = 1e-06
masked_score = -1000000000.0


def passed_along(block, axis, distance):
    devices = range(lax.axis_size(axis))
    route = [(i - distance, i) for i in devices if i - distance in devices]
    return lax.ppermute(block, axis, route)


def mask_for(bucket_id, valid_lengths):
    segment_rows = SEGMENT * (bucket_id + 1)
    row_index = jnp.arange(ROWS, dtype=jnp.int32)
    pair_index = row_index // segment_rows
    position = row_index - pair_index * segment_rows
    clipped = jnp.minimum(valid_lengths, segment_rows)
    matches = pair_index[:, None] == jnp.arange(PAIRS, dtype=jnp.int32)[None, :]
    row_valid = jnp.sum(jnp.where(matches, clipped[None, :], 0), axis=1)
    return (pair_index[:, None] == pair_index[None, :]) & (position < row_valid)[None, :]


def slot_mask(bucket, lengths, picked):
    bucket_id = lax.dynamic_index_in_dim(bucket, picked, 0, keepdims=False)[0]
    valid_lengths = lax.dynamic_index_in_dim(lengths, picked, 0, keepdims=False)
    return mask_for(bucket_id, valid_lengths)


def norm_parts(values, gain, shift):
    centered = values - jnp.mean(values, axis=-1, keepdims=True)
    variance = jnp.mean(centered * centered, axis=-1, keepdims=True)
    inverse = lax.rsqrt(variance + epsilon)
    normed = centered * inverse
    return (normed * gain.astype(jnp.float32) + shift.astype(jnp.float32), normed, inverse)


def norm_back(upstream, normed, inverse, gain):
    scaled = upstream * gain.astype(jnp.float32)
    return inverse * (
        scaled
        - jnp.mean(scaled, axis=-1, keepdims=True)
        - normed * jnp.mean(scaled * normed, axis=-1, keepdims=True)
    )


def forward(inputs, params, allowed):
    (
        w_qkv,
        bias_q,
        bias_v,
        w_out,
        bias_out,
        gain_attn,
        shift_attn,
        w_up,
        bias_up,
        w_down,
        bias_down,
        gain_ffn,
        shift_ffn,
    ) = params
    row_count, model_width = inputs.shape
    head_dim = model_width // HEADS
    scale = 1.0 / math.sqrt(head_dim)
    bias_all = jnp.concatenate([bias_q, jnp.zeros_like(bias_q), bias_v]).astype(jnp.float32)
    qkv = (jnp.dot(inputs, w_qkv, preferred_element_type=jnp.float32) + bias_all).astype(
        jnp.bfloat16
    )
    queries = qkv[:, :model_width].reshape(row_count, HEADS, head_dim)
    keys = qkv[:, model_width : 2 * model_width].reshape(row_count, HEADS, head_dim)
    values = qkv[:, 2 * model_width :].reshape(row_count, HEADS, head_dim)
    scores = jnp.einsum("qhd,khd->hqk", queries, keys, preferred_element_type=jnp.float32) * scale
    scores = jnp.where(allowed[None], scores, masked_score)
    probs = jax.nn.softmax(scores, axis=-1)
    probs_low = probs.astype(jnp.bfloat16)
    context = jnp.einsum("hqk,khd->qhd", probs_low, values, preferred_element_type=jnp.float32)
    context = context.reshape(row_count, model_width).astype(jnp.bfloat16)
    first_sum = (
        inputs.astype(jnp.float32)
        + jnp.dot(context, w_out, preferred_element_type=jnp.float32)
        + bias_out.astype(jnp.float32)
    )
    hidden, normed_one, inverse_one = norm_parts(first_sum, gain_attn, shift_attn)
    hidden_low = hidden.astype(jnp.bfloat16)
    pre = jnp.dot(hidden_low, w_up, preferred_element_type=jnp.float32) + bias_up.astype(
        jnp.float32
    )
    active = jax.nn.gelu(pre, approximate=False).astype(jnp.bfloat16)
    second_sum = (
        hidden
        + jnp.dot(active, w_down, preferred_element_type=jnp.float32)
        + bias_down.astype(jnp.float32)
    )
    output, normed_two, inverse_two = norm_parts(second_sum, gain_ffn, shift_ffn)
    saved = (
        queries,
        keys,
        values,
        probs,
        probs_low,
        context,
        normed_one,
        inverse_one,
        hidden_low,
        pre,
        active,
        normed_two,
        inverse_two,
    )
    return (output, saved)


def back_ffn(upstream, saved, params):
    (
        queries,
        keys,
        values,
        probs,
        probs_low,
        context,
        normed_one,
        inverse_one,
        hidden_low,
        pre,
        active,
        normed_two,
        inverse_two,
    ) = saved
    gain_attn = params[5]
    w_up = params[7]
    w_down = params[9]
    gain_ffn = params[11]
    outer = upstream.astype(jnp.float32)
    d_gain_ffn = jnp.sum(outer * normed_two, axis=0)
    d_shift_ffn = jnp.sum(outer, axis=0)
    d_second = norm_back(outer, normed_two, inverse_two, gain_ffn)
    d_ffn = d_second.astype(jnp.bfloat16)
    d_bias_down = jnp.sum(d_ffn.astype(jnp.float32), axis=0)
    d_w_down = jnp.einsum("rf,rd->fd", active, d_ffn, preferred_element_type=jnp.float32)
    d_active = jnp.einsum("rd,fd->rf", d_ffn, w_down, preferred_element_type=jnp.float32)
    d_pre = jax.vjp(lambda values_in: jax.nn.gelu(values_in, approximate=False), pre)[1](d_active)[
        0
    ]
    d_pre = d_pre.astype(jnp.bfloat16)
    d_bias_up = jnp.sum(d_pre.astype(jnp.float32), axis=0)
    d_w_up = jnp.einsum("rd,rf->df", hidden_low, d_pre, preferred_element_type=jnp.float32)
    d_hidden = d_second + jnp.einsum("rf,df->rd", d_pre, w_up, preferred_element_type=jnp.float32)
    d_gain_attn = jnp.sum(d_hidden * normed_one, axis=0)
    d_shift_attn = jnp.sum(d_hidden, axis=0)
    d_first = norm_back(d_hidden, normed_one, inverse_one, gain_attn)
    late_grads = (
        d_gain_attn,
        d_shift_attn,
        d_w_up,
        d_bias_up,
        d_w_down,
        d_bias_down,
        d_gain_ffn,
        d_shift_ffn,
    )
    return (d_first, late_grads)


def back_attn(inputs, d_first, saved, params):
    (
        queries,
        keys,
        values,
        probs,
        probs_low,
        context,
        normed_one,
        inverse_one,
        hidden_low,
        pre,
        active,
        normed_two,
        inverse_two,
    ) = saved
    w_qkv = params[0]
    w_out = params[3]
    row_count, model_width = inputs.shape
    head_dim = model_width // HEADS
    scale = 1.0 / math.sqrt(head_dim)
    d_branch = d_first.astype(jnp.bfloat16)
    d_bias_out = jnp.sum(d_branch.astype(jnp.float32), axis=0)
    d_w_out = jnp.einsum("rc,rd->cd", context, d_branch, preferred_element_type=jnp.float32)
    d_context = jnp.einsum("rd,cd->rc", d_branch, w_out, preferred_element_type=jnp.float32)
    d_context = d_context.astype(jnp.bfloat16).reshape(row_count, HEADS, head_dim)
    d_probs = jnp.einsum("qhd,khd->hqk", d_context, values, preferred_element_type=jnp.float32)
    d_values = jnp.einsum("hqk,qhd->khd", probs_low, d_context, preferred_element_type=jnp.float32)
    d_scores = probs * (d_probs - jnp.sum(probs * d_probs, axis=-1, keepdims=True))
    d_scores = d_scores.astype(jnp.bfloat16)
    d_queries = (
        jnp.einsum("hqk,khd->qhd", d_scores, keys, preferred_element_type=jnp.float32) * scale
    )
    d_keys = (
        jnp.einsum("hqk,qhd->khd", d_scores, queries, preferred_element_type=jnp.float32) * scale
    )
    d_qkv = jnp.concatenate(
        [
            d_queries.reshape(row_count, model_width),
            d_keys.reshape(row_count, model_width),
            d_values.reshape(row_count, model_width),
        ],
        axis=1,
    ).astype(jnp.bfloat16)
    d_bias_q = jnp.sum(d_qkv[:, :model_width].astype(jnp.float32), axis=0)
    d_bias_v = jnp.sum(d_qkv[:, 2 * model_width :].astype(jnp.float32), axis=0)
    d_w_qkv = jnp.einsum("rd,re->de", inputs, d_qkv, preferred_element_type=jnp.float32)
    input_grad = d_first + jnp.einsum("re,de->rd", d_qkv, w_qkv, preferred_element_type=jnp.float32)
    early_grads = (d_w_qkv, d_bias_q, d_bias_v, d_w_out, d_bias_out)
    return (input_grad, early_grads)


def backward(inputs, upstream, params, allowed):
    output, saved = forward(inputs, params, allowed)
    d_first, late_grads = back_ffn(upstream, saved, params)
    input_grad, early_grads = back_attn(inputs, d_first, saved, params)
    return (input_grad, early_grads + late_grads)


def on_device(
    tokens,
    cotangent,
    bucket,
    lengths,
    w_qkv,
    bias_q,
    bias_v,
    w_out,
    bias_out,
    gain_attn,
    shift_attn,
    w_up,
    bias_up,
    w_down,
    bias_down,
    gain_ffn,
    shift_ffn,
):
    gathered = (
        lax.all_gather(w_qkv.astype(jnp.bfloat16), "dp", axis=1, tiled=True),
        lax.all_gather(bias_q.astype(jnp.bfloat16), "dp", axis=1, tiled=True),
        lax.all_gather(bias_v.astype(jnp.bfloat16), "dp", axis=1, tiled=True),
        lax.all_gather(w_out.astype(jnp.bfloat16), "dp", axis=1, tiled=True),
        lax.all_gather(bias_out.astype(jnp.bfloat16), "dp", axis=1, tiled=True),
        lax.all_gather(gain_attn.astype(jnp.bfloat16), "dp", axis=1, tiled=True),
        lax.all_gather(shift_attn.astype(jnp.bfloat16), "dp", axis=1, tiled=True),
        lax.all_gather(w_up.astype(jnp.bfloat16), "dp", axis=1, tiled=True),
        lax.all_gather(bias_up.astype(jnp.bfloat16), "dp", axis=1, tiled=True),
        lax.all_gather(w_down.astype(jnp.bfloat16), "dp", axis=1, tiled=True),
        lax.all_gather(bias_down.astype(jnp.bfloat16), "dp", axis=1, tiled=True),
        lax.all_gather(gain_ffn.astype(jnp.bfloat16), "dp", axis=1, tiled=True),
        lax.all_gather(shift_ffn.astype(jnp.bfloat16), "dp", axis=1, tiled=True),
    )
    params = tuple((member[0] for member in gathered))
    section_id = lax.axis_index("section")
    micro_count = tokens.shape[0]
    row_count = tokens.shape[1]
    model_width = tokens.shape[2]
    received = jnp.zeros((row_count, model_width), jnp.bfloat16)
    layer_inputs = []
    layer_outputs = []
    for step_index in range(micro_count + 1):
        offset = step_index - section_id
        running = (offset >= 0) & (offset < micro_count)
        picked = jnp.clip(offset, 0, micro_count - 1)
        allowed = slot_mask(bucket, lengths, picked)
        incoming = jnp.where(section_id == 0, tokens[min(step_index, micro_count - 1)], received)
        produced = lax.cond(
            running,
            lambda values_in: forward(values_in, params, allowed)[0],
            lambda values_in: jnp.zeros(values_in.shape, jnp.float32),
            incoming,
        ).astype(jnp.bfloat16)
        layer_inputs.append(incoming)
        layer_outputs.append(produced)
        if step_index < micro_count:
            received = passed_along(produced, "section", 1)
    hidden_states = jnp.stack(
        [
            jnp.where(section_id == 0, layer_outputs[micro_index], layer_outputs[micro_index + 1])
            for micro_index in range(micro_count)
        ]
    )[None]
    section_inputs = jnp.stack(
        [
            jnp.where(section_id == 0, layer_inputs[micro_index], layer_inputs[micro_index + 1])
            for micro_index in range(micro_count)
        ]
    )
    zero_grads = tuple((jnp.zeros(param.shape, jnp.float32) for param in params))
    totals = zero_grads
    results = None
    back_received = jnp.zeros((row_count, model_width), jnp.bfloat16)
    grad_outputs = []
    for step_index in range(micro_count + 1):
        offset = step_index - 1 + section_id
        running = (offset >= 0) & (offset < micro_count)
        picked = jnp.clip(offset, 0, micro_count - 1)
        allowed = slot_mask(bucket, lengths, picked)
        upstream = jnp.where(
            section_id == 1, cotangent[min(step_index, micro_count - 1)], back_received
        )
        section_input = lax.dynamic_index_in_dim(section_inputs, picked, 0, keepdims=False)
        input_grad, grads = lax.cond(
            running,
            lambda: backward(section_input, upstream, params, allowed),
            lambda: (jnp.zeros((row_count, model_width), jnp.float32), zero_grads),
        )
        totals = tuple((total + grad for total, grad in zip(totals, grads)))
        input_low = input_grad.astype(jnp.bfloat16)
        grad_outputs.append(input_low)
        if step_index < micro_count:
            back_received = passed_along(input_low, "section", -1)
    input_grads = jnp.stack(
        [
            jnp.where(section_id == 0, grad_outputs[micro_index + 1], grad_outputs[micro_index])
            for micro_index in range(micro_count)
        ]
    )[None]
    (
        g_qkv,
        g_bias_q,
        g_bias_v,
        g_out,
        g_bias_out,
        g_gain_attn,
        g_shift_attn,
        g_up,
        g_bias_up,
        g_down,
        g_bias_down,
        g_gain_ffn,
        g_shift_ffn,
    ) = totals
    results = (
        lax.psum_scatter(g_qkv[None], "dp", scatter_dimension=1, tiled=True),
        lax.psum_scatter(g_bias_q[None], "dp", scatter_dimension=1, tiled=True),
        lax.psum_scatter(g_bias_v[None], "dp", scatter_dimension=1, tiled=True),
        lax.psum_scatter(g_out[None], "dp", scatter_dimension=1, tiled=True),
        lax.psum_scatter(g_bias_out[None], "dp", scatter_dimension=1, tiled=True),
        lax.psum_scatter(g_gain_attn[None], "dp", scatter_dimension=1, tiled=True),
        lax.psum_scatter(g_shift_attn[None], "dp", scatter_dimension=1, tiled=True),
        lax.psum_scatter(g_up[None], "dp", scatter_dimension=1, tiled=True),
        lax.psum_scatter(g_bias_up[None], "dp", scatter_dimension=1, tiled=True),
        lax.psum_scatter(g_down[None], "dp", scatter_dimension=1, tiled=True),
        lax.psum_scatter(g_bias_down[None], "dp", scatter_dimension=1, tiled=True),
        lax.psum_scatter(g_gain_ffn[None], "dp", scatter_dimension=1, tiled=True),
        lax.psum_scatter(g_shift_ffn[None], "dp", scatter_dimension=1, tiled=True),
    )
    return (
        hidden_states,
        input_grads,
        results[0],
        results[1],
        results[2],
        results[3],
        results[4],
        results[5],
        results[6],
        results[7],
        results[8],
        results[9],
        results[10],
        results[11],
        results[12],
    )


def solution(mesh):
    return jax.shard_map(
        on_device,
        mesh=mesh,
        in_specs=(
            P(None, "dp", None),
            P(None, "dp", None),
            P(None, "dp"),
            P(None, "dp"),
            P("section", "dp", None),
            P("section", "dp"),
            P("section", "dp"),
            P("section", "dp", None),
            P("section", "dp"),
            P("section", "dp"),
            P("section", "dp"),
            P("section", "dp", None),
            P("section", "dp"),
            P("section", "dp", None),
            P("section", "dp"),
            P("section", "dp"),
            P("section", "dp"),
        ),
        out_specs=(
            P("section", None, "dp", None),
            P("section", None, "dp", None),
            P("section", "dp", None),
            P("section", "dp"),
            P("section", "dp"),
            P("section", "dp", None),
            P("section", "dp"),
            P("section", "dp"),
            P("section", "dp"),
            P("section", "dp", None),
            P("section", "dp"),
            P("section", "dp", None),
            P("section", "dp"),
            P("section", "dp"),
            P("section", "dp"),
        ),
        check_vma=False,
    )
```

profile of v0, /device:TPU:0, one launch (start us, length us, event | category | flops | bytes accessed | tf_op | source)
XLA Modules:
  0.0 1628.3 jit_solution(15478068984643779348)
XLA Ops:
  24.7 63.6 %all-reduce.9 = (bf16[768]{0:T(1024)(128)(2,1)}, bf16[768]{0:T(1024)(128)(2,1)}, bf16[768]{0:T(1024)(128)(2,1)}, bf16[768]{0:T(1024)(128)(2,1)}, bf16[768]{0:T(1...) all-reduce(bf16[768]{0:T(1024)(128)(2,1)S(1)} %dynamic-update-slice, ...), channel_id=1, replica_groups=mesh['section'=2,'dp'=16] {'dp'}, use_global_device_ids=true, to_apply=%add | all-reduce | flops 9216 | bytes 36864 | tf_op jit(solution)/shard_map/squeeze | solution.py:269
  90.1 11.2 all-gather.5.cloned.1.call-done
  101.2 55.3 %all-gather.9.cloned.1.call-done = bf16[1,768,3072]{2,1,0:T(8,128)(2,1)} async-done(((bf16[1,48,3072]{2,1,0:T(8,128)(2,1)}), bf16[1,768,3072]{2,1,0:T(8,128)(2,1)}) %all-gather.9.cloned.1.call-update) | async-done | bytes 4718608 | tf_op jit(solution)/shard_map/all_gather | solution.py:262
  156.5 54.7 %all-gather.11.cloned.1.call-done = bf16[1,3072,768]{2,1,0:T(8,128)(2,1)} async-done(((bf16[1,192,768]{2,1,0:T(8,128)(2,1)}), bf16[1,3072,768]{2,1,0:T(8,128)(2,1)}) %all-gather.11.cloned.1.call-update) | async-done | bytes 4718608 | tf_op jit(solution)/shard_map/all_gather | solution.py:264
  213.6 53.8 %conditional.6 = (bf16[384,768]{1,0:T(8,128)(2,1)S(1)}) conditional(s32[]{:T(128)} %convert_element_type.993, () %tuple.128, (bf16[384,768]{1,0:T(8,128)(2,1)S(1)}, bf16[768,2304]{1,0:T(8,128)(2,1)}, bf16[768]{0:T(1024)(128)(2,1)}, bf16[768]{0:T(1024)(128)(2,1)}, s32[2,1]{0,1:T(1,128)S(1)}, /*index=5*/s32[384]{0:T(512)S(1)}, ...), branch_computations={%region_0.1_spmd, %region_1.0_spmd.clone.clone} | conditional | flops 5987634176 | bytes 58928212 | solution.py:283
  226.4 3.5 fusion.12
  234.5 7.0 fusion.401
  241.5 3.8 fusion.21
  247.3 17.7 %fusion.403 = (f32[384]{0:T(512)}, f32[384,768]{1,0:T(8,128)S(1)}) fusion(f32[768]{0:T(1024)} %convert_element_type.1155, bf16[3072,768]{1,0:T(8,128)(2,1)} %get-tuple-element.3162, bf16[768,3072]{1,0:T(8,128)(2,1)} %get-tuple-element.3160, f32[3072]{0:T(1024)} %convert_element_type.1153, f32[384,768]{1,0:T(8,128)S(1)} %get-tuple-element.3634, ...), kind=kOutput, calls=%fused_computation.668 | convolution fusion | flops 3705273856 | bytes 11822592 | tf_op jit(solution)/shard_map/cond/branch_1_fun/dot_general | solution.py:103
  268.8 13.2 collective-permute-done
  283.1 55.5 %conditional.7 = (bf16[384,768]{1,0:T(8,128)(2,1)S(1)}) conditional(s32[]{:T(128)} %convert_element_type.1007, () %tuple.130, (bf16[384,768]{1,0:T(8,128)(2,1)}, bf16[768,2304]{1,0:T(8,128)(2,1)}, bf16[768]{0:T(1024)(128)(2,1)}, bf16[768]{0:T(1024)(128)(2,1)}, s32[2,1]{0,1:T(1,128)}, /*index=5*/s32[384]{0:T(512)S(1)}, ...), branch_computations={%region_9.10_spmd, %region_10.18_spmd.clone.clone} | conditional | flops 5987634176 | bytes 54209564 | solution.py:283
  296.9 3.7 fusion.80
  305.3 7.0 fusion.408
  312.3 3.8 fusion.89
  319.1 17.6 %fusion.410 = (f32[384]{0:T(512)}, f32[384,768]{1,0:T(8,128)S(1)}) fusion(f32[768]{0:T(1024)} %convert_element_type.1170, bf16[3072,768]{1,0:T(8,128)(2,1)} %get-tuple-element.3230, bf16[768,3072]{1,0:T(8,128)(2,1)} %get-tuple-element.3228, f32[3072]{0:T(1024)} %convert_element_type.1168, f32[384,768]{1,0:T(8,128)S(1)} %get-tuple-element.3643, ...), kind=kOutput, calls=%fused_computation.673 | convolution fusion | flops 3705273856 | bytes 11822592 | tf_op jit(solution)/shard_map/cond/branch_1_fun/dot_general | solution.py:103
  338.7 4.8 collective-permute-start.1
  343.5 12.4 collective-permute-done.1
  360.2 21.2 %conditional.9 = (f32[768,2304]{1,0:T(8,128)}, f32[768]{0:T(1024)S(1)}, f32[768]{0:T(1024)S(1)}, f32[768,768]{1,0:T(8,128)}, f32[768]{0:T(1024)S(1)}, /*index=5*...) conditional(s32[]{:T(128)} %convert_element_type.1010, ...), branch_computations={%region_27.28_spmd, %region_28.50_spmd.clone.clone} | conditional | flops 17827745792 | bytes 348632768 | solution.py:319
  366.2 3.3 broadcast_in_dim.402
  369.4 4.1 broadcast_in_dim.406
  373.6 4.8 broadcast_in_dim.404
  385.6 97.6 %collective-permute-done.2 = bf16[384,768]{1,0:T(8,128)(2,1)S(1)} collective-permute-done((bf16[384,768]{1,0:T(8,128)(2,1)}, bf16[384,768]{1,0:T(8,128)(2,1)S(1)}, u32[]{:S(2)}, u32[]{:S(2)}) %collective-permute-start.2) | collective-permute-done | bytes 589856 | tf_op jit(solution)/shard_map/ppermute | solution.py:21
  483.2 103.8 %conditional.10 = (f32[768,2304]{1,0:T(8,128)}, f32[768]{0:T(1024)S(1)}, f32[768]{0:T(1024)S(1)}, f32[768,768]{1,0:T(8,128)}, f32[768]{0:T(1024)S(1)}, /*index=5...) conditional(s32[]{:T(128)} %convert_element_type.1009, ...), branch_computations={%region_50.51_spmd, %region_51.73_spmd.clone.clone} | conditional | flops 17827745792 | bytes 353938176 | solution.py:319
  496.2 3.7 fusion.275
  503.7 6.3 fusion.427
  510.0 3.8 fusion.291
  515.0 15.2 multiply_convert_fusion.3
  535.0 6.7 convert_reduce_fusion.6
  541.7 2.9 multiply_reduce_fusion.13
  549.3 4.5 fusion.294
  556.9 5.4 fusion.327
  562.3 5.5 fusion.319
  567.8 4.0 multiply_reduce_fusion.12
  571.8 4.2 multiply_convert_fusion.2
  582.0 4.9 fusion.302
  588.3 14.3 collective-permute-done.3
  602.6 101.9 %conditional.11 = (f32[768,2304]{1,0:T(8,128)}, f32[768]{0:T(1024)S(1)}, f32[768]{0:T(1024)S(1)}, f32[768,768]{1,0:T(8,128)}, f32[768]{0:T(1024)S(1)}, /*index=5...) conditional(s32[]{:T(128)} %convert_element_type.1011, ...), branch_computations={%region_73.74_spmd, %region_74.96_spmd.clone.clone} | conditional | flops 17827745792 | bytes 356359104 | solution.py:319
  615.8 3.7 fusion.338
  620.7 6.2 fusion.432
  626.9 3.8 fusion.354
  631.8 15.2 multiply_convert_fusion.5
  651.9 6.7 convert_reduce_fusion.12
  666.2 4.5 fusion.357
  673.8 5.4 fusion.390
  679.3 5.6 fusion.382
  684.9 4.1 multiply_reduce_fusion.18
  689.0 4.2 multiply_convert_fusion.4
  699.2 5.0 fusion.365
  719.2 5.0 add_bitcast_fusion.3
  724.3 11.3 add_bitcast_fusion.2
  735.7 14.8 add_bitcast_fusion.1
  750.6 13.9 add_bitcast_fusion
  773.6 44.3 %reduce-scatter.42.cloned.1.call-done = f32[48,1]{1,0:T(8,128)} async-done(((f32[768,1]{1,0:T(8,128)}), f32[48,1]{1,0:T(8,128)}) %reduce-scatter.42.cloned.1.call-update) | async-done | bytes 208
  819.2 56.9 %reduce-scatter.44.cloned.1.call-done = f32[48,1]{1,0:T(8,128)} async-done(((f32[768,1]{1,0:T(8,128)}), f32[48,1]{1,0:T(8,128)}) %reduce-scatter.44.cloned.1.call-update) | async-done | bytes 208
  877.4 57.2 %reduce-scatter.46.cloned.1.call-done = f32[48,1]{1,0:T(8,128)} async-done(((f32[768,1]{1,0:T(8,128)}), f32[48,1]{1,0:T(8,128)}) %reduce-scatter.46.cloned.1.call-update) | async-done | bytes 208
  935.9 56.8 %reduce-scatter.48.cloned.1.call-done = f32[48,1]{1,0:T(8,128)} async-done(((f32[768,1]{1,0:T(8,128)}), f32[48,1]{1,0:T(8,128)}) %reduce-scatter.48.cloned.1.call-update) | async-done | bytes 208
  994.0 57.0 %reduce-scatter.52.cloned.1.call-done = f32[48,1]{1,0:T(8,128)} async-done(((f32[768,1]{1,0:T(8,128)}), f32[48,1]{1,0:T(8,128)}) %reduce-scatter.52.cloned.1.call-update) | async-done | bytes 208
  1052.3 56.8 %reduce-scatter.54.cloned.1.call-done = f32[48,1]{1,0:T(8,128)} async-done(((f32[768,1]{1,0:T(8,128)}), f32[48,1]{1,0:T(8,128)}) %reduce-scatter.54.cloned.1.call-update) | async-done | bytes 208
  1110.4 57.1 %reduce-scatter.56.cloned.1.call-done = f32[48,1]{1,0:T(8,128)} async-done(((f32[768,1]{1,0:T(8,128)}), f32[48,1]{1,0:T(8,128)}) %reduce-scatter.56.cloned.1.call-update) | async-done | bytes 208
  1168.8 60.9 %reduce-scatter.50.cloned.1.call-done = f32[192,1]{1,0:T(8,128)} async-done(((f32[3072,1]{1,0:T(8,128)}), f32[192,1]{1,0:T(8,128)}) %reduce-scatter.50.cloned.1.call-update) | async-done | bytes 784
  1231.2 65.1 %reduce-scatter.34.cloned.1.call-done = f32[1,48,768]{2,1,0:T(8,128)} async-done(((f32[1,768,768]{2,1,0:T(8,128)}), f32[1,48,768]{2,1,0:T(8,128)}) %reduce-scatter.34.cloned.1.call-update) | async-done | bytes 147472 | tf_op jit(solution)/shard_map/reduce_scatter | solution.py:354
  1296.4 93.5 %reduce-scatter.32.cloned.1.call-done = f32[1,48,2304]{2,1,0:T(8,128)} async-done(((f32[1,768,2304]{2,1,0:T(8,128)}), f32[1,48,2304]{2,1,0:T(8,128)}) %reduce-scatter.32.cloned.1.call-update) | async-done | bytes 442384 | tf_op jit(solution)/shard_map/reduce_scatter | solution.py:351
  1389.9 116.0 %reduce-scatter.36.cloned.1.call-done = f32[1,48,3072]{2,1,0:T(8,128)} async-done(((f32[1,768,3072]{2,1,0:T(8,128)}), f32[1,48,3072]{2,1,0:T(8,128)}) %reduce-scatter.36.cloned.1.call-update) | async-done | bytes 589840 | tf_op jit(solution)/shard_map/reduce_scatter | solution.py:358
  1505.9 115.6 %reduce-scatter.38.cloned.1.call-done = f32[1,192,768]{2,1,0:T(8,128)} async-done(((f32[1,3072,768]{2,1,0:T(8,128)}), f32[1,192,768]{2,1,0:T(8,128)}) %reduce-scatter.38.cloned.1.call-update) | async-done | bytes 589840 | tf_op jit(solution)/shard_map/reduce_scatter | solution.py:360
  (538 shorter events, 187.8 us)
Async XLA Ops:
  7.2 206.4 %copy-start.135 = (s32[2,6]{1,0:T(2,128)S(1)}, s32[2,6]{1,0:T(2,128)}, u32[]{:S(2)}) copy-start(s32[2,6]{1,0:T(2,128)} %param.32) | copy-start | bytes 148
  7.2 206.4 %copy-start.108 = (s32[2,1]{0,1:T(1,128)S(1)}, s32[2,1]{0,1:T(1,128)}, u32[]{:S(2)}) copy-start(s32[2,1]{0,1:T(1,128)} %param.31) | copy-start | bytes 28
  7.2 82.9 %all-gather.7.cloned.1.call-start = ((), (), s32[]{:S(2)}) async-start(), calls=%async_computation.14 | async-start | bytes 1253376 | tf_op jit(solution)/shard_map/all_gather | solution.py:258
  8.8 92.4 %all-gather.5.cloned.1.call-start = ((), (), s32[]{:S(2)}) async-start(), calls=%async_computation.13 | async-start | bytes 3760128 | tf_op jit(solution)/shard_map/all_gather | solution.py:255
  10.6 145.9 %all-gather.9.cloned.1.call-start = ((), (), s32[]{:S(2)}) async-start(), calls=%async_computation.15 | async-start | bytes 5013504 | tf_op jit(solution)/shard_map/all_gather | solution.py:262
  12.5 198.7 %all-gather.11.cloned.1.call-start = ((), (), s32[]{:S(2)}) async-start(), calls=%async_computation.16 | async-start | bytes 5013504 | tf_op jit(solution)/shard_map/all_gather | solution.py:264
  14.4 757.9 %reduce-scatter.40.cloned.1.call-start = ((), (), s32[]{:S(2)}) async-start(), calls=%async_computation.21 | async-start | bytes 417792
  88.9 271.1 %copy-start.82 = (s32[384]{0:T(512)}, s32[384]{0:T(512)S(1)}, u32[]{:S(2)}) copy-start(s32[384]{0:T(512)S(1)} %iota_sign_fusion) | copy-start | bytes 4612
  213.6 68.4 %copy-start.15 = (bf16[2,384,768]{2,1,0:T(8,128)(2,1)S(1)}, bf16[2,384,768]{2,1,0:T(8,128)(2,1)}, u32[]{:S(2)}) copy-start(bf16[2,384,768]{2,1,0:T(8,128)(2,1)} %param.29) | copy-start | bytes 3538948
  213.9 12.5 copy-start.56
  216.0 14.0 copy-start.104
  267.4 15.7 copy-start.42
  267.4 14.6 collective-permute-start
  286.5 10.4 copy-start.105
  338.6 21.4 %copy-start.44 = (bf16[384,768]{1,0:T(8,128)(2,1)}, bf16[384,768]{1,0:T(8,128)(2,1)S(1)}, u32[]{:S(2)}) copy-start(bf16[384,768]{1,0:T(8,128)(2,1)S(1)} %get-tuple-element.3797) | copy-start | bytes 1769476
  338.7 21.4 %copy-start = (bf16[1,768,768]{2,1,0:T(8,128)(2,1)S(1)}, bf16[1,768,768]{2,1,0:T(8,128)(2,1)}, u32[]{:S(2)}) copy-start(bf16[1,768,768]{2,1,0:T(8,128)(2,1)} %all-gather.7.cloned.1.call-done) | copy-start | bytes 3538948
  338.7 17.3 %collective-permute-start.1 = (bf16[384,768]{1,0:T(8,128)(2,1)S(1)}, bf16[384,768]{1,0:T(8,128)(2,1)S(1)}, u32[]{:S(2)}, u32[]{:S(2)}) collective-permute-start(bf16[384,768]{1,0:T(8,128)(2,1)S(1)} %get-tuple-element.3797), channel_id=1, source_target_pairs={{0,16},{1,17},{2,18},{3,19},{4,20},{5,21},{6,22},{7,23},{8,24},{9,... | collective-permute-start | bytes 1769480 | tf_op jit(solution)/shard_map/ppermute | solution.py:21
  383.2 100.0 %collective-permute-start.2 = (bf16[384,768]{1,0:T(8,128)(2,1)}, bf16[384,768]{1,0:T(8,128)(2,1)S(1)}, u32[]{:S(2)}, u32[]{:S(2)}) collective-permute-start(bf16[384,768]{1,0:T(8,128)(2,1)} %get-tuple-element.2609), channel_id=1, source_target_pairs={{16,0},{17,1},{18,2},{19,3},{20,4},{21,5},{22,6},{23,7},{24,8},{25... | collective-permute-start | bytes 1769480 | tf_op jit(solution)/shard_map/ppermute | solution.py:21
  385.6 97.6 %copy-start.10 = (bf16[384,768]{1,0:T(8,128)(2,1)}, bf16[384,768]{1,0:T(8,128)(2,1)S(1)}, u32[]{:S(2)}) copy-start(bf16[384,768]{1,0:T(8,128)(2,1)S(1)} %slice_bitcast_fusion) | copy-start | bytes 1769476
  483.2 13.1 copy-start.54
  502.3 7.7 copy-start.30
  513.8 16.3 %slice-start.14 = ((s8[4718592]{0:T(1024)(128)(4,1)}), s8[4194304]{0:T(1024)(128)(4,1)S(1)}, s32[]{:S(2)}) async-start(s8[4718592]{0:T(1024)(128)(4,1)} %bitcast.458), calls=%async_computation.44 | async-start | bytes 8388608 | tf_op jit(solution)/shard_map/cond
  514.6 30.0 %copy-start.86 = (f32[384]{0:T(512)}, f32[384]{0:T(512)S(1)}, u32[]{:S(2)}) copy-start(f32[384]{0:T(512)S(1)} %broadcast_multiply_fusion.17) | copy-start | bytes 4612 | tf_op jit(solution)/shard_map/cond
  514.9 29.7 %copy-start.92 = (f32[384]{0:T(512)}, f32[384]{0:T(512)S(1)}, u32[]{:S(2)}) copy-start(f32[384]{0:T(512)S(1)} %add_rsqrt_fusion.9) | copy-start | bytes 4612 | tf_op jit(solution)/shard_map/cond
  515.0 15.2 copy-start.141
  515.0 15.2 slice-start.15
  534.0 7.7 slice-start.8
  535.0 6.7 copy-start.18
  535.0 6.7 slice-start.9
  556.9 10.9 slice-start.2
  586.9 15.6 copy-start.121
  586.9 15.6 copy-start.123
  586.9 15.6 copy-start.124
  587.0 15.6 collective-permute-start.3
  602.8 16.8 %copy-start.52 = (bf16[384,768]{1,0:T(8,128)(2,1)}, bf16[384,768]{1,0:T(8,128)(2,1)S(1)}, u32[]{:S(2)}) copy-start(bf16[384,768]{1,0:T(8,128)(2,1)S(1)} %get-tuple-element.3514) | copy-start | bytes 1769476 | tf_op jit(solution)/shard_map/cond
  620.0 6.8 copy-start.31
  630.7 16.4 %copy-start.73 = (bf16[12,64,384]{2,1,0:T(8,128)(2,1)}, bf16[12,64,384]{2,1,0:T(8,128)(2,1)S(1)}, u32[]{:S(2)}) copy-start(bf16[12,64,384]{2,1,0:T(8,128)(2,1)S(1)} %fusion.354) | copy-start | bytes 1769476 | tf_op jit(solution)/shard_map/cond
  630.7 16.3 %slice-start.16 = ((s8[4718592]{0:T(1024)(128)(4,1)}), s8[4194304]{0:T(1024)(128)(4,1)S(1)}, s32[]{:S(2)}) async-start(s8[4718592]{0:T(1024)(128)(4,1)} %bitcast.460), calls=%async_computation.46 | async-start | bytes 8388608 | tf_op jit(solution)/shard_map/cond
  631.5 30.1 %copy-start.88 = (f32[384]{0:T(512)}, f32[384]{0:T(512)S(1)}, u32[]{:S(2)}) copy-start(f32[384]{0:T(512)S(1)} %broadcast_multiply_fusion.23) | copy-start | bytes 4612 | tf_op jit(solution)/shard_map/cond
  631.8 29.8 %copy-start.94 = (f32[384]{0:T(512)}, f32[384]{0:T(512)S(1)}, u32[]{:S(2)}) copy-start(f32[384]{0:T(512)S(1)} %add_rsqrt_fusion.11) | copy-start | bytes 4612 | tf_op jit(solution)/shard_map/cond
  631.8 15.3 copy-start.142
  631.8 15.3 slice-start.17
  650.9 7.7 slice-start.10
  651.9 6.7 copy-start.20
  651.9 6.7 slice-start.11
  673.8 11.1 slice-start.4
  704.5 10.2 copy-start.112
  704.5 10.2 copy-start.119
  704.5 11.2 copy-start.111
  704.5 11.2 copy-start.118
  704.5 12.3 copy-start.96
  704.5 12.3 copy-start.97
  706.2 111.7 %reduce-scatter.42.cloned.1.call-start = ((), (), s32[]{:S(2)}) async-start(), calls=%async_computation.22 | async-start | bytes 417792
  707.9 168.2 %reduce-scatter.44.cloned.1.call-start = ((), (), s32[]{:S(2)}) async-start(), calls=%async_computation.23 | async-start | bytes 417792
  709.6 225.0 %reduce-scatter.46.cloned.1.call-start = ((), (), s32[]{:S(2)}) async-start(), calls=%async_computation.24 | async-start | bytes 417792
  711.3 281.4 %reduce-scatter.48.cloned.1.call-start = ((), (), s32[]{:S(2)}) async-start(), calls=%async_computation.25 | async-start | bytes 417792
  713.0 338.0 %reduce-scatter.52.cloned.1.call-start = ((), (), s32[]{:S(2)}) async-start(), calls=%async_computation.27 | async-start | bytes 417792
  714.7 394.4 %reduce-scatter.54.cloned.1.call-start = ((), (), s32[]{:S(2)}) async-start(), calls=%async_computation.28 | async-start | bytes 417792
  715.7 451.8 %reduce-scatter.56.cloned.1.call-start = ((), (), s32[]{:S(2)}) async-start(), calls=%async_computation.29 | async-start | bytes 417792
  716.7 513.0 %reduce-scatter.50.cloned.1.call-start = ((), (), s32[]{:S(2)}) async-start(), calls=%async_computation.26 | async-start | bytes 1671168
  719.2 577.2 %reduce-scatter.34.cloned.1.call-start = ((), (), s32[]{:S(2)}) async-start(), calls=%async_computation.18 | async-start | bytes 2506752 | tf_op jit(solution)/shard_map/reduce_scatter | solution.py:354
  724.2 665.6 %reduce-scatter.32.cloned.1.call-start = ((), (), s32[]{:S(2)}) async-start(), calls=%async_computation.17 | async-start | bytes 7520256 | tf_op jit(solution)/shard_map/reduce_scatter | solution.py:351
  735.6 770.2 %reduce-scatter.36.cloned.1.call-start = ((), (), s32[]{:S(2)}) async-start(), calls=%async_computation.19 | async-start | bytes 10027008 | tf_op jit(solution)/shard_map/reduce_scatter | solution.py:358
  750.6 871.0 %reduce-scatter.38.cloned.1.call-start = ((), (), s32[]{:S(2)}) async-start(), calls=%async_computation.20 | async-start | bytes 10027008 | tf_op jit(solution)/shard_map/reduce_scatter | solution.py:360
  (81 other events, 274.8 us)
Sparse Core Ops, SparseCore 0:
  10.9 41.1 all-gather.6
  55.0 46.2 all-gather.4
  104.1 52.3 all-gather.8
  159.3 51.9 all-gather.10
  706.3 53.1 reduce-scatter.39
  763.3 54.5 reduce-scatter.41
  821.4 54.6 reduce-scatter.43
  880.0 54.5 reduce-scatter.45
  938.0 54.5 reduce-scatter.47
  996.4 54.5 reduce-scatter.51
  1054.5 54.5 reduce-scatter.53
  1112.9 54.5 reduce-scatter.55
  1171.2 58.4 reduce-scatter.49
  1234.4 61.9 reduce-scatter.33
  1300.8 89.0 reduce-scatter.31
  1395.0 110.8 reduce-scatter.35
  1510.4 111.0 reduce-scatter.37
where the time goes:
time: 1640 us; the launch traced here: 1630 us
  waiting for transfers between devices  1100 us (67%)
  matrix products  217 us (13%)
  other arithmetic  152 us (9%)
  local copies, waits for them, and re-layouts  64.1 us (4%)
  blocking collectives  63.6 us (4%)
    unnamed x26, waiting for transfers between devices  447 us
    ppermute x4, waiting for transfers between devices, passed_along(): return lax.ppermute(block, axis, route)  138 us
    reduce_scatter x1, waiting for transfers between devices, on_device(): lax.psum_scatter(g_up[None], 'dp', scatter_dimension=1, tiled=True)  116 us
    reduce_scatter x1, waiting for transfers between devices, on_device(): lax.psum_scatter(g_down[None], 'dp', scatter_dimension=1, tiled=True)  116 us
    reduce_scatter x1, waiting for transfers between devices, on_device(): lax.psum_scatter(g_qkv[None], 'dp', scatter_dimension=1, tiled=True)  93.5 us
    reduce_scatter x1, waiting for transfers between devices, on_device(): lax.psum_scatter(g_out[None], 'dp', scatter_dimension=1, tiled=True)  65.1 us
    squeeze x1, blocking collectives, on_device(): params = tuple((member[0] for member in gathered))  63.6 us
    all_gather x1, waiting for transfers between devices, on_device(): lax.all_gather(w_up.astype(jnp.bfloat16), 'dp', axis=1, tiled=True)  55.3 us
  transfers between devices with their start and end apart: 21, of which 19 were waited for; matrix products, arithmetic and copies ran while one was open for 6% of the time, Pallas kernels for 0%

commit v1 on v0

v1 whole, which is shorter than its diff:
```python
import functools

import jax
import jax.numpy as jnp
from jax import lax
from jax.experimental import pallas as pl
from jax.experimental.pallas import tpu as pltpu
from jax.sharding import PartitionSpec as P

HEADS = 12
SEGMENT = 64
PAIRS = 6
ROWS = 384
EPSILON = 1e-06
MASKED = -1000000000.0
LANES = 128
FF_TILE = 512
VMEM_LIMIT = 60 * 1024 * 1024
F32 = jnp.float32
BF16 = jnp.bfloat16

BIAS_Q, BIAS_K, BIAS_V, BIAS_OUT, GAIN_ATTN, SHIFT_ATTN, BIAS_DOWN, GAIN_FFN, SHIFT_FFN = range(9)
RUN, MICRO, SECTION, BUCKET, LENGTHS = range(5)

ANY = pl.BlockSpec(memory_space=pl.ANY)
WHOLE = pl.BlockSpec(memory_space=pltpu.VMEM)
SCALARS = pl.BlockSpec(memory_space=pltpu.SMEM)


def dot_nn(a, b):
    return lax.dot_general(a, b, (((1,), (0,)), ((), ())), preferred_element_type=F32)


def dot_nt(a, b):
    return lax.dot_general(a, b, (((1,), (1,)), ((), ())), preferred_element_type=F32)


def dot_tn(a, b):
    return lax.dot_general(a, b, (((0,), (0,)), ((), ())), preferred_element_type=F32)


class Copies:
    def __init__(self, sems):
        self.sems = sems
        self.next = 0

    def start(self, src, dst):
        copy = pltpu.make_async_copy(src, dst, self.sems.at[self.next])
        self.next += 1
        copy.start()
        return copy


def fetch_either(first, one, other, dst, sem):
    @pl.when(first)
    def _():
        pltpu.make_async_copy(one, dst, sem).start()

    @pl.when(jnp.logical_not(first))
    def _():
        pltpu.make_async_copy(other, dst, sem).start()

    return pltpu.make_async_copy(other, dst, sem)


def fold(values):
    rows, n = values.shape
    return jnp.sum(values.reshape(rows // 8, 8, n), axis=0)


def write_bias(info, bias, block, count):
    segment = (info[BUCKET] + 1) * SEGMENT
    per_block = jnp.where(info[BUCKET] == 0, block // SEGMENT, 1)
    k_row = lax.broadcasted_iota(jnp.int32, (block, block), 0)
    q_row = lax.broadcasted_iota(jnp.int32, (block, block), 1)

    def pair_of(row):
        return (row >= segment).astype(jnp.int32) + (row >= 2 * segment).astype(jnp.int32)

    k_pair = pair_of(k_row)
    same = k_pair == pair_of(q_row)
    position = k_row - k_pair * segment
    for at in range(count):
        valid = [
            jnp.minimum(info[LENGTHS + jnp.minimum(at * per_block + i, PAIRS - 1)], segment)
            for i in range(3)
        ]
        length = jnp.where(k_pair == 0, valid[0], jnp.where(k_pair == 1, valid[1], valid[2]))
        bias[at, :block, :block] = jnp.where(same & (position < length), 0.0, MASKED)


def half_masks():
    lane = lax.broadcasted_iota(jnp.int32, (1, LANES), 1)
    low = (lane < LANES // 2).astype(F32)
    return low.astype(BF16), (1.0 - low).astype(BF16)


def by_block(info, body):
    @pl.when(info[BUCKET] == 1)
    def _():
        body(2 * SEGMENT, ROWS // (2 * SEGMENT))

    @pl.when(info[BUCKET] != 1)
    def _():
        body(3 * SEGMENT, ROWS // (3 * SEGMENT))


def attention(info, qkv, context, lse, bias):
    width = context.shape[1]
    low, high = half_masks()

    def body(block, count):
        write_bias(info, bias, block, count)

        def pair_step(pair, carry):
            at_q = pl.multiple_of(pair * LANES, LANES)
            at_k = pl.multiple_of(width + pair * LANES, LANES)
            at_v = pl.multiple_of(2 * width + pair * LANES, LANES)
            is_low = lax.broadcasted_iota(jnp.int32, (block, LANES), 1) < LANES // 2
            for at in range(count):
                rows = pl.ds(at * block, block)
                q = qkv[rows, pl.ds(at_q, LANES)]
                k = qkv[rows, pl.ds(at_k, LANES)]
                v = qkv[rows, pl.ds(at_v, LANES)]
                parts = []
                for half, mask in enumerate((low, high)):
                    scores = dot_nt(k * mask, q) + bias[at, :block, :block]
                    top = jnp.max(scores, axis=0, keepdims=True)
                    weights = jnp.exp(scores - top)
                    total = jnp.sum(weights, axis=0, keepdims=True)
                    probs = weights * (1.0 / total)
                    lse[2 * pair + half, at : at + 1, :block] = top + jnp.log(total)
                    parts.append(dot_tn(probs.astype(BF16), v))
                context[rows, pl.ds(at_q, LANES)] = jnp.where(is_low, parts[0], parts[1]).astype(
                    BF16
                )
            return carry

        lax.fori_loop(0, HEADS // 2, pair_step, 0)

    by_block(info, body)


def attention_back(info, qkv, d_context, lse, bias, d_qkv):
    width = d_context.shape[1]
    low, high = half_masks()
    scale = (width // HEADS) ** -0.5

    def body(block, count):
        write_bias(info, bias, block, count)

        def pair_step(pair, carry):
            at_q = pl.multiple_of(pair * LANES, LANES)
            at_k = pl.multiple_of(width + pair * LANES, LANES)
            at_v = pl.multiple_of(2 * width + pair * LANES, LANES)
            is_low = lax.broadcasted_iota(jnp.int32, (block, LANES), 1) < LANES // 2
            for at in range(count):
                rows = pl.ds(at * block, block)
                q = qkv[rows, pl.ds(at_q, LANES)]
                k = qkv[rows, pl.ds(at_k, LANES)]
                v = qkv[rows, pl.ds(at_v, LANES)]
                d_out = d_context[rows, pl.ds(at_q, LANES)]
                d_q, d_k, d_v = [], [], []
                for half, mask in enumerate((low, high)):
                    scores = dot_nt(k * mask, q) + bias[at, :block, :block]
                    probs = jnp.exp(scores - lse[2 * pair + half, at : at + 1, :block])
                    d_probs = dot_nt(v * mask, d_out)
                    d_v.append(dot_nn(probs.astype(BF16), d_out))
                    inner = jnp.sum(probs * d_probs, axis=0, keepdims=True)
                    d_scores = (probs * (d_probs - inner)).astype(BF16)
                    d_k.append(dot_nn(d_scores, q))
                    d_q.append(dot_tn(d_scores, k))
                d_qkv[rows, pl.ds(at_q, LANES)] = (
                    jnp.where(is_low, d_q[0], d_q[1]) * scale
                ).astype(BF16)
                d_qkv[rows, pl.ds(at_k, LANES)] = jnp.where(is_low, d_k[0], d_k[1]).astype(BF16)
                d_qkv[rows, pl.ds(at_v, LANES)] = jnp.where(is_low, d_v[0], d_v[1]).astype(BF16)
            return carry

        lax.fori_loop(0, HEADS // 2, pair_step, 0)

    by_block(info, body)


def norm(values):
    centered = values - jnp.mean(values, axis=-1, keepdims=True)
    inverse = lax.rsqrt(jnp.mean(centered * centered, axis=-1, keepdims=True) + EPSILON)
    return centered * inverse, inverse


def norm_back(upstream, normed, inverse, gain):
    scaled = upstream * gain
    return inverse * (
        scaled
        - jnp.mean(scaled, axis=-1, keepdims=True)
        - normed * jnp.mean(scaled * normed, axis=-1, keepdims=True)
    )


CHUNK = 64


def forward_kernel(n_saved, info, tok, rec, w_a, w_up, w_down, small, bias_up, *refs):
    refs = refs[len(refs) - (n_saved + 1 + n_saved + 11) :]
    saved_out, produced = refs[:n_saved], refs[n_saved]
    scratch = refs[n_saved + 1 :]
    x, qkv, lse, context, n1, inv1, hid, act, d_act, n2, inv2, out = scratch[:n_saved]
    wa, wu, wd, hid_f, acc, bias, sem_x, sem_a, sem_u, sem_d, sem_out = scratch[n_saved:]
    width = x.shape[1]
    ff = act.shape[1]
    tiles = ff // FF_TILE

    @pl.when(info[RUN] == 1)
    def _():
        micro = info[MICRO]
        get_x = fetch_either(info[SECTION] == 0, tok.at[micro], rec, x, sem_x)

        def get_a(j):
            cols = pl.ds(pl.multiple_of(j * width, LANES), width)
            return pltpu.make_async_copy(w_a.at[:, cols], wa.at[:, cols], sem_a.at[j])

        def get_up(j):
            cols = pl.ds(pl.multiple_of(j * FF_TILE, LANES), FF_TILE)
            return pltpu.make_async_copy(w_up.at[:, cols], wu.at[:, cols], sem_u.at[j])

        def get_down(j):
            rows = pl.ds(pl.multiple_of(j * FF_TILE, LANES), FF_TILE)
            return pltpu.make_async_copy(w_down.at[rows, :], wd.at[rows, :], sem_d.at[j])

        for j in range(4):
            get_a(j).start()
        for j in range(tiles):
            get_up(j).start()
        for j in range(tiles):
            get_down(j).start()
        outs = Copies(sem_out)
        waits = []

        def save(index):
            waits.append(outs.start(scratch[index], saved_out[index].at[micro]))

        get_x.wait()
        save(0)

        def project(j, carry):
            get_a(j).wait()
            cols = pl.ds(pl.multiple_of(j * width, LANES), width)
            factor = jnp.where(j == 0, (width // HEADS) ** -0.5, 1.0)
            part = dot_nn(x[...], wa[:, cols]) + small[pl.ds(j, 1), :]
            qkv[:, cols] = (part * factor).astype(BF16)
            return carry

        lax.fori_loop(0, 3, project, 0)
        save(1)
        attention(info, qkv, context, lse, bias)
        save(2)
        save(3)
        get_a(3).wait()
        acc[...] = dot_nn(context[...], wa[:, 3 * width : 4 * width])

        def norm_one(i, carry):
            rows = pl.ds(pl.multiple_of(i * CHUNK, CHUNK), CHUNK)
            total = x[rows, :].astype(F32) + acc[rows, :] + small[BIAS_OUT : BIAS_OUT + 1, :]
            normed, inverse = norm(total)
            n1[rows, :] = normed
            inv1[rows, :] = jnp.broadcast_to(inverse, (CHUNK, LANES))
            hidden = normed * small[GAIN_ATTN : GAIN_ATTN + 1, :] + small[SHIFT_ATTN : SHIFT_ATTN + 1, :]
            hid_f[rows, :] = hidden
            hid[rows, :] = hidden.astype(BF16)
            return carry

        lax.fori_loop(0, ROWS // CHUNK, norm_one, 0)
        save(4)
        save(5)
        save(6)
        acc[...] = hid_f[...] + small[BIAS_DOWN : BIAS_DOWN + 1, :]

        def up(j):
            cols = pl.ds(pl.multiple_of(j * FF_TILE, LANES), FF_TILE)
            get_up(j).wait()
            pre = dot_nn(hid[...], wu[:, cols]) + bias_up[:, cols]
            below = 0.5 * (1.0 + lax.erf(pre * 0.7071067811865476))
            density = jnp.exp(pre * pre * -0.5) * 0.3989422804014327
            act[:, cols] = (pre * below).astype(BF16)
            d_act[:, cols] = (below + pre * density).astype(BF16)

        def down(j):
            cols = pl.ds(pl.multiple_of(j * FF_TILE, LANES), FF_TILE)
            get_down(j).wait()
            acc[...] += dot_nn(act[:, cols], wd[cols, :])

        up(0)

        def ffn_step(j, carry):
            down(j - 1)
            up(j)
            return carry

        lax.fori_loop(1, tiles, ffn_step, 0)
        save(7)
        save(8)
        down(tiles - 1)

        def norm_two(i, carry):
            rows = pl.ds(pl.multiple_of(i * CHUNK, CHUNK), CHUNK)
            normed, inverse = norm(acc[rows, :])
            n2[rows, :] = normed
            inv2[rows, :] = jnp.broadcast_to(inverse, (CHUNK, LANES))
            out[rows, :] = (
                normed * small[GAIN_FFN : GAIN_FFN + 1, :] + small[SHIFT_FFN : SHIFT_FFN + 1, :]
            ).astype(BF16)
            return carry

        lax.fori_loop(0, ROWS // CHUNK, norm_two, 0)
        waits.append(outs.start(out, produced))
        for index in range(9, 12):
            save(index)
        for copy in waits:
            copy.wait()


def saved_shapes(width, ff):
    return (
        ((ROWS, width), BF16),
        ((ROWS, 3 * width), BF16),
        ((HEADS, 8, 256), F32),
        ((ROWS, width), BF16),
        ((ROWS, width), F32),
        ((ROWS, LANES), F32),
        ((ROWS, width), BF16),
        ((ROWS, ff), BF16),
        ((ROWS, ff), BF16),
        ((ROWS, width), F32),
        ((ROWS, LANES), F32),
        ((ROWS, width), BF16),
    )


def hold(shapes):
    return [jax.ShapeDtypeStruct((2,) + shape, kind) for shape, kind in shapes]


def vmem(shapes):
    return [pltpu.VMEM(shape, kind) for shape, kind in shapes]


def forward(info, tokens, received, w_a, w_up, w_down, small, bias_up, saved=None):
    width, ff = w_up.shape
    shapes = saved_shapes(width, ff)
    n = len(shapes)
    tiles = ff // FF_TILE
    aliased = [] if saved is None else list(saved)
    flops = 2 * ROWS * width * (4 * width + 2 * ff) + 4 * ROWS * ROWS * width
    return pl.pallas_call(
        functools.partial(forward_kernel, n),
        in_specs=[SCALARS, ANY, ANY, ANY, ANY, ANY, WHOLE, WHOLE] + [ANY] * len(aliased),
        out_specs=[ANY] * (n + 1),
        out_shape=hold(shapes) + [jax.ShapeDtypeStruct((ROWS, width), BF16)],
        input_output_aliases={8 + i: i for i in range(len(aliased))},
        scratch_shapes=vmem(shapes)
        + [
            pltpu.VMEM((width, 4 * width), BF16),
            pltpu.VMEM((width, ff), BF16),
            pltpu.VMEM((ff, width), BF16),
            pltpu.VMEM((ROWS, width), F32),
            pltpu.VMEM((ROWS, width), F32),
            pltpu.VMEM((3, 3 * SEGMENT, 3 * SEGMENT), F32),
            pltpu.SemaphoreType.DMA,
            pltpu.SemaphoreType.DMA((4,)),
            pltpu.SemaphoreType.DMA((tiles,)),
            pltpu.SemaphoreType.DMA((tiles,)),
            pltpu.SemaphoreType.DMA((n + 1,)),
        ],
        compiler_params=pltpu.CompilerParams(vmem_limit_bytes=VMEM_LIMIT),
        cost_estimate=pl.CostEstimate(flops=flops, bytes_accessed=30_000_000, transcendentals=0),
        name="layer_forward",
    )(info, tokens, received, w_a, w_up, w_down, small, bias_up, *aliased)


def ffn_back_kernel(info, cot, rec, w_up, w_down, small, n1_h, inv1_h, d_act_h, n2_h, inv2_h, *refs):
    refs = refs[len(refs) - (5 + 16) :]
    d_ffn_h, d_pre_h, d_branch_h, sums_h, d_first_h = refs[:5]
    (
        g,
        n1,
        inv1,
        d_act,
        n2,
        inv2,
        d_ffn,
        d_pre,
        d_branch,
        sums,
        d_second,
        wu,
        wd,
        acc,
        sem_in,
        sem_out,
    ) = refs[5:]
    width = g.shape[1]
    ff = d_pre.shape[1]
    tiles = ff // FF_TILE

    @pl.when(info[RUN] == 1)
    def _():
        micro = info[MICRO]
        get_g = fetch_either(info[SECTION] == 1, cot.at[micro], rec, g, sem_in.at[0])

        def get_up(j):
            cols = pl.ds(pl.multiple_of(j * FF_TILE, LANES), FF_TILE)
            return pltpu.make_async_copy(w_up.at[:, cols], wu.at[:, cols], sem_in.at[8 + j])

        def get_down(j):
            rows = pl.ds(pl.multiple_of(j * FF_TILE, LANES), FF_TILE)
            return pltpu.make_async_copy(w_down.at[rows, :], wd.at[rows, :], sem_in.at[8 + tiles + j])

        gets = [
            pltpu.make_async_copy(src.at[micro], dst, sem_in.at[1 + i])
            for i, (src, dst) in enumerate(
                ((n2_h, n2), (inv2_h, inv2), (d_act_h, d_act), (n1_h, n1), (inv1_h, inv1))
            )
        ]
        gets[0].start()
        gets[1].start()
        get_down(0).start()
        gets[2].start()
        for j in range(tiles):
            get_up(j).start()
            if j + 1 < tiles:
                get_down(j + 1).start()
        gets[3].start()
        gets[4].start()
        outs = Copies(sem_out)
        waits = []
        get_g.wait()
        gets[0].wait()
        gets[1].wait()
        zeros = jnp.zeros((8, width), F32)

        def back_two(i, carry):
            sum_g, sum_gn, sum_d = carry
            rows = pl.ds(pl.multiple_of(i * CHUNK, CHUNK), CHUNK)
            upstream = g[rows, :].astype(F32)
            normed = n2[rows, :]
            grad = norm_back(upstream, normed, inv2[rows, :1], small[GAIN_FFN : GAIN_FFN + 1, :])
            d_second[rows, :] = grad
            low = grad.astype(BF16)
            d_ffn[rows, :] = low
            return (
                sum_g + fold(upstream),
                sum_gn + fold(upstream * normed),
                sum_d + fold(low.astype(F32)),
            )

        sum_g, sum_gn, sum_d = lax.fori_loop(0, ROWS // CHUNK, back_two, (zeros, zeros, zeros))
        waits.append(outs.start(d_ffn, d_ffn_h.at[micro]))
        sums[1:2, :width] = jnp.sum(sum_d, axis=0, keepdims=True)
        sums[1:2, width : 2 * width] = jnp.sum(sum_gn, axis=0, keepdims=True)
        sums[1:2, 2 * width : 3 * width] = jnp.sum(sum_g, axis=0, keepdims=True)
        gets[2].wait()
        acc[...] = d_second[...]

        def first(j):
            cols = pl.ds(pl.multiple_of(j * FF_TILE, LANES), FF_TILE)
            get_down(j).wait()
            low = (dot_nt(d_ffn[...], wd[cols, :]) * d_act[:, cols].astype(F32)).astype(BF16)
            d_pre[:, cols] = low
            sums[0:1, cols] = jnp.sum(low.astype(F32), axis=0, keepdims=True)

        def second(j):
            cols = pl.ds(pl.multiple_of(j * FF_TILE, LANES), FF_TILE)
            get_up(j).wait()
            acc[...] += dot_nt(d_pre[:, cols], wu[:, cols])

        first(0)

        def ffn_step(j, carry):
            second(j - 1)
            first(j)
            return carry

        lax.fori_loop(1, tiles, ffn_step, 0)
        waits.append(outs.start(d_pre, d_pre_h.at[micro]))
        second(tiles - 1)
        gets[3].wait()
        gets[4].wait()

        def back_one(i, carry):
            sum_g, sum_gn, sum_d = carry
            rows = pl.ds(pl.multiple_of(i * CHUNK, CHUNK), CHUNK)
            upstream = acc[rows, :]
            normed = n1[rows, :]
            grad = norm_back(upstream, normed, inv1[rows, :1], small[GAIN_ATTN : GAIN_ATTN + 1, :])
            d_second[rows, :] = grad
            low = grad.astype(BF16)
            d_branch[rows, :] = low
            return (
                sum_g + fold(upstream),
                sum_gn + fold(upstream * normed),
                sum_d + fold(low.astype(F32)),
            )

        sum_g, sum_gn, sum_d = lax.fori_loop(0, ROWS // CHUNK, back_one, (zeros, zeros, zeros))
        sums[1:2, 3 * width :] = jnp.sum(sum_gn, axis=0, keepdims=True)
        sums[2:3, :width] = jnp.sum(sum_g, axis=0, keepdims=True)
        sums[2:3, width : 2 * width] = jnp.sum(sum_d, axis=0, keepdims=True)
        waits.append(outs.start(d_branch, d_branch_h.at[micro]))
        waits.append(outs.start(d_second, d_first_h))
        waits.append(outs.start(sums, sums_h.at[micro]))
        for copy in waits:
            copy.wait()


def ffn_back(info, cotangent, received, w_up, w_down, small, saved, held=None):
    width, ff = w_up.shape
    tiles = ff // FF_TILE
    n1, inv1, d_act, n2, inv2 = saved[4], saved[5], saved[8], saved[9], saved[10]
    shapes = (
        ((ROWS, width), BF16),
        ((ROWS, ff), BF16),
        ((ROWS, width), BF16),
        ((8, ff), F32),
    )
    aliased = [] if held is None else list(held)
    return pl.pallas_call(
        ffn_back_kernel,
        in_specs=[SCALARS, ANY, ANY, ANY, ANY, WHOLE] + [ANY] * (5 + len(aliased)),
        out_specs=[ANY] * 5,
        out_shape=hold(shapes) + [jax.ShapeDtypeStruct((ROWS, width), F32)],
        input_output_aliases={11 + i: i for i in range(len(aliased))},
        scratch_shapes=vmem(
            (
                ((ROWS, width), BF16),
                ((ROWS, width), F32),
                ((ROWS, LANES), F32),
                ((ROWS, ff), BF16),
                ((ROWS, width), F32),
                ((ROWS, LANES), F32),
            )
            + shapes
            + (
                ((ROWS, width), F32),
                ((width, ff), BF16),
                ((ff, width), BF16),
                ((ROWS, width), F32),
            )
        )
        + [pltpu.SemaphoreType.DMA((8 + 2 * tiles,)), pltpu.SemaphoreType.DMA((5,))],
        compiler_params=pltpu.CompilerParams(vmem_limit_bytes=VMEM_LIMIT),
        cost_estimate=pl.CostEstimate(
            flops=4 * ROWS * width * ff, bytes_accessed=20_000_000, transcendentals=0
        ),
        name="ffn_backward",
    )(info, cotangent, received, w_up, w_down, small, n1, inv1, d_act, n2, inv2, *aliased)


def attn_back_kernel(info, w_a, d_first_h, d_branch_h, qkv_h, lse_h, *refs):
    refs = refs[len(refs) - (4 + 13) :]
    d_qkv_h, grad_h, sums_h, produced = refs[:4]
    d_first, d_branch, qkv, lse, d_qkv, grad, sums, wa, d_context, bias, acc, sem_in, sem_out = refs[4:]
    width = grad.shape[1]

    @pl.when(info[RUN] == 1)
    def _():
        micro = info[MICRO]

        def get_a(j):
            cols = pl.ds(pl.multiple_of(j * width, LANES), width)
            return pltpu.make_async_copy(w_a.at[:, cols], wa.at[:, cols], sem_in.at[j])

        gets = [
            pltpu.make_async_copy(src, dst, sem_in.at[4 + i])
            for i, (src, dst) in enumerate(
                (
                    (d_branch_h.at[micro], d_branch),
                    (qkv_h.at[micro], qkv),
                    (lse_h.at[micro], lse),
                    (d_first_h, d_first),
                )
            )
        ]
        gets[0].start()
        get_a(3).start()
        gets[1].start()
        gets[2].start()
        for j in range(3):
            get_a(j).start()
        gets[3].start()
        outs = Copies(sem_out)
        waits = []
        gets[0].wait()
        get_a(3).wait()
        d_context[...] = dot_nt(d_branch[...], wa[:, 3 * width : 4 * width]).astype(BF16)
        gets[1].wait()
        gets[2].wait()
        attention_back(info, qkv, d_context, lse, bias, d_qkv)
        waits.append(outs.start(d_qkv, d_qkv_h.at[micro]))
        for row, at in ((0, 0), (1, 2 * width)):
            sums[row : row + 1, :] = jnp.sum(
                fold(d_qkv[:, at : at + width].astype(F32)), axis=0, keepdims=True
            )
        waits.append(outs.start(sums, sums_h.at[micro]))
        gets[3].wait()
        acc[...] = d_first[...]

        def project(j, carry):
            get_a(j).wait()
            cols = pl.ds(pl.multiple_of(j * width, LANES), width)
            acc[...] += dot_nt(d_qkv[:, cols], wa[:, cols])
            return carry

        lax.fori_loop(0, 3, project, 0)
        grad[...] = acc[...].astype(BF16)
        waits.append(outs.start(grad, produced))
        waits.append(outs.start(grad, grad_h.at[micro]))
        for copy in waits:
            copy.wait()


def attn_back(info, w_a, d_first, d_branch, saved, held=None):
    width = d_first.shape[1]
    shapes = (
        ((ROWS, 3 * width), BF16),
        ((ROWS, width), BF16),
        ((8, width), F32),
    )
    aliased = [] if held is None else list(held)
    flops = 2 * ROWS * width * 4 * width + 10 * ROWS * ROWS * width
    return pl.pallas_call(
        attn_back_kernel,
        in_specs=[SCALARS] + [ANY] * (5 + len(aliased)),
        out_specs=[ANY] * 4,
        out_shape=hold(shapes) + [jax.ShapeDtypeStruct((ROWS, width), BF16)],
        input_output_aliases={6 + i: i for i in range(len(aliased))},
        scratch_shapes=vmem(
            (
                ((ROWS, width), F32),
                ((ROWS, width), BF16),
                ((ROWS, 3 * width), BF16),
                ((HEADS, 8, 256), F32),
            )
            + shapes
            + (
                ((width, 4 * width), BF16),
                ((ROWS, width), BF16),
                ((3, 3 * SEGMENT, 3 * SEGMENT), F32),
                ((ROWS, width), F32),
            )
        )
        + [pltpu.SemaphoreType.DMA((8,)), pltpu.SemaphoreType.DMA((4,))],
        compiler_params=pltpu.CompilerParams(vmem_limit_bytes=VMEM_LIMIT),
        cost_estimate=pl.CostEstimate(flops=flops, bytes_accessed=15_000_000, transcendentals=0),
        name="attention_backward",
    )(info, w_a, d_first, d_branch, saved[1], saved[2], *aliased)


def weight_grad_kernel(a, b, out):
    out[...] = (dot_tn(a[0], b[0]) + dot_tn(a[1], b[1])).astype(BF16)


def weight_grad(a, b, name):
    rows, m = a.shape[1:]
    n = b.shape[2]
    tile = 256
    return pl.pallas_call(
        weight_grad_kernel,
        grid=(m // tile,),
        in_specs=[
            pl.BlockSpec((2, rows, tile), lambda i: (0, 0, i)),
            pl.BlockSpec((2, rows, n), lambda i: (0, 0, 0)),
        ],
        out_specs=pl.BlockSpec((tile, n), lambda i: (i, 0)),
        out_shape=jax.ShapeDtypeStruct((m, n), BF16),
        compiler_params=pltpu.CompilerParams(vmem_limit_bytes=VMEM_LIMIT),
        cost_estimate=pl.CostEstimate(
            flops=4 * rows * m * n, bytes_accessed=2 * m * n, transcendentals=0
        ),
        name=name,
    )(a, b)


def passed_along(block, axis, distance):
    devices = range(lax.axis_size(axis))
    route = [(i - distance, i) for i in devices if i - distance in devices]
    return lax.ppermute(block, axis, route)


def on_device(
    tokens,
    cotangent,
    bucket,
    lengths,
    w_qkv,
    bias_q,
    bias_v,
    w_out,
    bias_out,
    gain_attn,
    shift_attn,
    w_up,
    bias_up,
    w_down,
    bias_down,
    gain_ffn,
    shift_ffn,
):
    section = lax.axis_index("section")
    width = tokens.shape[2]
    ff = w_up.shape[2]
    share = bias_q.shape[1]
    n_dp = width // share
    vectors = (bias_q, bias_v, bias_out, gain_attn, shift_attn, bias_down, gain_ffn, shift_ffn)

    part_a = jnp.concatenate([w_qkv[0], w_out[0]], axis=1).astype(BF16)
    part_s = jnp.concatenate(vectors + (bias_up,), axis=1).astype(BF16)
    w_a = lax.all_gather(part_a, "dp", axis=0, tiled=True)
    smalls = lax.all_gather(part_s, "dp", axis=0, tiled=True)
    full_up = lax.all_gather(w_up[0].astype(BF16), "dp", axis=0, tiled=True)
    full_down = lax.all_gather(w_down[0].astype(BF16), "dp", axis=0, tiled=True)
    rows = smalls[:, : 8 * share].reshape(n_dp, 8, share).transpose(1, 0, 2).reshape(8, width)
    rows = rows.astype(F32)
    small = jnp.concatenate(
        [rows[:1], jnp.zeros((1, width), F32), rows[1:], jnp.zeros((7, width), F32)]
    )
    full_bias_up = smalls[:, 8 * share :].reshape(1, ff).astype(F32)

    def info(step, micro):
        picked = jnp.clip(micro, 0, 1)
        run = ((micro >= 0) & (micro <= 1)).astype(jnp.int32)
        head = jnp.stack([run, picked, section, lax.dynamic_index_in_dim(bucket, picked, 0, False)[0]])
        return jnp.concatenate([head, lax.dynamic_index_in_dim(lengths, picked, 0, False)])

    ahead = [info(step, step - section) for step in range(3)]
    back = [info(step, step - 1 + section) for step in range(3)]
    none = jnp.zeros((ROWS, width), BF16)

    weights = (w_a, full_up, full_down, small, full_bias_up)
    *saved, made = forward(ahead[0], tokens, none, *weights)
    got = passed_along(made, "section", 1)
    *saved, made = forward(ahead[1], tokens, got, *weights, saved=saved)
    got = passed_along(made, "section", 1)

    def backward(step, upstream, saved, held):
        ffn_held, attn_held = (None, None) if held is None else held
        *ffn_held, d_first = ffn_back(
            back[step], cotangent, upstream, full_up, full_down, small, saved, ffn_held
        )
        *attn_held, made = attn_back(back[step], w_a, d_first, ffn_held[2], saved, attn_held)
        return (ffn_held, attn_held), made

    held, made = backward(0, none, saved, None)
    sent = passed_along(made, "section", -1)
    *saved, made = forward(ahead[2], tokens, got, *weights, saved=saved)
    held, made = backward(1, sent, saved, held)
    sent = passed_along(made, "section", -1)
    (ffn_held, attn_held), made = backward(2, sent, saved, held)
    d_ffn, d_pre, d_branch, sums_ffn = ffn_held
    d_qkv, input_grads, sums_attn = attn_held

    g_down = weight_grad(saved[7], d_ffn, "grad_down")
    g_up = weight_grad(saved[6], d_pre, "grad_up")
    g_out = weight_grad(saved[3], d_branch, "grad_out")
    g_qkv = weight_grad(saved[0], d_qkv, "grad_qkv")
    total = sums_ffn[0] + sums_ffn[1]
    total_attn = sums_attn[0] + sums_attn[1]
    vector = [
        total_attn[0],
        total_attn[1],
        total[2, width : 2 * width],
        total[1, 3 * width :],
        total[2, :width],
        total[1, :width],
        total[1, width : 2 * width],
        total[1, 2 * width : 3 * width],
    ]
    table = jnp.stack(vector).reshape(8, n_dp, share).transpose(1, 0, 2).reshape(n_dp, 8 * share)
    table = jnp.concatenate([table, total[0].reshape(n_dp, ff // n_dp)], axis=1)

    def summed(values):
        return lax.psum_scatter(values, "dp", scatter_dimension=0, tiled=True).astype(F32)[None]

    g_down, g_up, g_out, g_qkv = (summed(g) for g in (g_down, g_up, g_out, g_qkv))
    table = summed(table)[0]
    g_vectors = [table[:, i * share : (i + 1) * share] for i in range(8)]
    g_bias_up = table[:, 8 * share :]
    (
        g_bias_q,
        g_bias_v,
        g_bias_out,
        g_gain_attn,
        g_shift_attn,
        g_bias_down,
        g_gain_ffn,
        g_shift_ffn,
    ) = g_vectors
    return (
        saved[11][None],
        input_grads[None],
        g_qkv,
        g_bias_q,
        g_bias_v,
        g_out,
        g_bias_out,
        g_gain_attn,
        g_shift_attn,
        g_up,
        g_bias_up,
        g_down,
        g_bias_down,
        g_gain_ffn,
        g_shift_ffn,
    )


def solution(mesh):
    matrix = P("section", "dp", None)
    vector = P("section", "dp")
    rows = P(None, "dp", None)
    outs = P("section", None, "dp", None)
    params = (
        matrix,
        vector,
        vector,
        matrix,
        vector,
        vector,
        vector,
        matrix,
        vector,
        matrix,
        vector,
        vector,
        vector,
    )
    return jax.shard_map(
        on_device,
        mesh=mesh,
        in_specs=(rows, rows, P(None, "dp"), P(None, "dp")) + params,
        out_specs=(outs, outs) + params,
        check_vma=False,
    )
```

time: 1640 us -> 678 us (0.41)
  waiting for transfers between devices: 1100 us -> 378 us
  matrix products: 217 us -> 0 us
  Pallas kernels: 0 us -> 146 us
  other arithmetic: 152 us -> 13.1 us
  local copies, waits for them, and re-layouts: 64.1 us -> 17.6 us
  blocking collectives: 63.6 us -> 81.6 us
    unnamed x26 -> x7, waiting for transfers between devices: 447 us -> 0.11 us
    reduce_scatter x4, waiting for transfers between devices: 390 us -> 170 us  [summed(): lax.psum_scatter(values, 'dp', scatter_dimension=0, tiled=True).astype(F32)]
    dot_general x42 -> x0, matrix products: 191 us -> none  [the longest x4 39.6 us: forward(): jnp.dot(active, w_down, preferred_element_type=jnp.float32)]
    pallas_call x0 -> x13, Pallas kernels: none -> 146 us  [the longest x3 55.2 us: forward(): pl.pallas_call(functools.partial(forward_kernel, n), in_specs=[SCALARS, A...]
    ppermute x4, waiting for transfers between devices: 138 us -> 71.9 us  [passed_along(): return lax.ppermute(block, axis, route)]
    squeeze x1 -> x0, blocking collectives: 63.6 us -> none  [on_device(): params = tuple((member[0] for member in gathered))]
    unnamed x0 -> x1, blocking collectives: none -> 58.4 us
    convert_element_type x39 -> x4, other arithmetic: 52.2 us -> 2.57 us  [the longest x1 1.81 us: on_device(): full_up = lax.all_gather(w_up[0].astype(BF16), 'dp', axis=0, tiled=True)]
  transfers between devices with their start and end apart: 21 -> 11, of which waited for: 19 -> 10; matrix products, arithmetic and copies ran while one was open for 6% -> 3% of each run, Pallas kernels for 0% -> 7%
where the time goes in v1:
time: 678 us; the launch traced here: 666 us
  waiting for transfers between devices  378 us (56%)
  Pallas kernels  146 us (22%)
  blocking collectives  81.6 us (12%)
  local copies, waits for them, and re-layouts  17.6 us (3%)
  between operations  15.1 us (2%)
  starting transfers between devices  14 us (2%)
  other arithmetic  13.1 us (2%)
    reduce_scatter x4, waiting for transfers between devices, summed(): lax.psum_scatter(values, 'dp', scatter_dimension=0, tiled=True).astype(F32)  170 us
    ppermute x4, waiting for transfers between devices, passed_along(): return lax.ppermute(block, axis, route)  71.9 us
    unnamed x1, blocking collectives  58.4 us
    pallas_call x3, Pallas kernels, forward(): pl.pallas_call(functools.partial(forward_kernel, n), in_specs=[SCALARS, A...  55.2 us
    all_gather x1, waiting for transfers between devices, on_device(): full_down = lax.all_gather(w_down[0].astype(BF16), 'dp', axis=0, tiled=True)  54.8 us
    all_gather x1, waiting for transfers between devices, on_device(): full_up = lax.all_gather(w_up[0].astype(BF16), 'dp', axis=0, tiled=True)  54.8 us
    pallas_call x4, Pallas kernels, weight_grad(): pl.pallas_call(weight_grad_kernel, grid=(m // tile,), in_specs=[pl.BlockS...  33.7 us
    pallas_call x3, Pallas kernels, attn_back(): pl.pallas_call(attn_back_kernel, in_specs=[SCALARS] + [ANY] * (5 + len(al...  31.6 us
  transfers between devices with their start and end apart: 11, of which 10 were waited for; matrix products, arithmetic and copies ran while one was open for 3% of the time, Pallas kernels for 7%

profile of v1, /device:TPU:0, one launch (start us, length us, event | category | flops | bytes accessed | tf_op | source)
XLA Modules:
  0.0 666.3 jit_solution(4816032766230887176)
XLA Ops:
  7.4 1.2 convert_bitcast_fusion
  8.5 0.9 convert_bitcast_fusion.1
  9.5 0.7 pad_maximum_fusion
  10.3 1.8 convert_element_type.47
  12.2 0.7 convert_element_type.49
  13.2 0.1 concatenate.44
  13.3 23.2 %all-gather.2 = bf16[16,1,576]{2,1,0:T(2,128)(2,1)S(1)} all-gather(bf16[1,1,576]{2,1,0:T(2,128)(2,1)S(1)} %bitcast.82), channel_id=1, replica_groups=mesh['section'=2,'dp'=16] {'dp'}, dimensions={0}, use_global_device_ids=true | all-gather | bytes 19584 | tf_op jit(solution)/shard_map/all_gather | solution.py:718
  36.5 0.1 reshape.190
  36.7 0.1 slice.91
  36.8 0.1 slice.89
  36.9 0.1 pad.5.clone
  36.9 0.1 pad.3.clone
  37.0 0.7 reshape.182.bias_up
  37.7 0.7 constant_dynamic-slice_fusion.1
  38.4 1.3 concatenate.42.info
  39.7 0.7 maximum_maximum_fusion.small
  40.3 26.9 %all-gather.7.cloned.1.call-done.w_a = bf16[768,3072]{1,0:T(8,128)(2,1)} async-done(((bf16[48,3072]{1,0:T(8,128)(2,1)}), bf16[768,3072]{1,0:T(8,128)(2,1)}) %all-gather.7.cloned.1.call-update) | async-done | bytes 4718608 | tf_op jit(solution)/shard_map/all_gather | solution.py:717
  67.2 54.8 %all-gather.9.cloned.1.call-done = bf16[1,768,3072]{2,1,0:T(8,128)(2,1)} async-done(((bf16[1,48,3072]{2,1,0:T(8,128)(2,1)}), bf16[1,768,3072]{2,1,0:T(8,128)(2,1)}) %all-gather.9.cloned.1.call-update) | async-done | bytes 4718608 | tf_op jit(solution)/shard_map/all_gather | solution.py:719
  122.1 54.8 %all-gather.11.cloned.1.call-done = bf16[1,3072,768]{2,1,0:T(8,128)(2,1)} async-done(((bf16[1,192,768]{2,1,0:T(8,128)(2,1)}), bf16[1,3072,768]{2,1,0:T(8,128)(2,1)}) %all-gather.11.cloned.1.call-update) | async-done | bytes 4718608 | tf_op jit(solution)/shard_map/all_gather | solution.py:720
  176.9 0.9 broadcast_in_dim.39.rec
  177.7 29.7 %layer_forward.3 = (bf16[2,384,768]{2,1,0:T(8,128)(2,1)}, bf16[2,384,2304]{2,1,0:T(8,128)(2,1)}, f32[2,12,8,256]{3,2,1,0:T(8,128)}, bf16[2,384,768]{2,1,0:T(8,12...) custom-call(s32[10]{0:T(128)} %concatenate.42.info, ...), custom_call_target="tpu_custom_call" | custom-call | flops 5888802816 | bytes 30000000 | tf_op jit(solution)/shard_map/layer_forward/pallas_call | solution.py:354
  207.4 1.3 collective-permute-start
  208.8 1.3 concatenate.41.info
  210.0 1.2 concatenate.48.info
  211.3 11.0 %collective-permute-done.rec = bf16[384,768]{1,0:T(8,128)(2,1)S(1)} collective-permute-done((bf16[384,768]{1,0:T(8,128)(2,1)}, bf16[384,768]{1,0:T(8,128)(2,1)S(1)}, u32[]{:S(2)}, u32[]{:S(2)}) %collective-permute-start) | collective-permute-done | bytes 589856 | tf_op jit(solution)/shard_map/ppermute | solution.py:686
  222.3 0.8 copy-done.4
  223.1 24.5 %layer_forward.4 = (bf16[2,384,768]{2,1,0:T(8,128)(2,1)}, bf16[2,384,2304]{2,1,0:T(8,128)(2,1)}, f32[2,12,8,256]{3,2,1,0:T(8,128)}, bf16[2,384,768]{2,1,0:T(8,12...) custom-call(s32[10]{0:T(128)} %concatenate.41.info, ...), custom_call_target="tpu_custom_call", output_to_operand_aliasing={{0}: (8, {}), {1}: (9, {}), {2}: (10, {}), {3}: (11, {}), {... | custom-call | flops 5888802816 | bytes 30000000 | tf_op jit(solution)/shard_map/layer_forward/pallas_call | solution.py:354
  247.6 9.8 %collective-permute-start.1 = (bf16[384,768]{1,0:T(8,128)(2,1)}, bf16[384,768]{1,0:T(8,128)(2,1)S(1)}, u32[]{:S(2)}, u32[]{:S(2)}) collective-permute-start(bf16[384,768]{1,0:T(8,128)(2,1)} %get-tuple-element.92), channel_id=1, source_target_pairs={{0,16},{1,17},{2,18},{3,19},{4,20},{5,21},{6,22},{7,23},{8,24},{9,... | collective-permute-start | bytes 1769480 | tf_op jit(solution)/shard_map/ppermute | solution.py:686
  257.4 1.2 ffn_backward.3
  258.6 0.8 attention_backward.3
  259.4 1.3 collective-permute-start.2
  260.7 1.3 concatenate.40.info
  262.0 1.2 concatenate.47.info
  263.2 7.0 %collective-permute-done.1.rec = bf16[384,768]{1,0:T(8,128)(2,1)S(1)} collective-permute-done((bf16[384,768]{1,0:T(8,128)(2,1)}, bf16[384,768]{1,0:T(8,128)(2,1)S(1)}, u32[]{:S(2)}, u32[]{:S(2)}) %collective-permute-start.1) | collective-permute-done | bytes 589856 | tf_op jit(solution)/shard_map/ppermute | solution.py:686
  270.2 0.8 copy-done.2
  271.0 1.1 layer_forward.5
  272.1 27.7 %collective-permute-done.2.rec = bf16[384,768]{1,0:T(8,128)(2,1)S(1)} collective-permute-done((bf16[384,768]{1,0:T(8,128)(2,1)}, bf16[384,768]{1,0:T(8,128)(2,1)S(1)}, u32[]{:S(2)}, u32[]{:S(2)}) %collective-permute-start.2) | collective-permute-done | bytes 589856 | tf_op jit(solution)/shard_map/ppermute | solution.py:686
  299.8 0.8 copy-done.3
  300.6 12.4 %ffn_backward.4 = (bf16[2,384,768]{2,1,0:T(8,128)(2,1)}, bf16[2,384,3072]{2,1,0:T(8,128)(2,1)}, bf16[2,384,768]{2,1,0:T(8,128)(2,1)}, f32[2,8,3072]{2,1,0:T(8,128)}, f32[384,768]{1,0:T(8,128)}) custom-call(s32[10]{0:T(128)} %concatenate.47.info, ...), custom_call_target="tpu_custom_call", output_to_operand_aliasing={{0}: (11, {}), {1}: (12, {}), {2}: (13, {}), {3}: (14, {})} | custom-call | flops 3623878656 | bytes 20000000 | tf_op jit(solution)/shard_map/ffn_backward/pallas_call | solution.py:526
  313.1 15.9 %attention_backward.4 = (bf16[2,384,2304]{2,1,0:T(8,128)(2,1)}, bf16[2,384,768]{2,1,0:T(8,128)(2,1)}, f32[2,8,768]{2,1,0:T(8,128)}, bf16[384,768]{1,0:T(8,128)(2,1)}) custom-call(s32[10]{0:T(128)} %concatenate.47.info, bf16[768,3072]{1,0:T(8,128)(2,1)} %all-gather.7.cloned.1.call-done.w_a, ...), custom_call_target="tpu_custom_call", output_to_operand_aliasing={{0}: (6, {}), {1}: (7, {}), {2}: (8, {})} | custom-call | flops 2944401408 | bytes 15000000 | tf_op jit(solution)/shard_map/attention_backward/pallas_call | solution.py:630
  328.9 1.3 collective-permute-start.3
  330.2 1.2 concatenate.46.info
  331.5 26.2 %collective-permute-done.3.rec = bf16[384,768]{1,0:T(8,128)(2,1)S(1)} collective-permute-done((bf16[384,768]{1,0:T(8,128)(2,1)}, bf16[384,768]{1,0:T(8,128)(2,1)S(1)}, u32[]{:S(2)}, u32[]{:S(2)}) %collective-permute-start.3) | collective-permute-done | bytes 589856 | tf_op jit(solution)/shard_map/ppermute | solution.py:686
  357.7 0.8 copy-done.5
  358.5 12.2 %ffn_backward.5 = (bf16[2,384,768]{2,1,0:T(8,128)(2,1)}, bf16[2,384,3072]{2,1,0:T(8,128)(2,1)}, bf16[2,384,768]{2,1,0:T(8,128)(2,1)}, f32[2,8,3072]{2,1,0:T(8,128)}, f32[384,768]{1,0:T(8,128)}) custom-call(s32[10]{0:T(128)} %concatenate.46.info, ...), custom_call_target="tpu_custom_call", output_to_operand_aliasing={{0}: (11, {}), {1}: (12, {}), {2}: (13, {}), {3}: (14, {})} | custom-call | flops 3623878656 | bytes 20000000 | tf_op jit(solution)/shard_map/ffn_backward/pallas_call | solution.py:526
  370.7 4.5 grad_out.1
  375.3 15.0 %attention_backward.5 = (bf16[2,384,2304]{2,1,0:T(8,128)(2,1)}, bf16[2,384,768]{2,1,0:T(8,128)(2,1)}, f32[2,8,768]{2,1,0:T(8,128)}, bf16[384,768]{1,0:T(8,128)(2,1)}) custom-call(s32[10]{0:T(128)} %concatenate.46.info, bf16[768,3072]{1,0:T(8,128)(2,1)} %all-gather.7.cloned.1.call-done.w_a, ...), custom_call_target="tpu_custom_call", output_to_operand_aliasing={{0}: (6, {}), {1}: (7, {}), {2}: (8, {})} | custom-call | flops 2944401408 | bytes 15000000 | tf_op jit(solution)/shard_map/attention_backward/pallas_call | solution.py:630
  390.3 7.5 %grad_qkv.1 = bf16[768,2304]{1,0:T(8,128)(2,1)} custom-call(bf16[2,384,768]{2,1,0:T(8,128)(2,1)} %get-tuple-element.134.a, bf16[2,384,2304]{2,1,0:T(8,128)(2,1)} %get-tuple-element.135.b), custom_call_target="tpu_custom_call" | custom-call | flops 2717908992 | bytes 3538944 | tf_op jit(solution)/shard_map/grad_qkv/pallas_call | solution.py:666
  397.9 12.4 %grad_down.1 = bf16[3072,768]{1,0:T(8,128)(2,1)} custom-call(bf16[2,384,3072]{2,1,0:T(8,128)(2,1)} %get-tuple-element.141.a, bf16[2,384,768]{2,1,0:T(8,128)(2,1)} %get-tuple-element.142.b), custom_call_target="tpu_custom_call" | custom-call | flops 3623878656 | bytes 4718592 | tf_op jit(solution)/shard_map/grad_down/pallas_call | solution.py:666
  410.4 9.2 %grad_up.1 = bf16[768,3072]{1,0:T(8,128)(2,1)} custom-call(bf16[2,384,768]{2,1,0:T(8,128)(2,1)} %get-tuple-element.139.a, bf16[2,384,3072]{2,1,0:T(8,128)(2,1)} %get-tuple-element.140.b), custom_call_target="tpu_custom_call" | custom-call | flops 3623878656 | bytes 4718592 | tf_op jit(solution)/shard_map/grad_up/pallas_call | solution.py:666
  419.6 0.6 copy-done.18
  420.3 0.6 dynamic-slice
  421.0 0.1 reshape.177
  421.1 0.1 reshape.178
  421.3 58.4 %all-reduce = f32[16,576]{1,0:T(8,128)S(1)} all-reduce(f32[16,576]{1,0:T(8,128)S(1)} %pad_maximum_fusion.1), channel_id=5, replica_groups=mesh['section'=2,'dp'=16] {'dp'}, use_global_device_ids=true, to_apply=%region_1.2.clone | all-reduce | flops 9216 | bytes 73728
  479.7 1.3 dynamic-slice.7
  481.0 1.3 fusion.9
  482.3 1.6 bitcast_convert_fusion.3
  483.8 16.2 %reduce-scatter.5.cloned.1.call-done = bf16[48,2304]{1,0:T(8,128)(2,1)} async-done(((bf16[768,2304]{1,0:T(8,128)(2,1)}), bf16[48,2304]{1,0:T(8,128)(2,1)}) %reduce-scatter.5.cloned.1.call-update) | async-done | bytes 221200 | tf_op jit(solution)/shard_map/reduce_scatter | solution.py:781
  500.0 1.7 bitcast_convert_fusion.2
  501.8 76.5 %reduce-scatter.11.cloned.1.call-done = bf16[192,768]{1,0:T(8,128)(2,1)} async-done(((bf16[3072,768]{1,0:T(8,128)(2,1)}), bf16[192,768]{1,0:T(8,128)(2,1)}) %reduce-scatter.11.cloned.1.call-update) | async-done | bytes 294928 | tf_op jit(solution)/shard_map/reduce_scatter | solution.py:781
  578.2 1.8 bitcast_convert_fusion
  580.0 77.2 %reduce-scatter.9.cloned.1.call-done = bf16[48,3072]{1,0:T(8,128)(2,1)} async-done(((bf16[768,3072]{1,0:T(8,128)(2,1)}), bf16[48,3072]{1,0:T(8,128)(2,1)}) %reduce-scatter.9.cloned.1.call-update) | async-done | bytes 294928 | tf_op jit(solution)/shard_map/reduce_scatter | solution.py:781
  657.2 1.8 bitcast_convert_fusion.1
  (75 shorter events, 0.8 us)
Async XLA Ops:
  7.2 5.0 copy-start.1
  7.2 5.8 copy-start.9
  7.2 5.8 copy-start.10
  7.2 5.8 copy-start.11
  7.2 5.8 copy-start.12
  7.2 5.9 copy-start.13
  7.2 5.9 copy-start.14
  7.3 5.9 copy-start.15
  7.3 5.9 copy-start.16
  7.3 5.9 copy-start.17
  7.3 30.4 %copy-start.7 = (s32[2,1]{0,1:T(1,128)S(1)}, s32[2,1]{0,1:T(1,128)}, u32[]{:S(2)}) copy-start(s32[2,1]{0,1:T(1,128)} %param.19) | copy-start | bytes 28
  7.3 31.1 %copy-start.8 = (s32[2,6]{1,0:T(2,128)S(1)}, s32[2,6]{1,0:T(2,128)}, u32[]{:S(2)}) copy-start(s32[2,6]{1,0:T(2,128)} %param.20) | copy-start | bytes 148
  7.3 59.9 %all-gather.7.cloned.1.call-start = ((), (), s32[]{:S(2)}) async-start(), calls=%async_computation.4 | async-start | bytes 5013504 | tf_op jit(solution)/shard_map/all_gather | solution.py:717
  10.2 111.8 %all-gather.9.cloned.1.call-start = ((), (), s32[]{:S(2)}) async-start(), calls=%async_computation.9 | async-start | bytes 5013504 | tf_op jit(solution)/shard_map/all_gather | solution.py:719
  12.1 164.8 %all-gather.11.cloned.1.call-start = ((), (), s32[]{:S(2)}) async-start(), calls=%async_computation.10 | async-start | bytes 5013504 | tf_op jit(solution)/shard_map/all_gather | solution.py:720
  12.9 469.3 %reduce-scatter.7.cloned.1.call-start = ((), (), s32[]{:S(2)}) async-start(), calls=%async_computation.6 | async-start | bytes 1253376 | tf_op jit(solution)/shard_map/reduce_scatter | solution.py:781
  207.4 14.9 %collective-permute-start = (bf16[384,768]{1,0:T(8,128)(2,1)}, bf16[384,768]{1,0:T(8,128)(2,1)S(1)}, u32[]{:S(2)}, u32[]{:S(2)}) collective-permute-start(bf16[384,768]{1,0:T(8,128)(2,1)} %get-tuple-element.79), channel_id=1, source_target_pairs={{0,16},{1,17},{2,18},{3,19},{4,20},{5,21},{6,22},{7,23},{8,24},{9,... | collective-permute-start | bytes 1769480 | tf_op jit(solution)/shard_map/ppermute | solution.py:686
  222.3 0.8 copy-start.4
  247.6 22.6 %collective-permute-start.1 = (bf16[384,768]{1,0:T(8,128)(2,1)}, bf16[384,768]{1,0:T(8,128)(2,1)S(1)}, u32[]{:S(2)}, u32[]{:S(2)}) collective-permute-start(bf16[384,768]{1,0:T(8,128)(2,1)} %get-tuple-element.92), channel_id=1, source_target_pairs={{0,16},{1,17},{2,18},{3,19},{4,20},{5,21},{6,22},{7,23},{8,24},{9,... | collective-permute-start | bytes 1769480 | tf_op jit(solution)/shard_map/ppermute | solution.py:686
  259.4 40.4 %collective-permute-start.2 = (bf16[384,768]{1,0:T(8,128)(2,1)}, bf16[384,768]{1,0:T(8,128)(2,1)S(1)}, u32[]{:S(2)}, u32[]{:S(2)}) collective-permute-start(bf16[384,768]{1,0:T(8,128)(2,1)} %get-tuple-element.108), channel_id=1, source_target_pairs={{16,0},{17,1},{18,2},{19,3},{20,4},{21,5},{22,6},{23,7},{24,8},{25... | collective-permute-start | bytes 1769480 | tf_op jit(solution)/shard_map/ppermute | solution.py:686
  270.2 0.8 copy-start.2
  299.8 0.8 copy-start.3
  328.9 28.7 %collective-permute-start.3 = (bf16[384,768]{1,0:T(8,128)(2,1)}, bf16[384,768]{1,0:T(8,128)(2,1)S(1)}, u32[]{:S(2)}, u32[]{:S(2)}) collective-permute-start(bf16[384,768]{1,0:T(8,128)(2,1)} %get-tuple-element.124), channel_id=1, source_target_pairs={{16,0},{17,1},{18,2},{19,3},{20,4},{21,5},{22,6},{23,7},{24,8},{25... | collective-permute-start | bytes 1769480 | tf_op jit(solution)/shard_map/ppermute | solution.py:686
  357.7 0.8 copy-start.5
  375.3 124.8 %reduce-scatter.5.cloned.1.call-start = ((), (), s32[]{:S(2)}) async-start(), calls=%async_computation.5 | async-start | bytes 3760128 | tf_op jit(solution)/shard_map/reduce_scatter | solution.py:781
  397.9 180.3 %reduce-scatter.11.cloned.1.call-start = ((), (), s32[]{:S(2)}) async-start(), calls=%async_computation.8 | async-start | bytes 5013504 | tf_op jit(solution)/shard_map/reduce_scatter | solution.py:781
  410.3 246.9 %reduce-scatter.9.cloned.1.call-start = ((), (), s32[]{:S(2)}) async-start(), calls=%async_computation.7 | async-start | bytes 5013504 | tf_op jit(solution)/shard_map/reduce_scatter | solution.py:781
  419.6 0.7 copy-start.18
  419.6 1.2 copy-start
  419.6 1.3 copy-start.6
Sparse Core Ops, SparseCore 0:
  11.0 56.1 all-gather.6
  70.1 51.9 all-gather.8
  124.9 51.9 all-gather.10
  375.4 53.9 reduce-scatter.6
  433.1 66.9 reduce-scatter.4
  503.7 74.4 reduce-scatter.10
  582.6 74.5 reduce-scatter.8

commit v2 on v1

v2 whole, which is shorter than its diff:
```python
import functools

import jax
import jax.numpy as jnp
from jax import lax
from jax.experimental import pallas as pl
from jax.experimental.pallas import tpu as pltpu
from jax.sharding import PartitionSpec as P

HEADS = 12
SEGMENT = 64
PAIRS = 6
ROWS = 384
EPSILON = 1e-06
MASKED = -1000000000.0
LANES = 128
FF_TILE = 1024
LIMIT = 10
LIMIT_GRAD = 16
VMEM_LIMIT = 60 * 1024 * 1024
F32 = jnp.float32
BF16 = jnp.bfloat16

BIAS_Q, BIAS_K, BIAS_V, BIAS_OUT, GAIN_ATTN, SHIFT_ATTN, BIAS_DOWN, GAIN_FFN, SHIFT_FFN = range(9)
RUN, MICRO, SECTION, BUCKET, LENGTHS = range(5)
CORE, Y = LENGTHS + PAIRS, LENGTHS + PAIRS + 1

ANY = pl.BlockSpec(memory_space=pl.ANY)
WHOLE = pl.BlockSpec(memory_space=pltpu.VMEM)
SCALARS = pl.BlockSpec(memory_space=pltpu.SMEM)


def dot_nn(a, b):
    return lax.dot_general(a, b, (((1,), (0,)), ((), ())), preferred_element_type=F32)


def dot_nt(a, b):
    return lax.dot_general(a, b, (((1,), (1,)), ((), ())), preferred_element_type=F32)


def dot_tn(a, b):
    return lax.dot_general(a, b, (((0,), (0,)), ((), ())), preferred_element_type=F32)


class Row:
    def __init__(self, table, row):
        self.table, self.row = table, row

    def __getitem__(self, at):
        return self.table[self.row, at]


def fold(values):
    rows, n = values.shape
    return jnp.sum(values.reshape(rows // 8, 8, n), axis=0)


def write_bias(info, bias, block, count):
    segment = (info[BUCKET] + 1) * SEGMENT
    per_block = jnp.where(info[BUCKET] == 0, block // SEGMENT, 1)
    k_row = lax.broadcasted_iota(jnp.int32, (block, block), 0)
    q_row = lax.broadcasted_iota(jnp.int32, (block, block), 1)

    def pair_of(row):
        return (row >= segment).astype(jnp.int32) + (row >= 2 * segment).astype(jnp.int32)

    k_pair = pair_of(k_row)
    same = k_pair == pair_of(q_row)
    position = k_row - k_pair * segment
    for at in range(count):
        valid = [
            jnp.minimum(info[LENGTHS + jnp.minimum(at * per_block + i, PAIRS - 1)], segment)
            for i in range(3)
        ]
        length = jnp.where(k_pair == 0, valid[0], jnp.where(k_pair == 1, valid[1], valid[2]))
        bias[at, :block, :block] = jnp.where(same & (position < length), 0.0, MASKED)


def half_masks():
    lane = lax.broadcasted_iota(jnp.int32, (1, LANES), 1)
    low = (lane < LANES // 2).astype(F32)
    return low.astype(BF16), (1.0 - low).astype(BF16)


def by_block(info, body):
    @pl.when(info[BUCKET] == 1)
    def _():
        body(2 * SEGMENT, ROWS // (2 * SEGMENT))

    @pl.when(info[BUCKET] != 1)
    def _():
        body(3 * SEGMENT, ROWS // (3 * SEGMENT))


def attention(info, qkv, context, lse, bias):
    width = context.shape[1]
    low, high = half_masks()

    def body(block, count):
        write_bias(info, bias, block, count)

        def pair_step(pair, carry):
            at_q = pl.multiple_of(pair * LANES, LANES)
            at_k = pl.multiple_of(width + pair * LANES, LANES)
            at_v = pl.multiple_of(2 * width + pair * LANES, LANES)
            is_low = lax.broadcasted_iota(jnp.int32, (block, LANES), 1) < LANES // 2
            units = [(at, half) for at in range(count) for half in range(2)]
            rows = [pl.ds(at * block, block) for at in range(count)]
            q = [qkv[r, pl.ds(at_q, LANES)] for r in rows]
            k = [qkv[r, pl.ds(at_k, LANES)] for r in rows]
            v = [qkv[r, pl.ds(at_v, LANES)] for r in rows]
            scores = [
                dot_nt(k[at] * (low, high)[half], q[at]) + bias[at, :block, :block]
                for at, half in units
            ]
            tops = [jnp.max(x, axis=0, keepdims=True) for x in scores]
            weights = [jnp.exp(x - top) for x, top in zip(scores, tops)]
            totals = [jnp.sum(x, axis=0, keepdims=True) for x in weights]
            probs = [(x * (1.0 / total)).astype(BF16) for x, total in zip(weights, totals)]
            parts = [dot_tn(x, v[at]) for x, (at, half) in zip(probs, units)]
            for index, (at, half) in enumerate(units):
                lse[2 * pair + half, at : at + 1, :block] = tops[index] + jnp.log(
                    totals[index]
                )
            for at in range(count):
                context[rows[at], pl.ds(at_q, LANES)] = jnp.where(
                    is_low, parts[2 * at], parts[2 * at + 1]
                ).astype(BF16)
            return carry

        lax.fori_loop(0, HEADS // 2, pair_step, 0)

    by_block(info, body)


def attention_back(info, qkv, d_context, lse, bias, d_qkv):
    width = d_context.shape[1]
    low, high = half_masks()
    scale = (width // HEADS) ** -0.5

    def body(block, count):
        write_bias(info, bias, block, count)

        def pair_step(pair, carry):
            at_q = pl.multiple_of(pair * LANES, LANES)
            at_k = pl.multiple_of(width + pair * LANES, LANES)
            at_v = pl.multiple_of(2 * width + pair * LANES, LANES)
            is_low = lax.broadcasted_iota(jnp.int32, (block, LANES), 1) < LANES // 2
            units = [(at, half) for at in range(count) for half in range(2)]
            rows = [pl.ds(at * block, block) for at in range(count)]
            q = [qkv[r, pl.ds(at_q, LANES)] for r in rows]
            k = [qkv[r, pl.ds(at_k, LANES)] for r in rows]
            v = [qkv[r, pl.ds(at_v, LANES)] for r in rows]
            d_out = [d_context[r, pl.ds(at_q, LANES)] for r in rows]
            scores = [
                dot_nt(k[at] * (low, high)[half], q[at]) + bias[at, :block, :block]
                for at, half in units
            ]
            d_probs = [dot_nt(v[at] * (low, high)[half], d_out[at]) for at, half in units]
            probs = [
                jnp.exp(x - lse[2 * pair + half, at : at + 1, :block])
                for x, (at, half) in zip(scores, units)
            ]
            d_v = [dot_nn(x.astype(BF16), d_out[at]) for x, (at, half) in zip(probs, units)]
            inner = [jnp.sum(x * d_x, axis=0, keepdims=True) for x, d_x in zip(probs, d_probs)]
            d_scores = [
                (x * (d_x - total)).astype(BF16)
                for x, d_x, total in zip(probs, d_probs, inner)
            ]
            d_k = [dot_nn(x, q[at]) for x, (at, half) in zip(d_scores, units)]
            d_q = [dot_tn(x, k[at]) for x, (at, half) in zip(d_scores, units)]
            for at in range(count):
                one, two = 2 * at, 2 * at + 1
                r = rows[at]
                d_qkv[r, pl.ds(at_q, LANES)] = (
                    jnp.where(is_low, d_q[one], d_q[two]) * scale
                ).astype(BF16)
                d_qkv[r, pl.ds(at_k, LANES)] = jnp.where(
                    is_low, d_k[one], d_k[two]
                ).astype(BF16)
                d_qkv[r, pl.ds(at_v, LANES)] = jnp.where(
                    is_low, d_v[one], d_v[two]
                ).astype(BF16)
            return carry

        lax.fori_loop(0, HEADS // 2, pair_step, 0)

    by_block(info, body)


def norm(values):
    centered = values - jnp.mean(values, axis=-1, keepdims=True)
    inverse = lax.rsqrt(jnp.mean(centered * centered, axis=-1, keepdims=True) + EPSILON)
    return centered * inverse, inverse


def norm_back(upstream, normed, inverse, gain):
    scaled = upstream * gain
    return inverse * (
        scaled
        - jnp.mean(scaled, axis=-1, keepdims=True)
        - normed * jnp.mean(scaled * normed, axis=-1, keepdims=True)
    )


CHUNK = 64


def by_rows(step, carry=0):
    def body(i, carry):
        return step(pl.ds(pl.multiple_of(i * CHUNK, CHUNK), CHUNK), carry)

    return lax.fori_loop(0, ROWS // CHUNK, body, carry)


def carry_over(src, dst):
    if src.shape[0] == ROWS:

        def step(rows, carry):
            dst[rows, :] = src[rows, :]
            return carry

        by_rows(step)
    else:
        dst[...] = src[...]


def kernel_call(body, name, step, ins, out_shapes, held, after, scratch, flops, limit):
    held = [] if held is None else list(held)
    given = len(ins) - 1

    def kernel(table, *refs):
        info = Row(table, step)
        kept = refs[given : given + len(held)]
        outs = refs[given + len(held) + len(after) :]

        @pl.when(info[RUN] == 1)
        def _():
            body(info, *refs[:given], *outs)

        if held:

            @pl.when(info[RUN] != 1)
            def _():
                for src, dst in zip(kept, outs):
                    carry_over(src, dst)

    return pl.pallas_call(
        kernel,
        in_specs=[SCALARS] + [WHOLE] * (given + len(held)) + [ANY] * len(after),
        out_specs=[WHOLE] * len(out_shapes),
        out_shape=[jax.ShapeDtypeStruct(shape, kind) for shape, kind in out_shapes],
        input_output_aliases={1 + given + i: i for i in range(len(held))},
        scratch_shapes=scratch,
        compiler_params=pltpu.CompilerParams(vmem_limit_bytes=limit * 1024 * 1024),
        cost_estimate=pl.CostEstimate(flops=flops, bytes_accessed=0, transcendentals=0),
        name=name,
    )(*ins, *held, *after)


def forward_attn_body(info, tok, rec, w_a, small, x, qkv, lse, context, n1, inv1, hid, acc, bias):
    width = x.shape[1]

    micro = info[MICRO]

    @pl.when(info[SECTION] == 0)
    def _():
        x[...] = tok[micro]

    @pl.when(info[SECTION] != 0)
    def _():
        x[...] = rec[...]

    for j, (row, factor) in enumerate(
        ((BIAS_Q, (width // HEADS) ** -0.5), (BIAS_K, 1.0), (BIAS_V, 1.0))
    ):
        cols = slice(j * width, (j + 1) * width)
        part = dot_nn(x[...], w_a[:, cols]) + small[row : row + 1, :]
        qkv[:, cols] = (part * factor).astype(BF16)
    attention(info, qkv, context, lse, bias)
    acc[...] = dot_nn(context[...], w_a[:, 3 * width : 4 * width])

    def norm_one(rows, carry):
        total = x[rows, :].astype(F32) + acc[rows, :]
        normed, inverse = norm(total + small[BIAS_OUT : BIAS_OUT + 1, :])
        n1[rows, :] = normed
        inv1[rows, :] = jnp.broadcast_to(inverse, (CHUNK, LANES))
        hidden = normed * small[GAIN_ATTN : GAIN_ATTN + 1, :]
        hid[rows, :] = (hidden + small[SHIFT_ATTN : SHIFT_ATTN + 1, :]).astype(BF16)
        return carry

    by_rows(norm_one)


def forward_ffn_body(
    info, w_up, w_down, small, bias_up, n1, hid, act, d_act, n2, inv2, out, acc
):
    ff = act.shape[1]

    def up(j):
        cols = slice(j * FF_TILE, (j + 1) * FF_TILE)
        pre = dot_nn(hid[...], w_up[:, cols]) + bias_up[:, cols]
        below = 0.5 * (1.0 + lax.erf(pre * 0.7071067811865476))
        density = jnp.exp(pre * pre * -0.5) * 0.3989422804014327
        act[:, cols] = (pre * below).astype(BF16)
        d_act[:, cols] = (below + pre * density).astype(BF16)

    def down(j):
        cols = slice(j * FF_TILE, (j + 1) * FF_TILE)
        part = dot_nn(act[:, cols], w_down[cols, :])
        acc[...] = part if j == 0 else acc[...] + part

    up(0)
    for j in range(1, ff // FF_TILE):
        up(j)
        down(j - 1)
    down(ff // FF_TILE - 1)

    def norm_two(rows, carry):
        hidden = n1[rows, :] * small[GAIN_ATTN : GAIN_ATTN + 1, :]
        hidden = hidden + small[SHIFT_ATTN : SHIFT_ATTN + 1, :]
        normed, inverse = norm(hidden + acc[rows, :] + small[BIAS_DOWN : BIAS_DOWN + 1, :])
        n2[rows, :] = normed
        inv2[rows, :] = jnp.broadcast_to(inverse, (CHUNK, LANES))
        low = (
            normed * small[GAIN_FFN : GAIN_FFN + 1, :] + small[SHIFT_FFN : SHIFT_FFN + 1, :]
        ).astype(BF16)
        out[rows, :] = low
        return carry

    by_rows(norm_two)


def bias_scratch():
    return pltpu.VMEM((3, 3 * SEGMENT, 3 * SEGMENT), F32)


def forward_attn(step, info, tokens, received, w_a, small, held=None, after=()):
    width = small.shape[1]
    shapes = (
        ((ROWS, width), BF16),
        ((ROWS, 3 * width), BF16),
        ((HEADS, 8, 256), F32),
        ((ROWS, width), BF16),
        ((ROWS, width), F32),
        ((ROWS, LANES), F32),
        ((ROWS, width), BF16),
    )
    return kernel_call(
        forward_attn_body,
        "forward_attn",
        step,
        (info, tokens, received, w_a, small),
        shapes,
        held,
        after,
        [pltpu.VMEM((ROWS, width), F32), bias_scratch()],
        8 * ROWS * width * width + 4 * ROWS * ROWS * width,
        LIMIT,
    )


def forward_ffn(step, info, w_up, w_down, small, bias_up, n1, hid, held=None, after=()):
    width, ff = small.shape[1], bias_up.shape[1]
    shapes = (
        ((ROWS, ff), BF16),
        ((ROWS, ff), BF16),
        ((ROWS, width), F32),
        ((ROWS, LANES), F32),
        ((ROWS, width), BF16),
    )
    return kernel_call(
        forward_ffn_body,
        "forward_ffn",
        step,
        (info, w_up, w_down, small, bias_up, n1, hid),
        shapes,
        held,
        after,
        [pltpu.VMEM((ROWS, width), F32)],
        4 * ROWS * width * ff,
        LIMIT,
    )


def norm_back_rows(upstream, normed, inverse, gain, grad, low):
    zeros = jnp.zeros((8, grad.shape[1]), F32)

    def step(rows, carry):
        up, nm = upstream(rows), normed(rows)
        values = norm_back(up, nm, inverse(rows), gain)
        grad[rows, :] = values
        rounded = values.astype(BF16)
        low(rows, rounded)
        return (
            carry[0] + fold(up),
            carry[1] + fold(up * nm),
            carry[2] + fold(rounded.astype(F32)),
        )

    sums = by_rows(step, (zeros, zeros, zeros))
    return [jnp.sum(part, axis=0, keepdims=True) for part in sums]


def ffn_back_body(
    info,
    cot,
    rec,
    w_up,
    w_down,
    small,
    n1,
    inv1,
    d_act,
    n2,
    inv2,
    d_ffn,
    d_pre,
    d_branch,
    sums,
    d_first,
    acc,
):
    width = rec.shape[1]
    ff = d_pre.shape[1]
    tiles = ff // FF_TILE

    micro = info[MICRO]
    last = info[SECTION] == 1

    def upstream(rows):
        return jnp.where(last, cot[micro, rows, :], rec[rows, :]).astype(F32)

    def keep_ffn(rows, low):
        d_ffn[rows, :] = low

    sum_g, sum_gn, sum_d = norm_back_rows(
        upstream,
        lambda rows: n2[rows, :],
        lambda rows: inv2[rows, :1],
        small[GAIN_FFN : GAIN_FFN + 1, :],
        acc,
        keep_ffn,
    )
    sums[1:2, :width] = sum_d
    sums[1:2, width : 2 * width] = sum_gn
    sums[1:2, 2 * width : 3 * width] = sum_g

    def first(j):
        cols = slice(j * FF_TILE, (j + 1) * FF_TILE)
        part = dot_nt(d_ffn[...], w_down[cols, :]) * d_act[:, cols].astype(F32)
        low = part.astype(BF16)
        d_pre[:, cols] = low
        sums[0:1, cols] = jnp.sum(fold(low.astype(F32)), axis=0, keepdims=True)

    def second(j):
        cols = slice(j * FF_TILE, (j + 1) * FF_TILE)
        acc[...] += dot_nt(d_pre[:, cols], w_up[:, cols])

    first(0)
    for j in range(1, tiles):
        first(j)
        second(j - 1)
    second(tiles - 1)

    def keep_branch(rows, low):
        d_branch[rows, :] = low

    sum_g, sum_gn, sum_d = norm_back_rows(
        lambda rows: acc[rows, :],
        lambda rows: n1[rows, :],
        lambda rows: inv1[rows, :1],
        small[GAIN_ATTN : GAIN_ATTN + 1, :],
        d_first,
        keep_branch,
    )
    sums[1:2, 3 * width :] = sum_gn
    sums[2:3, :width] = sum_g
    sums[2:3, width : 2 * width] = sum_d


def ffn_back(step, info, cotangent, received, w_up, w_down, small, attn, ffn, held=None, after=()):
    width, ff = w_up.shape
    shapes = (
        ((ROWS, width), BF16),
        ((ROWS, ff), BF16),
        ((ROWS, width), BF16),
        ((8, ff), F32),
        ((ROWS, width), F32),
    )
    return kernel_call(
        ffn_back_body,
        "ffn_backward",
        step,
        (info, cotangent, received, w_up, w_down, small, attn[4], attn[5], ffn[1], ffn[2], ffn[3]),
        shapes,
        held,
        after,
        [pltpu.VMEM((ROWS, width), F32)],
        4 * ROWS * width * ff,
        LIMIT,
    )


def attn_back_body(
    info, w_a, d_first, d_branch, qkv, lse, d_qkv, grads, sums, d_context, bias
):
    width = d_first.shape[1]

    d_context[...] = dot_nt(d_branch[...], w_a[:, 3 * width : 4 * width]).astype(BF16)
    attention_back(info, qkv, d_context, lse, bias, d_qkv)
    grad = d_first[...] + dot_nt(d_qkv[...], w_a[:, : 3 * width])
    low = grad.astype(BF16)
    grads[...] = low
    for row, at in ((0, 0), (1, 2 * width)):
        sums[row : row + 1, :] = jnp.sum(
            fold(d_qkv[:, at : at + width].astype(F32)), axis=0, keepdims=True
        )


def attn_back(step, info, w_a, d_first, d_branch, attn, held=None, after=()):
    width = d_first.shape[1]
    shapes = (
        ((ROWS, 3 * width), BF16),
        ((ROWS, width), BF16),
        ((8, width), F32),
    )
    return kernel_call(
        attn_back_body,
        "attention_backward",
        step,
        (info, w_a, d_first, d_branch, attn[1], attn[2]),
        shapes,
        held,
        after,
        [pltpu.VMEM((ROWS, width), BF16), bias_scratch()],
        8 * ROWS * width * width + 10 * ROWS * ROWS * width,
        LIMIT,
    )


def split_blocks(values, place, mine, theirs, cols, first_z=0):
    share = mine.shape[2]
    core, y = place[0], place[1]
    zs = values.shape[0] // (4 * share)
    for z in range(zs):
        for yy in range(2):
            first = values[(z * 4 + yy * 2) * share : (z * 4 + yy * 2 + 1) * share].astype(BF16)
            second = values[(z * 4 + yy * 2 + 1) * share : (z * 4 + yy * 2 + 2) * share].astype(BF16)
            to = jnp.bitwise_xor(y, yy)

            @pl.when(core == 0)
            def _():
                mine[pl.ds(to, 1), first_z + z, :, cols] = first[None]
                theirs[pl.ds(to, 1), first_z + z, :, cols] = second[None]

            @pl.when(core == 1)
            def _():
                theirs[pl.ds(to, 1), first_z + z, :, cols] = first[None]
                mine[pl.ds(to, 1), first_z + z, :, cols] = second[None]


def both(refs, cols=slice(None)):
    return jnp.concatenate([ref[:, cols] for ref in refs], axis=0)


def grad_call(body, name, place, ins, share, n, after):
    shape = jax.ShapeDtypeStruct((2, 4, share, n), BF16)

    def kernel(place, *refs):
        body(place, *refs[: len(ins)], *refs[-2:])

    return pl.pallas_call(
        kernel,
        in_specs=[SCALARS] + [WHOLE] * len(ins) + [ANY] * len(after),
        out_specs=[WHOLE] * 2,
        out_shape=[shape, shape],
        compiler_params=pltpu.CompilerParams(vmem_limit_bytes=LIMIT_GRAD * 1024 * 1024),
        cost_estimate=pl.CostEstimate(
            flops=4 * ROWS * 16 * share * n, bytes_accessed=0, transcendentals=0
        ),
        name=name,
    )(place, *ins, *after)


def grad_by_rows_body(place, a, a2, b, b2, mine, theirs):
    rows = 4 * mine.shape[2]
    right = both((b, b2))
    for z in range(4):
        left = both((a, a2), slice(z * rows, (z + 1) * rows))
        split_blocks(dot_tn(left, right), place, mine, theirs, slice(None), z)


def grad_by_cols_body(place, a, a2, b, b2, mine, theirs):
    tile = 768
    left = both((a, a2))
    for at in range(0, b.shape[1], tile):
        cols = slice(at, at + tile)
        split_blocks(dot_tn(left, both((b, b2), cols)), place, mine, theirs, cols)


def grad_attn_body(
    place, x, x2, d_qkv, d_qkv2, context, context2, d_branch, d_branch2, table, mine, theirs
):
    width = x.shape[1]
    grad_by_cols_body(place, x, x2, d_qkv, d_qkv2, mine, theirs)
    values = dot_tn(both((context, context2)), both((d_branch, d_branch2)))
    split_blocks(values, place, mine, theirs, slice(3 * width, 4 * width))
    split_blocks(table[...], place, mine, theirs, slice(4 * width, 4 * width + LANES))


def grad_by_rows(place, a, b, name, after=()):
    share, n = a[0].shape[1] // 16, b[0].shape[1]
    return grad_call(grad_by_rows_body, name, place, (*a, *b), share, n, after)


def grad_by_cols(place, a, b, name, after=()):
    share, n = a[0].shape[1] // 16, b[0].shape[1]
    return grad_call(grad_by_cols_body, name, place, (*a, *b), share, n, after)


def grad_attn(place, x, d_qkv, context, d_branch, table, after=()):
    width = x[0].shape[1]
    ins = (*x, *d_qkv, *context, *d_branch, table)
    return grad_call(
        grad_attn_body, "grad_attn", place, ins, width // 16, 4 * width + LANES, after
    )


def join_body(place, own, other, own_sibling, other_sibling, out, sems):
    core, y = place[0], place[1]
    share = own.shape[1]
    copies = []
    for src, dy, dc in ((own, 0, 0), (other, 1, 0), (own_sibling, 0, 1), (other_sibling, 1, 1)):
        for z in range(4):
            at = z * 4 + jnp.bitwise_xor(y, dy) * 2 + jnp.bitwise_xor(core, dc)
            rows = pl.ds(pl.multiple_of(at * share, 16), share)
            copy = pltpu.make_async_copy(src.at[z], out.at[rows, :], sems.at[len(copies)])
            copy.start()
            copies.append(copy)
    for copy in copies:
        copy.wait()


def in_order(place, parts, name):
    z, share, n = parts[0].shape
    return pl.pallas_call(
        join_body,
        in_specs=[SCALARS] + [ANY] * 4,
        out_specs=WHOLE,
        out_shape=jax.ShapeDtypeStruct((4 * z * share, n), BF16),
        scratch_shapes=[pltpu.SemaphoreType.DMA((16,))],
        compiler_params=pltpu.CompilerParams(vmem_limit_bytes=24 * 1024 * 1024),
        cost_estimate=pl.CostEstimate(flops=0, bytes_accessed=32 * z * share * n, transcendentals=0),
        name=name,
    )(place, *parts)


def weight_grad(a, b):
    return sum(dot_tn(one, two) for one, two in zip(a, b)).astype(BF16)


def tie(value, *others):
    return lax.optimization_barrier((value, others))[0]


class Grid:
    def __init__(self):
        self.index = lax.axis_index("dp")
        self.z = self.index // 4
        self.y = (self.index // 2) % 2
        self.core = self.index % 2

    def swap_core(self, block):
        return lax.ppermute(block, "dp", [(i, i ^ 1) for i in range(16)])

    def swap_y(self, block):
        return lax.ppermute(block, "dp", [(i, i ^ 2) for i in range(16)])

    def shift(self, block, step, low, high):
        return lax.ppermute(
            block, "dp", [(i, i + 4 * step) for i in range(4 * low, 4 * high + 4)]
        )

    def near(self, block):
        return self.shift(block, 1, 0, 2), self.shift(block, -1, 1, 3)

    def far(self, got):
        up, down = got
        return (
            self.shift(up, 1, 1, 2),
            self.shift(down, -1, 1, 2),
            self.shift(up, 2, 1, 1),
            self.shift(down, -2, 2, 2),
        )

    def in_line(self, block, near, far):
        ups, downs = (near[0], far[0], far[2]), (near[1], far[1], far[3])

        def found(z, at):
            if z == at:
                return block
            return ups[z - at - 1] if z > at else downs[at - z - 1]

        picked = []
        for at in range(4):
            value = found(3, at)
            for z in range(3):
                value = jnp.where(self.z == z, found(z, at), value)
            picked.append(value)
        return jnp.stack(picked)

    def gather(self, part_a, part_up, part_down):
        near_a = self.near(part_a)
        down_other = self.swap_y(part_down)
        far_a = self.far(near_a)
        near_up = self.near(tie(part_up, *near_a))
        own_a = self.in_line(part_a, near_a, far_a)
        other_a = self.swap_y(own_a)
        far_up = self.far(tie(near_up, *far_a))
        down = tie(jnp.stack([part_down, down_other]), *far_a)
        near_down = self.near(down)
        own_up = self.in_line(part_up, near_up, far_up)
        other_up = self.swap_y(own_up)
        far_down = self.far(tie(near_down, *far_up))
        both = self.in_line(down, near_down, far_down)
        own_down, other_down = both[:, 0], both[:, 1]
        return tuple(
            (own, other, self.swap_core(own), self.swap_core(other))
            for own, other in ((own_a, other_a), (own_up, other_up), (own_down, other_down))
        )

    def ordered(self, pieces):
        own, other, own_sibling, other_sibling = pieces

        def by_y(one, two):
            first = self.y == 0
            return jnp.stack([jnp.where(first, one, two), jnp.where(first, two, one)], axis=1)

        mine, theirs = by_y(own, other), by_y(own_sibling, other_sibling)
        first = self.core == 0
        both = jnp.stack([jnp.where(first, mine, theirs), jnp.where(first, theirs, mine)], axis=2)
        return both.reshape((-1,) + both.shape[4:])

    def block(self, total, at):
        return lax.dynamic_index_in_dim(total, jnp.clip(at, 0, 3), 1, keepdims=False)

    def for_far(self, total):
        three_up, three_down = total[:, 3], total[:, 0]
        return tuple(
            part.astype(BF16)
            for part in (
                self.block(total, self.z + 2),
                self.block(total, self.z - 2),
                three_up,
                three_down,
            )
        )

    def send_far(self, sent):
        return (
            self.shift(sent[0], 1, 0, 1),
            self.shift(sent[1], -1, 2, 3),
            self.shift(sent[2], 2, 0, 0),
            self.shift(sent[3], -2, 3, 3),
        )

    def for_near(self, total, got):
        up, down, up_two, down_two = (part.astype(F32) for part in got)
        return (
            (self.block(total, self.z + 1) + up + up_two).astype(BF16),
            (self.block(total, self.z - 1) + down + down_two).astype(BF16),
        )

    def send_near(self, sent):
        return self.shift(sent[0], 1, 0, 2), self.shift(sent[1], -1, 1, 3)

    def line_end(self, total, got):
        return self.block(total, self.z) + got[0].astype(F32) + got[1].astype(F32)


def passed_along(block, axis, distance):
    devices = range(lax.axis_size(axis))
    route = [(i - distance, i) for i in devices if i - distance in devices]
    return lax.ppermute(block, axis, route)


def on_device(
    tokens,
    cotangent,
    bucket,
    lengths,
    w_qkv,
    bias_q,
    bias_v,
    w_out,
    bias_out,
    gain_attn,
    shift_attn,
    w_up,
    bias_up,
    w_down,
    bias_down,
    gain_ffn,
    shift_ffn,
):
    section = lax.axis_index("section")
    width = tokens.shape[2]
    ff = w_up.shape[2]
    share = bias_q.shape[1]
    n_dp = width // share
    vectors = (bias_q, bias_v, bias_out, gain_attn, shift_attn, bias_down, gain_ffn, shift_ffn)
    by_links = n_dp == 16 and share % 16 == 0
    low_up, low_down = w_up[0].astype(BF16), w_down[0].astype(BF16)
    columns = [v[0] for v in vectors] + list(bias_up[0].reshape(-1, share))
    table = jnp.stack(columns + [jnp.zeros((share,), F32)] * (LANES - len(columns)), axis=1)
    part_a = jnp.concatenate([w_qkv[0], w_out[0], table], axis=1).astype(BF16)
    if by_links:
        grid = Grid()
        place = jnp.stack([grid.core, grid.y])
        pieces = grid.gather(part_a, low_up, low_down)
        table = grid.ordered([piece[:, :, 4 * width :] for piece in pieces[0]]).astype(F32)
        w_a, full_up, full_down = (
            in_order(place, parts, name)
            for parts, name in zip(pieces, ("join_attn", "join_up", "join_down"))
        )
    else:
        place = jnp.zeros((2,), jnp.int32)
        w_a, full_up, full_down = (
            lax.all_gather(part, "dp", axis=0, tiled=True) for part in (part_a, low_up, low_down)
        )
        table = w_a[:, 4 * width :].astype(F32)
    rows = table[:, :8].T
    small = jnp.concatenate(
        [rows[:1], jnp.zeros((1, width), F32), rows[1:], jnp.zeros((7, width), F32)]
    )
    bias_columns = ff // width
    full_bias_up = table[:, 8 : 8 + bias_columns].reshape(n_dp, share, bias_columns)
    full_bias_up = full_bias_up.transpose(0, 2, 1).reshape(1, ff)

    def info(step, micro):
        picked = jnp.clip(micro, 0, 1)
        run = ((micro >= 0) & (micro <= 1)).astype(jnp.int32)
        head = jnp.stack([run, picked, section, lax.dynamic_index_in_dim(bucket, picked, 0, False)[0]])
        return jnp.concatenate([head, lax.dynamic_index_in_dim(lengths, picked, 0, False), place])

    steps = jnp.stack(
        [info(step, step - section) for step in range(3)]
        + [info(step, step - 1 + section) for step in range(3)]
    )
    none = jnp.zeros((ROWS, width), BF16)

    def ahead(step, received, held=None):
        attn_held, ffn_held = (None, None) if held is None else held
        attn = forward_attn(step, steps, tokens, received, w_a, small, attn_held)
        return attn, forward_ffn(
            step, steps, full_up, full_down, small, full_bias_up, attn[4], attn[6], ffn_held
        )

    def back_ffn(step, upstream, kept, held=None):
        return ffn_back(3 + step, steps, cotangent, upstream, full_up, full_down, small, *kept, held)

    outer = ahead(0, none)
    got = passed_along(outer[1][4], "section", 1)
    middle = ahead(1, got)
    got = passed_along(middle[1][4], "section", 1)
    back_outer = back_ffn(0, none, middle)
    back_attn_outer = attn_back(3, steps, w_a, back_outer[4], back_outer[2], middle[0])
    sent = passed_along(back_attn_outer[1], "section", -1)
    outer = ahead(2, got, outer)
    back_middle = back_ffn(1, sent, outer)
    back_attn_middle = attn_back(4, steps, w_a, back_middle[4], back_middle[2], outer[0])
    sent = passed_along(back_attn_middle[1], "section", -1)
    back_outer = back_ffn(2, sent, middle, back_outer)

    def last_attn_back(after=()):
        return attn_back(
            5, steps, w_a, back_outer[4], back_outer[2], middle[0], back_attn_outer, after
        )

    attn = tuple(zip(outer[0], middle[0]))
    ffn = tuple(zip(outer[1], middle[1]))
    d_ffn, d_pre, d_branch, sums_ffn, _ = zip(back_middle, back_outer)

    def by_micro(one, two):
        first = section == 0
        return jnp.stack([jnp.where(first, one, two), jnp.where(first, two, one)])[None]

    hidden_states = by_micro(*ffn[4])
    if by_links:
        mine, theirs = grad_by_rows(place, ffn[0], d_ffn, "grad_down")
        got_down = grid.swap_core(theirs)
        mine_up, theirs = grad_by_cols(place, attn[6], d_pre, "grad_up", after=(mine,))
        got_up = grid.swap_core(theirs)
        total_down = mine.astype(F32) + got_down.astype(F32)
        sent = grid.for_far(total_down)
        got_down = grid.send_far(sent)
        last = last_attn_back((mine_up,) + sent)
    else:
        last = last_attn_back()
    d_qkv, input_grads, sums_attn = zip(back_attn_middle, last)
    input_grads = by_micro(*input_grads)
    total = sums_ffn[0] + sums_ffn[1]
    total_attn = sums_attn[0] + sums_attn[1]
    vector = [
        total_attn[0],
        total_attn[1],
        total[2, width : 2 * width],
        total[1, 3 * width :],
        total[2, :width],
        total[1, :width],
        total[1, width : 2 * width],
        total[1, 2 * width : 3 * width],
    ]
    up_columns = total[0].reshape(n_dp, bias_columns, share).transpose(0, 2, 1)
    table = jnp.concatenate(
        [
            jnp.stack(vector, axis=1),
            up_columns.reshape(width, bias_columns),
            jnp.zeros((width, LANES - 8 - bias_columns), F32),
        ],
        axis=1,
    )
    if by_links:
        both_up = mine_up.astype(F32) + got_up.astype(F32)
        away_up = both_up[1].astype(BF16)
        sent = grid.for_near(total_down, got_down)
        got_down = grid.send_near(sent)
        got_up = grid.swap_y(away_up)
        mine_a, theirs = grad_attn(
            place, attn[0], d_qkv, attn[3], d_branch, table, after=sent + (away_up,)
        )
        got_a = grid.swap_core(theirs)
        both_a = mine_a.astype(F32) + got_a.astype(F32)
        got_a = grid.swap_y(both_a[1].astype(BF16))
        both_down = grid.line_end(total_down, got_down)
        got_down = grid.swap_y(both_down[1].astype(BF16))
        total_up = (both_up[0] + got_up.astype(F32))[None]
        got = grid.send_far(grid.for_far(total_up))
        got = grid.send_near(grid.for_near(total_up, got))
        g_up = grid.line_end(total_up, got)[0]
        g_down = both_down[0] + got_down.astype(F32)
        total_a = (both_a[0] + got_a.astype(F32))[None]
        got = grid.send_far(grid.for_far(total_a))
        got = grid.send_near(grid.for_near(total_a, got))
        g_a = grid.line_end(total_a, got)[0]
    else:

        def summed(values):
            return lax.psum_scatter(values, "dp", scatter_dimension=0, tiled=True).astype(F32)

        g_down = summed(weight_grad(ffn[0], d_ffn))
        g_up = summed(weight_grad(attn[6], d_pre))
        g_qkv = weight_grad(attn[0], d_qkv)
        g_out = weight_grad(attn[3], d_branch)
        g_a = summed(jnp.concatenate([g_qkv, g_out, table.astype(BF16)], axis=1))
    g_down, g_up = g_down[None], g_up[None]
    g_qkv, g_out = g_a[None, :, : 3 * width], g_a[None, :, 3 * width : 4 * width]
    g_vectors = [g_a[None, :, 4 * width + i] for i in range(8)]
    g_bias_up = g_a[:, 4 * width + 8 : 4 * width + 8 + bias_columns].T.reshape(1, ff // n_dp)
    (
        g_bias_q,
        g_bias_v,
        g_bias_out,
        g_gain_attn,
        g_shift_attn,
        g_bias_down,
        g_gain_ffn,
        g_shift_ffn,
    ) = g_vectors
    return (
        hidden_states,
        input_grads,
        g_qkv,
        g_bias_q,
        g_bias_v,
        g_out,
        g_bias_out,
        g_gain_attn,
        g_shift_attn,
        g_up,
        g_bias_up,
        g_down,
        g_bias_down,
        g_gain_ffn,
        g_shift_ffn,
    )


def solution(mesh):
    matrix = P("section", "dp", None)
    vector = P("section", "dp")
    rows = P(None, "dp", None)
    outs = P("section", None, "dp", None)
    params = (
        matrix,
        vector,
        vector,
        matrix,
        vector,
        vector,
        vector,
        matrix,
        vector,
        matrix,
        vector,
        vector,
        vector,
    )
    return jax.shard_map(
        on_device,
        mesh=mesh,
        in_specs=(rows, rows, P(None, "dp"), P(None, "dp")) + params,
        out_specs=(outs, outs) + params,
        check_vma=False,
    )
```

time: 678 us -> 446 us (0.66)
  waiting for transfers between devices: 378 us -> 171 us
  blocking collectives: 81.6 us -> 0 us
  starting transfers between devices: 14 us -> 89.7 us
  Pallas kernels: 146 us -> 94.7 us
  local copies, waits for them, and re-layouts: 17.6 us -> 45.5 us
  other arithmetic: 13.1 us -> 34.1 us
  between operations: 15.1 us -> 2.33 us
    reduce_scatter x4 -> x0, waiting for transfers between devices: 170 us -> none  [summed(): lax.psum_scatter(values, 'dp', scatter_dimension=0, tiled=True).astype(F32)]
    all_gather x3 -> x0, waiting for transfers between devices: 137 us -> none  [the longest x1 54.8 us: on_device(): full_down = lax.all_gather(w_down[0].astype(BF16), 'dp', axis=0, tiled=True)]
    ppermute x0 -> x51, waiting for transfers between devices: none -> 119 us  [the longest x36 78.1 us: shift(): lax.ppermute(block, 'dp', [(i, i + 4 * step) for i in range(4 * low, 4 *...]
    ppermute x0 -> x51, starting transfers between devices: none -> 82.4 us  [the longest x36 73.1 us: shift(): lax.ppermute(block, 'dp', [(i, i + 4 * step) for i in range(4 * low, 4 *...]
    unnamed x1 -> x0, blocking collectives: 58.4 us -> none
    pallas_call x13 -> x18, Pallas kernels: 146 us -> 94.7 us  [the longest x12 62.3 us: kernel_call(): pl.pallas_call(kernel, in_specs=[SCALARS] + [WHOLE] * (given + len(held))...]
    all_gather x1 -> x0, blocking collectives: 23.2 us -> none  [on_device(): smalls = lax.all_gather(part_s, 'dp', axis=0, tiled=True)]
    ppermute x4, waiting for transfers between devices: 71.9 us -> 52.2 us  [passed_along(): return lax.ppermute(block, axis, route)]
  transfers between devices with their start and end apart: 11 -> 55, of which waited for: 10 -> 18; matrix products, arithmetic and copies ran while one was open for 3% -> 11% of each run, Pallas kernels for 7% -> 8%
where the time goes in v2:
time: 446 us; the launch traced here: 438 us
  waiting for transfers between devices  171 us (38%)
  Pallas kernels  94.7 us (21%)
  starting transfers between devices  89.7 us (20%)
  local copies, waits for them, and re-layouts  45.5 us (10%)
  other arithmetic  34.1 us (8%)
    ppermute x36, waiting for transfers between devices, shift(): lax.ppermute(block, 'dp', [(i, i + 4 * step) for i in range(4 * low, 4 *...  78.1 us
    ppermute x36, starting transfers between devices, shift(): lax.ppermute(block, 'dp', [(i, i + 4 * step) for i in range(4 * low, 4 *...  73.1 us
    pallas_call x12, Pallas kernels, kernel_call(): pl.pallas_call(kernel, in_specs=[SCALARS] + [WHOLE] * (given + len(held))...  62.3 us
    ppermute x4, waiting for transfers between devices, passed_along(): return lax.ppermute(block, axis, route)  52.2 us
    ppermute x6, waiting for transfers between devices, swap_y(): return lax.ppermute(block, 'dp', [(i, i ^ 2) for i in range(16)])  37.2 us
    pallas_call x3, Pallas kernels, grad_call(): pl.pallas_call(kernel, in_specs=[SCALARS] + [WHOLE] * len(ins) + [ANY] *...  23.6 us
    unnamed x117, local copies, waits for them, and re-layouts  13.3 us
  transfers between devices with their start and end apart: 55, of which 18 were waited for; matrix products, arithmetic and copies ran while one was open for 11% of the time, Pallas kernels for 8%

profile of v2, /device:TPU:0, one launch (start us, length us, event | category | flops | bytes accessed | tf_op | source)
XLA Modules:
  0.0 437.5 jit_solution(6952235024771697009)
XLA Ops:
  10.3 4.9 %collective-permute-start = (bf16[48,3200]{1,0:T(8,128)(2,1)S(1)}, bf16[48,3200]{1,0:T(8,128)(2,1)S(1)}, u32[]{:S(2)}, u32[]{:S(2)}) collective-permute-start(bf16[48,3200]{1,0:T(8,128)(2,1)S(1)} %concatenate.84), channel_id=1, source_target_pairs={{0,4},{1,5},{2,6},{3,7},{4,8},{5,9},{6,10},{7,11},{8,12},{9,13},{1... | collective-permute-start | bytes 921608 | tf_op jit(solution)/shard_map/ppermute | solution.py:681
  16.6 1.6 collective-permute-start.15
  18.9 2.8 collective-permute-done
  21.7 4.1 collective-permute-done.1
  25.9 4.2 collective-permute-start.2
  37.1 16.4 %collective-permute-done.3 = bf16[48,3072]{1,0:T(8,128)(2,1)} collective-permute-done((bf16[48,3072]{1,0:T(8,128)(2,1)}, bf16[48,3072]{1,0:T(8,128)(2,1)}, u32[]{:S(2)}, u32[]{:S(2)}) %collective-permute-start.3) | collective-permute-done | bytes 294944 | tf_op jit(solution)/shard_map/ppermute | solution.py:681
  55.0 5.1 %collective-permute-start.16 = (bf16[2,192,768]{2,1,0:T(8,128)(2,1)S(1)}, bf16[2,192,768]{2,1,0:T(8,128)(2,1)S(1)}, u32[]{:S(2)}, u32[]{:S(2)}) collective-permute-start(bf16[2,192,768]{2,1,0:T(8,128)(2,1)S(1)} %pad_maximum_fusion.3), channel_id=1, source_target_pairs={{0,4},{1,5},{2,6},{3,7},{4,8},{5,9},{6,10},{7,11},{8,12},{9,13},{1... | collective-permute-start | bytes 1769480 | tf_op jit(solution)/shard_map/ppermute | solution.py:681
  65.4 1.6 collective-permute-start.24
  67.0 19.9 %collective-permute-done.10 = bf16[48,3072]{1,0:T(8,128)(2,1)S(1)} collective-permute-done((bf16[48,3072]{1,0:T(8,128)(2,1)}, bf16[48,3072]{1,0:T(8,128)(2,1)S(1)}, u32[]{:S(2)}, u32[]{:S(2)}) %collective-permute-start.10) | collective-permute-done | bytes 294944 | tf_op jit(solution)/shard_map/ppermute | solution.py:681
  92.3 1.6 collective-permute-start.12
  93.9 11.5 %collective-permute-done.20 = bf16[2,192,768]{2,1,0:T(8,128)(2,1)S(1)} collective-permute-done((bf16[2,192,768]{2,1,0:T(8,128)(2,1)S(1)}, bf16[2,192,768]{2,1,0:T(8,128)(2,1)S(1)}, u32[]{:S(2)}, u32[]{:S(2)}) %collective-permute-start.20) | collective-permute-done | bytes 589856 | tf_op jit(solution)/shard_map/ppermute | solution.py:681
  105.4 10.0 %collective-permute-done.21 = bf16[2,192,768]{2,1,0:T(8,128)(2,1)S(1)} collective-permute-done((bf16[2,192,768]{2,1,0:T(8,128)(2,1)S(1)}, bf16[2,192,768]{2,1,0:T(8,128)(2,1)S(1)}, u32[]{:S(2)}, u32[]{:S(2)}) %collective-permute-start.21) | collective-permute-done | bytes 589856 | tf_op jit(solution)/shard_map/ppermute | solution.py:681
  115.9 1.6 slice_bitcast_fusion.2
  118.6 3.7 collective-permute-done.22.own_sibling
  128.6 3.0 join_down.1.refs_1_.refs_3_
  131.6 2.1 copy-done
  137.1 3.0 join_attn.1.refs_2_.refs_0_
  140.2 7.3 %forward_attn.3 = (bf16[384,768]{1,0:T(8,128)(2,1)S(1)}, bf16[384,2304]{1,0:T(8,128)(2,1)S(1)}, f32[12,8,256]{2,1,0:T(8,128)S(1)}, bf16[384,768]{1,0:T(8,128)(2,...) custom-call(s32[6,12]{1,0:T(8,128)S(1)} %stack.212.table, ...), custom_call_target="tpu_custom_call" | custom-call | flops 2264924160 | tf_op jit(solution)/shard_map/forward_attn/pallas_call | solution.py:248
  147.5 2.9 join_up.1.refs_0_.refs_2_
  150.5 6.9 %forward_ffn.3 = (bf16[384,3072]{1,0:T(8,128)(2,1)S(1)}, bf16[384,3072]{1,0:T(8,128)(2,1)S(1)}, f32[384,768]{1,0:T(8,128)S(1)}, f32[384,128]{1,0:T(8,128)S(1)}, bf16[384,768]{1,0:T(8,128)(2,1)S(1)}) custom-call(s32[6,12]{1,0:T(8,128)S(1)} %stack.212.table, bf16[768,3072]{1,0:T(8,128)(2,1)S(1)} %join_up.1.refs_0_.refs_2_, bf16[3072,768]{1,0:T(8,128)(2,1)S(1)} %bitcast.230, ...), custom_call_target="tpu_custom_call" | custom-call | flops 3623878656 | tf_op jit(solution)/shard_map/forward_ffn/pallas_call | solution.py:248
  157.3 1.3 collective-permute-start.27
  158.7 13.4 %collective-permute-done.27.refs_1_ = bf16[384,768]{1,0:T(8,128)(2,1)S(1)} collective-permute-done((bf16[384,768]{1,0:T(8,128)(2,1)S(1)}, bf16[384,768]{1,0:T(8,128)(2,1)S(1)}, u32[]{:S(2)}, u32[]{:S(2)}) %collective-permute-start.27) | collective-permute-done | bytes 589856 | tf_op jit(solution)/shard_map/ppermute | solution.py:785
  172.0 8.3 %forward_attn.4 = (bf16[384,768]{1,0:T(8,128)(2,1)S(1)}, bf16[384,2304]{1,0:T(8,128)(2,1)S(1)}, f32[12,8,256]{2,1,0:T(8,128)S(1)}, bf16[384,768]{1,0:T(8,128)(2,...) custom-call(s32[6,12]{1,0:T(8,128)S(1)} %stack.212.table, ...), custom_call_target="tpu_custom_call" | custom-call | flops 2264924160 | tf_op jit(solution)/shard_map/forward_attn/pallas_call | solution.py:248
  182.0 6.6 %forward_ffn.4 = (bf16[384,3072]{1,0:T(8,128)(2,1)S(1)}, bf16[384,3072]{1,0:T(8,128)(2,1)S(1)}, f32[384,768]{1,0:T(8,128)S(1)}, f32[384,128]{1,0:T(8,128)S(1)}, bf16[384,768]{1,0:T(8,128)(2,1)S(1)}) custom-call(s32[6,12]{1,0:T(8,128)S(1)} %stack.212.table, bf16[768,3072]{1,0:T(8,128)(2,1)S(1)} %join_up.1.refs_0_.refs_2_, bf16[3072,768]{1,0:T(8,128)(2,1)S(1)} %bitcast.230, ...), custom_call_target="tpu_custom_call" | custom-call | flops 3623878656 | tf_op jit(solution)/shard_map/forward_ffn/pallas_call | solution.py:248
  188.6 1.5 copy-done.34
  190.1 3.4 collective-permute-start.28
  197.8 8.1 %collective-permute-done.28.refs_1_ = bf16[384,768]{1,0:T(8,128)(2,1)S(1)} collective-permute-done((bf16[384,768]{1,0:T(8,128)(2,1)S(1)}, bf16[384,768]{1,0:T(8,128)(2,1)S(1)}, u32[]{:S(2)}, u32[]{:S(2)}) %collective-permute-start.28) | collective-permute-done | bytes 589856 | tf_op jit(solution)/shard_map/ppermute | solution.py:785
  207.3 1.7 forward_ffn.5
  209.0 14.2 %collective-permute-done.29.refs_1_ = bf16[384,768]{1,0:T(8,128)(2,1)S(1)} collective-permute-done((bf16[384,768]{1,0:T(8,128)(2,1)S(1)}, bf16[384,768]{1,0:T(8,128)(2,1)S(1)}, u32[]{:S(2)}, u32[]{:S(2)}) %collective-permute-start.29) | collective-permute-done | bytes 589856 | tf_op jit(solution)/shard_map/ppermute | solution.py:785
  223.1 6.8 %ffn_backward.4 = (bf16[384,768]{1,0:T(8,128)(2,1)S(1)}, bf16[384,3072]{1,0:T(8,128)(2,1)S(1)}, bf16[384,768]{1,0:T(8,128)(2,1)S(1)}, f32[8,3072]{1,0:T(8,128)S(1)}, f32[384,768]{1,0:T(8,128)S(1)}) custom-call(s32[6,12]{1,0:T(8,128)S(1)} %stack.212.table, bf16[2,384,768]{2,1,0:T(8,128)(2,1)S(1)} %copy-done.2, ...), custom_call_target="tpu_custom_call" | custom-call | flops 3623878656 | tf_op jit(solution)/shard_map/ffn_backward/pallas_call | solution.py:248
  230.0 7.1 %attention_backward.4 = (bf16[384,2304]{1,0:T(8,128)(2,1)S(1)}, bf16[384,768]{1,0:T(8,128)(2,1)S(1)}, f32[8,768]{1,0:T(8,128)S(1)}) custom-call(s32[6,12]{1,0:T(8,128)S(1)} %stack.212.table, bf16[768,3200]{1,0:T(8,128)(2,1)S(1)} %join_attn.1.refs_2_.refs_0_, f32[384,768]{1,0:T(8,128)S(1)} %get-tuple-element.124.refs_1_, ...), custom_call_target="tpu_custom_call" | custom-call | flops 2944401408 | tf_op jit(solution)/shard_map/attention_backward/pallas_call | solution.py:248
  238.4 16.5 %collective-permute-done.30.refs_1_ = bf16[384,768]{1,0:T(8,128)(2,1)S(1)} collective-permute-done((bf16[384,768]{1,0:T(8,128)(2,1)S(1)}, bf16[384,768]{1,0:T(8,128)(2,1)S(1)}, u32[]{:S(2)}, u32[]{:S(2)}) %collective-permute-start.30) | collective-permute-done | bytes 589856 | tf_op jit(solution)/shard_map/ppermute | solution.py:785
  254.9 7.0 %ffn_backward.5 = (bf16[384,768]{1,0:T(8,128)(2,1)S(1)}, bf16[384,3072]{1,0:T(8,128)(2,1)S(1)}, bf16[384,768]{1,0:T(8,128)(2,1)S(1)}, f32[8,3072]{1,0:T(8,128)S(1)}, f32[384,768]{1,0:T(8,128)S(1)}) custom-call(s32[6,12]{1,0:T(8,128)S(1)} %stack.212.table, ...), custom_call_target="tpu_custom_call", output_to_operand_aliasing={{0}: (11, {}), {1}: (12, {}), {2}: (13, {}), {3}: (14, {}),... | custom-call | flops 3623878656 | tf_op jit(solution)/shard_map/ffn_backward/pallas_call | solution.py:248
  262.8 6.7 %grad_down.1 = (bf16[2,4,192,768]{3,2,1,0:T(8,128)(2,1)S(1)}, bf16[2,4,192,768]{3,2,1,0:T(8,128)(2,1)S(1)}) custom-call(s32[2]{0:T(128)S(1)} %pad_add_fusion.place, bf16[384,3072]{1,0:T(8,128)(2,1)S(1)} %get-tuple-element.138.refs_0_, bf16[384,3072]{1,0:T(8,128)(2,1)S(1)} %copy-done.35, bf16[384,768]{1,0:T(8,128)(2,1)S(1)} %get-tuple-element.140.refs_2_, ...), custom_call_target="tpu_custom_call" | custom-call | flops 3623878656 | tf_op jit(solution)/shard_map/grad_down/pallas_call | solution.py:573
  269.5 1.7 copy.91
  271.2 8.5 %grad_up.1 = (bf16[2,4,48,3072]{3,2,1,0:T(8,128)(2,1)S(1)}, bf16[2,4,48,3072]{3,2,1,0:T(8,128)(2,1)}) custom-call(s32[2]{0:T(128)S(1)} %pad_add_fusion.place, bf16[384,768]{1,0:T(8,128)(2,1)S(1)} %get-tuple-element.105.refs_5_.refs_0_, bf16[384,768]{1,0:T(8,128)(2,1)S(1)} %copy-done.43, bf16[384,3072]{1,0:T(8,128)(2,1)S(1)} %get-tuple-element.136.refs_2_, ...), custom_call_target="tpu_custom_call" | custom-call | flops 3623878656 | tf_op jit(solution)/shard_map/grad_up/pallas_call | solution.py:573
  287.1 3.3 fusion.20
  291.5 1.6 collective-permute-start.35
  294.3 1.6 collective-permute-start.34
  295.9 5.5 %collective-permute-start.33 = (bf16[2,192,768]{2,1,0:T(8,128)(2,1)}, bf16[2,192,768]{2,1,0:T(8,128)(2,1)}, u32[]{:S(2)}, u32[]{:S(2)}) collective-permute-start(bf16[2,192,768]{2,1,0:T(8,128)(2,1)} %get-tuple-element.190.refs_11_), channel_id=1, source_target_pairs={{0,8},{1,9},{2,10},{3,11},{16,24},{17,25},{18,26},{19,27}} | collective-permute-start | bytes 1769480 | tf_op jit(solution)/shard_map/ppermute | solution.py:681
  301.4 2.1 collective-permute-start.32
  303.5 7.6 %attention_backward.5 = (bf16[384,2304]{1,0:T(8,128)(2,1)S(1)}, bf16[384,768]{1,0:T(8,128)(2,1)S(1)}, f32[8,768]{1,0:T(8,128)S(1)}) custom-call(s32[6,12]{1,0:T(8,128)S(1)} %stack.212.table, bf16[768,3200]{1,0:T(8,128)(2,1)S(1)} %bitcast.232, f32[384,768]{1,0:T(8,128)S(1)} %copy-done.4, ...), custom_call_target="tpu_custom_call", output_to_operand_aliasing={{0}: (6, {}), {1}: (7, {}), {2}: (8, {})} | custom-call | flops 2944401408 | tf_op jit(solution)/shard_map/attention_backward/pallas_call | solution.py:248
  316.0 3.6 concatenate.86.refs_8_
  319.6 2.6 convert_add_fusion.1
  322.2 2.1 copy-done.45
  326.0 2.2 fusion.6
  329.0 8.4 %grad_attn.1 = (bf16[2,4,48,3200]{3,2,1,0:T(8,128)(2,1)S(1)}, bf16[2,4,48,3200]{3,2,1,0:T(8,128)(2,1)}) custom-call(s32[2]{0:T(128)S(1)} %pad_add_fusion.place, bf16[384,768]{1,0:T(8,128)(2,1)S(1)} %copy-done.29, bf16[384,768]{1,0:T(8,128)(2,1)S(1)} %copy-done.39, bf16[384,2304]{1,0:T(8,128)(2,1)S(1)} %copy-done.37, bf16[384,2304]{1,0:T(8,128)(2,1)S(1)} %copy-done.19, ...), custom_call_target="tpu_custom_call" | custom-call | flops 3774873600 | tf_op jit(solution)/shard_map/grad_attn/pallas_call | solution.py:573
  338.4 1.4 select_bitcast_fusion.3
  339.9 1.6 maximum_bitcast_fusion
  341.5 1.5 collective-permute-start.53
  343.1 4.6 %collective-permute-start.52 = (bf16[2,192,768]{2,1,0:T(8,128)(2,1)S(1)}, bf16[2,192,768]{2,1,0:T(8,128)(2,1)S(1)}, u32[]{:S(2)}, u32[]{:S(2)}) collective-permute-start(bf16[2,192,768]{2,1,0:T(8,128)(2,1)S(1)} %copy-done.22), channel_id=1, source_target_pairs={{0,4},{1,5},{2,6},{3,7},{4,8},{5,9},{6,10},{7,11},{8,12},{9,13},{1... | collective-permute-start | bytes 1769480 | tf_op jit(solution)/shard_map/ppermute | solution.py:681
  347.7 18.5 %collective-permute-done.45 = bf16[4,48,3072]{2,1,0:T(8,128)(2,1)} collective-permute-done((bf16[4,48,3072]{2,1,0:T(8,128)(2,1)}, bf16[4,48,3072]{2,1,0:T(8,128)(2,1)}, u32[]{:S(2)}, u32[]{:S(2)}) %collective-permute-start.45) | collective-permute-done | bytes 1179680 | tf_op jit(solution)/shard_map/ppermute | solution.py:678
  366.2 1.6 convert_bitcast_fusion.1
  367.8 2.2 convert_add_fusion
  371.1 4.7 %collective-permute-start.47 = (bf16[1,48,3072]{2,1,0:T(8,128)(2,1)S(1)}, bf16[1,48,3072]{2,1,0:T(8,128)(2,1)S(1)}, u32[]{:S(2)}, u32[]{:S(2)}) collective-permute-start(bf16[1,48,3072]{2,1,0:T(8,128)(2,1)S(1)} %get-tuple-element.199), channel_id=1, source_target_pairs={{0,8},{1,9},{2,10},{3,11},{16,24},{17,25},{18,26},{19,27}} | collective-permute-start | bytes 884744 | tf_op jit(solution)/shard_map/ppermute | solution.py:681
  378.6 1.5 fusion.4
  380.1 18.7 %collective-permute-done.38 = bf16[4,48,3200]{2,1,0:T(8,128)(2,1)S(1)} collective-permute-done((bf16[4,48,3200]{2,1,0:T(8,128)(2,1)S(1)}, bf16[4,48,3200]{2,1,0:T(8,128)(2,1)S(1)}, u32[]{:S(2)}, u32[]{:S(2)}) %collective-permute-start.38) | collective-permute-done | bytes 1228832 | tf_op jit(solution)/shard_map/ppermute | solution.py:678
  400.0 4.7 %collective-permute-start.40 = (bf16[1,48,3200]{2,1,0:T(8,128)(2,1)S(1)}, bf16[1,48,3200]{2,1,0:T(8,128)(2,1)S(1)}, u32[]{:S(2)}, u32[]{:S(2)}) collective-permute-start(bf16[1,48,3200]{2,1,0:T(8,128)(2,1)S(1)} %get-tuple-element.197), channel_id=1, source_target_pairs={{0,8},{1,9},{2,10},{3,11},{16,24},{17,25},{18,26},{19,27}} | collective-permute-start | bytes 921608 | tf_op jit(solution)/shard_map/ppermute | solution.py:681
  404.7 1.3 collective-permute-start.39
  409.8 2.6 collective-permute-done.40
  412.4 2.0 collective-permute-start.48
  414.4 4.6 %collective-permute-done.39 = bf16[1,48,3200]{2,1,0:T(8,128)(2,1)S(1)} collective-permute-done((bf16[1,48,3200]{2,1,0:T(8,128)(2,1)S(1)}, bf16[1,48,3200]{2,1,0:T(8,128)(2,1)S(1)}, u32[]{:S(2)}, u32[]{:S(2)}) %collective-permute-start.39) | collective-permute-done | bytes 307232 | tf_op jit(solution)/shard_map/ppermute | solution.py:681
  420.5 7.0 %collective-permute-start.41 = (bf16[1,48,3200]{2,1,0:T(8,128)(2,1)S(1)}, bf16[1,48,3200]{2,1,0:T(8,128)(2,1)S(1)}, u32[]{:S(2)}, u32[]{:S(2)}) collective-permute-start(bf16[1,48,3200]{2,1,0:T(8,128)(2,1)S(1)} %get-tuple-element.177), channel_id=1, source_target_pairs={{0,4},{1,5},{2,6},{3,7},{4,8},{5,9},{6,10},{7,11},{8,12},{9,13},{1... | collective-permute-start | bytes 921608 | tf_op jit(solution)/shard_map/ppermute | solution.py:681
  428.5 4.5 %collective-permute-done.44 = bf16[1,48,3200]{2,1,0:T(8,128)(2,1)S(1)} collective-permute-done((bf16[1,48,3200]{2,1,0:T(8,128)(2,1)S(1)}, bf16[1,48,3200]{2,1,0:T(8,128)(2,1)S(1)}, u32[]{:S(2)}, u32[]{:S(2)}) %collective-permute-start.44) | collective-permute-done | bytes 307232 | tf_op jit(solution)/shard_map/ppermute | solution.py:681
  (297 shorter events, 84.8 us)
Async XLA Ops:
  0.6 15.9 %copy-start.47 = (f32[1,192,768]{2,1,0:T(8,128)S(1)}, f32[1,192,768]{2,1,0:T(8,128)}, u32[]{:S(2)}) copy-start(f32[1,192,768]{2,1,0:T(8,128)} %param.30) | copy-start | bytes 1769476
  1.8 16.4 %copy-start.48 = (f32[1,48,3072]{2,1,0:T(8,128)S(1)}, f32[1,48,3072]{2,1,0:T(8,128)}, u32[]{:S(2)}) copy-start(f32[1,48,3072]{2,1,0:T(8,128)} %param.28) | copy-start | bytes 1769476
  10.3 11.4 %collective-permute-start = (bf16[48,3200]{1,0:T(8,128)(2,1)S(1)}, bf16[48,3200]{1,0:T(8,128)(2,1)S(1)}, u32[]{:S(2)}, u32[]{:S(2)}) collective-permute-start(bf16[48,3200]{1,0:T(8,128)(2,1)S(1)} %concatenate.84), channel_id=1, source_target_pairs={{0,4},{1,5},{2,6},{3,7},{4,8},{5,9},{6,10},{7,11},{8,12},{9,13},{1... | collective-permute-start | bytes 921608 | tf_op jit(solution)/shard_map/ppermute | solution.py:681
  15.2 10.6 %collective-permute-start.1 = (bf16[48,3200]{1,0:T(8,128)(2,1)S(1)}, bf16[48,3200]{1,0:T(8,128)(2,1)S(1)}, u32[]{:S(2)}, u32[]{:S(2)}) collective-permute-start(bf16[48,3200]{1,0:T(8,128)(2,1)S(1)} %concatenate.84), channel_id=1, source_target_pairs={{4,0},{5,1},{6,2},{7,3},{8,4},{9,5},{10,6},{11,7},{12,8},{13,9},{1... | collective-permute-start | bytes 921608 | tf_op jit(solution)/shard_map/ppermute | solution.py:681
  16.6 16.1 %collective-permute-start.15 = (bf16[192,768]{1,0:T(8,128)(2,1)S(1)}, bf16[192,768]{1,0:T(8,128)(2,1)S(1)}, u32[]{:S(2)}, u32[]{:S(2)}) collective-permute-start(bf16[192,768]{1,0:T(8,128)(2,1)S(1)} %convert_bitcast_fusion.13), channel_id=1, source_target_pairs={{0,2},{1,3},{2,0},{3,1},{4,6},{5,7},{6,4},{7,5},{8,10},{9,11},{10,... | collective-permute-start | bytes 884744 | tf_op jit(solution)/shard_map/ppermute | solution.py:678
  25.9 8.9 %collective-permute-start.2 = (bf16[48,3072]{1,0:T(8,128)(2,1)}, bf16[48,3072]{1,0:T(8,128)(2,1)}, u32[]{:S(2)}, u32[]{:S(2)}) collective-permute-start(bf16[48,3072]{1,0:T(8,128)(2,1)} %convert_bitcast_fusion.2), channel_id=1, source_target_pairs={{0,4},{1,5},{2,6},{3,7},{4,8},{5,9},{6,10},{7,11},{8,12},{9,13},{1... | collective-permute-start | bytes 884744 | tf_op jit(solution)/shard_map/ppermute | solution.py:681
  30.0 23.5 %collective-permute-start.4 = (bf16[48,3200]{1,0:T(8,128)(2,1)S(1)}, bf16[48,3200]{1,0:T(8,128)(2,1)S(1)}, u32[]{:S(2)}, u32[]{:S(2)}) collective-permute-start(bf16[48,3200]{1,0:T(8,128)(2,1)S(1)} %collective-permute-done), channel_id=1, source_target_pairs={{4,8},{5,9},{6,10},{7,11},{8,12},{9,13},{10,14},{11,15},{20,24},{2... | collective-permute-start | bytes 921608 | tf_op jit(solution)/shard_map/ppermute | solution.py:681
  30.7 22.9 %collective-permute-start.5 = (bf16[48,3200]{1,0:T(8,128)(2,1)S(1)}, bf16[48,3200]{1,0:T(8,128)(2,1)S(1)}, u32[]{:S(2)}, u32[]{:S(2)}) collective-permute-start(bf16[48,3200]{1,0:T(8,128)(2,1)S(1)} %collective-permute-done.1), channel_id=1, source_target_pairs={{4,0},{5,1},{6,2},{7,3},{8,4},{9,5},{10,6},{11,7},{20,16},{21,17},... | collective-permute-start | bytes 921608 | tf_op jit(solution)/shard_map/ppermute | solution.py:681
  32.0 21.6 %collective-permute-start.6 = (bf16[48,3200]{1,0:T(8,128)(2,1)S(1)}, bf16[48,3200]{1,0:T(8,128)(2,1)S(1)}, u32[]{:S(2)}, u32[]{:S(2)}) collective-permute-start(bf16[48,3200]{1,0:T(8,128)(2,1)S(1)} %collective-permute-done), channel_id=1, source_target_pairs={{4,12},{5,13},{6,14},{7,15},{20,28},{21,29},{22,30},{23,31}} | collective-permute-start | bytes 921608 | tf_op jit(solution)/shard_map/ppermute | solution.py:681
  33.4 20.1 %collective-permute-start.7 = (bf16[48,3200]{1,0:T(8,128)(2,1)S(1)}, bf16[48,3200]{1,0:T(8,128)(2,1)}, u32[]{:S(2)}, u32[]{:S(2)}) collective-permute-start(bf16[48,3200]{1,0:T(8,128)(2,1)S(1)} %collective-permute-done.1), channel_id=1, source_target_pairs={{8,0},{9,1},{10,2},{11,3},{24,16},{25,17},{26,18},{27,19}} | collective-permute-start | bytes 921608 | tf_op jit(solution)/shard_map/ppermute | solution.py:681
  34.7 18.8 %collective-permute-start.3 = (bf16[48,3072]{1,0:T(8,128)(2,1)}, bf16[48,3072]{1,0:T(8,128)(2,1)}, u32[]{:S(2)}, u32[]{:S(2)}) collective-permute-start(bf16[48,3072]{1,0:T(8,128)(2,1)} %convert_bitcast_fusion.2), channel_id=1, source_target_pairs={{4,0},{5,1},{6,2},{7,3},{8,4},{9,5},{10,6},{11,7},{12,8},{13,9},{1... | collective-permute-start | bytes 884744 | tf_op jit(solution)/shard_map/ppermute | solution.py:681
  53.6 10.3 %collective-permute-start.8 = (bf16[48,3072]{1,0:T(8,128)(2,1)}, bf16[48,3072]{1,0:T(8,128)(2,1)S(1)}, u32[]{:S(2)}, u32[]{:S(2)}) collective-permute-start(bf16[48,3072]{1,0:T(8,128)(2,1)} %collective-permute-done.2), channel_id=1, source_target_pairs={{4,8},{5,9},{6,10},{7,11},{8,12},{9,13},{10,14},{11,15},{20,24},{2... | collective-permute-start | bytes 884744 | tf_op jit(solution)/shard_map/ppermute | solution.py:681
  54.3 11.1 %collective-permute-start.9 = (bf16[48,3072]{1,0:T(8,128)(2,1)}, bf16[48,3072]{1,0:T(8,128)(2,1)S(1)}, u32[]{:S(2)}, u32[]{:S(2)}) collective-permute-start(bf16[48,3072]{1,0:T(8,128)(2,1)} %collective-permute-done.2), channel_id=1, source_target_pairs={{4,12},{5,13},{6,14},{7,15},{20,28},{21,29},{22,30},{23,31}} | collective-permute-start | bytes 884744 | tf_op jit(solution)/shard_map/ppermute | solution.py:681
  55.0 31.9 %collective-permute-start.16 = (bf16[2,192,768]{2,1,0:T(8,128)(2,1)S(1)}, bf16[2,192,768]{2,1,0:T(8,128)(2,1)S(1)}, u32[]{:S(2)}, u32[]{:S(2)}) collective-permute-start(bf16[2,192,768]{2,1,0:T(8,128)(2,1)S(1)} %pad_maximum_fusion.3), channel_id=1, source_target_pairs={{0,4},{1,5},{2,6},{3,7},{4,8},{5,9},{6,10},{7,11},{8,12},{9,13},{1... | collective-permute-start | bytes 1769480 | tf_op jit(solution)/shard_map/ppermute | solution.py:681
  60.1 26.8 %collective-permute-start.17 = (bf16[2,192,768]{2,1,0:T(8,128)(2,1)S(1)}, bf16[2,192,768]{2,1,0:T(8,128)(2,1)S(1)}, u32[]{:S(2)}, u32[]{:S(2)}) collective-permute-start(bf16[2,192,768]{2,1,0:T(8,128)(2,1)S(1)} %pad_maximum_fusion.3), channel_id=1, source_target_pairs={{4,0},{5,1},{6,2},{7,3},{8,4},{9,5},{10,6},{11,7},{12,8},{13,9},{1... | collective-permute-start | bytes 1769480 | tf_op jit(solution)/shard_map/ppermute | solution.py:681
  61.4 25.5 %collective-permute-start.10 = (bf16[48,3072]{1,0:T(8,128)(2,1)}, bf16[48,3072]{1,0:T(8,128)(2,1)S(1)}, u32[]{:S(2)}, u32[]{:S(2)}) collective-permute-start(bf16[48,3072]{1,0:T(8,128)(2,1)} %collective-permute-done.3), channel_id=1, source_target_pairs={{4,0},{5,1},{6,2},{7,3},{8,4},{9,5},{10,6},{11,7},{20,16},{21,17},... | collective-permute-start | bytes 884744 | tf_op jit(solution)/shard_map/ppermute | solution.py:681
  63.9 23.0 %collective-permute-start.11 = (bf16[48,3072]{1,0:T(8,128)(2,1)}, bf16[48,3072]{1,0:T(8,128)(2,1)S(1)}, u32[]{:S(2)}, u32[]{:S(2)}) collective-permute-start(bf16[48,3072]{1,0:T(8,128)(2,1)} %collective-permute-done.3), channel_id=1, source_target_pairs={{8,0},{9,1},{10,2},{11,3},{24,16},{25,17},{26,18},{27,19}} | collective-permute-start | bytes 884744 | tf_op jit(solution)/shard_map/ppermute | solution.py:681
  65.4 52.6 %collective-permute-start.24 = (bf16[4,48,3200]{2,1,0:T(8,128)(2,1)S(1)}, bf16[4,48,3200]{2,1,0:T(8,128)(2,1)}, u32[]{:S(2)}, u32[]{:S(2)}) collective-permute-start(bf16[4,48,3200]{2,1,0:T(8,128)(2,1)S(1)} %pad_maximum_fusion.1.own), channel_id=1, source_target_pairs={{0,2},{1,3},{2,0},{3,1},{4,6},{5,7},{6,4},{7,5},{8,10},{9,11},{10,... | collective-permute-start | bytes 3686408 | tf_op jit(solution)/shard_map/ppermute | solution.py:678
  86.9 5.4 %collective-permute-start.18 = (bf16[2,192,768]{2,1,0:T(8,128)(2,1)S(1)}, bf16[2,192,768]{2,1,0:T(8,128)(2,1)S(1)}, u32[]{:S(2)}, u32[]{:S(2)}) collective-permute-start(bf16[2,192,768]{2,1,0:T(8,128)(2,1)S(1)} %collective-permute-done.16), channel_id=1, source_target_pairs={{4,8},{5,9},{6,10},{7,11},{8,12},{9,13},{10,14},{11,15},{20,24},{2... | collective-permute-start | bytes 1769480 | tf_op jit(solution)/shard_map/ppermute | solution.py:681
  87.6 6.3 %collective-permute-start.19 = (bf16[2,192,768]{2,1,0:T(8,128)(2,1)S(1)}, bf16[2,192,768]{2,1,0:T(8,128)(2,1)S(1)}, u32[]{:S(2)}, u32[]{:S(2)}) collective-permute-start(bf16[2,192,768]{2,1,0:T(8,128)(2,1)S(1)} %collective-permute-done.16), channel_id=1, source_target_pairs={{4,12},{5,13},{6,14},{7,15},{20,28},{21,29},{22,30},{23,31}} | collective-permute-start | bytes 1769480 | tf_op jit(solution)/shard_map/ppermute | solution.py:681
  88.3 17.1 %collective-permute-start.20 = (bf16[2,192,768]{2,1,0:T(8,128)(2,1)S(1)}, bf16[2,192,768]{2,1,0:T(8,128)(2,1)S(1)}, u32[]{:S(2)}, u32[]{:S(2)}) collective-permute-start(bf16[2,192,768]{2,1,0:T(8,128)(2,1)S(1)} %collective-permute-done.17), channel_id=1, source_target_pairs={{4,0},{5,1},{6,2},{7,3},{8,4},{9,5},{10,6},{11,7},{20,16},{21,17},... | collective-permute-start | bytes 1769480 | tf_op jit(solution)/shard_map/ppermute | solution.py:681
  89.6 25.8 %collective-permute-start.21 = (bf16[2,192,768]{2,1,0:T(8,128)(2,1)S(1)}, bf16[2,192,768]{2,1,0:T(8,128)(2,1)S(1)}, u32[]{:S(2)}, u32[]{:S(2)}) collective-permute-start(bf16[2,192,768]{2,1,0:T(8,128)(2,1)S(1)} %collective-permute-done.17), channel_id=1, source_target_pairs={{8,0},{9,1},{10,2},{11,3},{24,16},{25,17},{26,18},{27,19}} | collective-permute-start | bytes 1769480 | tf_op jit(solution)/shard_map/ppermute | solution.py:681
  92.3 26.2 %collective-permute-start.12 = (bf16[4,48,3072]{2,1,0:T(8,128)(2,1)S(1)}, bf16[4,48,3072]{2,1,0:T(8,128)(2,1)}, u32[]{:S(2)}, u32[]{:S(2)}) collective-permute-start(bf16[4,48,3072]{2,1,0:T(8,128)(2,1)S(1)} %pad_maximum_fusion.2.own), channel_id=1, source_target_pairs={{0,2},{1,3},{2,0},{3,1},{4,6},{5,7},{6,4},{7,5},{8,10},{9,11},{10,... | collective-permute-start | bytes 3538952 | tf_op jit(solution)/shard_map/ppermute | solution.py:678
  117.5 4.8 %collective-permute-start.22 = (bf16[4,192,768]{2,1,0:T(8,128)(2,1)}, bf16[4,192,768]{2,1,0:T(8,128)(2,1)}, u32[]{:S(2)}, u32[]{:S(2)}) collective-permute-start(bf16[4,192,768]{2,1,0:T(8,128)(2,1)} %get-tuple-element.192.own), channel_id=1, source_target_pairs={{0,1},{1,0},{2,3},{3,2},{4,5},{5,4},{6,7},{7,6},{8,9},{9,8},{10,11... | collective-permute-start | bytes 3538952 | tf_op jit(solution)/shard_map/ppermute | solution.py:675
  117.5 16.2 %collective-permute-start.25 = (bf16[4,48,3200]{2,1,0:T(8,128)(2,1)S(1)}, bf16[4,48,3200]{2,1,0:T(8,128)(2,1)}, u32[]{:S(2)}, u32[]{:S(2)}) collective-permute-start(bf16[4,48,3200]{2,1,0:T(8,128)(2,1)S(1)} %pad_maximum_fusion.1.own), channel_id=1, source_target_pairs={{0,1},{1,0},{2,3},{3,2},{4,5},{5,4},{6,7},{7,6},{8,9},{9,8},{10,11... | collective-permute-start | bytes 3686408 | tf_op jit(solution)/shard_map/ppermute | solution.py:675
  118.0 15.7 %collective-permute-start.26 = (bf16[4,48,3200]{2,1,0:T(8,128)(2,1)}, bf16[4,48,3200]{2,1,0:T(8,128)(2,1)}, u32[]{:S(2)}, u32[]{:S(2)}) collective-permute-start(bf16[4,48,3200]{2,1,0:T(8,128)(2,1)} %collective-permute-done.24.other), channel_id=1, source_target_pairs={{0,1},{1,0},{2,3},{3,2},{4,5},{5,4},{6,7},{7,6},{8,9},{9,8},{10,11... | collective-permute-start | bytes 3686408 | tf_op jit(solution)/shard_map/ppermute | solution.py:675
  118.0 10.6 %collective-permute-start.23 = (bf16[4,192,768]{2,1,0:T(8,128)(2,1)}, bf16[4,192,768]{2,1,0:T(8,128)(2,1)}, u32[]{:S(2)}, u32[]{:S(2)}) collective-permute-start(bf16[4,192,768]{2,1,0:T(8,128)(2,1)} %get-tuple-element.191.other), channel_id=1, source_target_pairs={{0,1},{1,0},{2,3},{3,2},{4,5},{5,4},{6,7},{7,6},{8,9},{9,8},{10,11... | collective-permute-start | bytes 3538952 | tf_op jit(solution)/shard_map/ppermute | solution.py:675
  118.6 29.0 %collective-permute-start.13 = (bf16[4,48,3072]{2,1,0:T(8,128)(2,1)S(1)}, bf16[4,48,3072]{2,1,0:T(8,128)(2,1)}, u32[]{:S(2)}, u32[]{:S(2)}) collective-permute-start(bf16[4,48,3072]{2,1,0:T(8,128)(2,1)S(1)} %pad_maximum_fusion.2.own), channel_id=1, source_target_pairs={{0,1},{1,0},{2,3},{3,2},{4,5},{5,4},{6,7},{7,6},{8,9},{9,8},{10,11... | collective-permute-start | bytes 3538952 | tf_op jit(solution)/shard_map/ppermute | solution.py:675
  122.4 25.2 %collective-permute-start.14 = (bf16[4,48,3072]{2,1,0:T(8,128)(2,1)}, bf16[4,48,3072]{2,1,0:T(8,128)(2,1)}, u32[]{:S(2)}, u32[]{:S(2)}) collective-permute-start(bf16[4,48,3072]{2,1,0:T(8,128)(2,1)} %collective-permute-done.12.other), channel_id=1, source_target_pairs={{0,1},{1,0},{2,3},{3,2},{4,5},{5,4},{6,7},{7,6},{8,9},{9,8},{10,11... | collective-permute-start | bytes 3538952 | tf_op jit(solution)/shard_map/ppermute | solution.py:675
  140.1 89.9 %copy-start.1 = (bf16[768,3200]{1,0:T(8,128)(2,1)}, bf16[768,3200]{1,0:T(8,128)(2,1)S(1)}, u32[]{:S(2)}) copy-start(bf16[768,3200]{1,0:T(8,128)(2,1)S(1)} %join_attn.1.refs_2_.refs_0_) | copy-start | bytes 14745604
  157.3 14.7 %collective-permute-start.27 = (bf16[384,768]{1,0:T(8,128)(2,1)S(1)}, bf16[384,768]{1,0:T(8,128)(2,1)S(1)}, u32[]{:S(2)}, u32[]{:S(2)}) collective-permute-start(bf16[384,768]{1,0:T(8,128)(2,1)S(1)} %get-tuple-element.95.refs_10_), channel_id=1, source_target_pairs={{0,16},{1,17},{2,18},{3,19},{4,20},{5,21},{6,22},{7,23},{8,24},{9,... | collective-permute-start | bytes 1769480 | tf_op jit(solution)/shard_map/ppermute | solution.py:785
  190.1 15.9 %collective-permute-start.28 = (bf16[384,768]{1,0:T(8,128)(2,1)S(1)}, bf16[384,768]{1,0:T(8,128)(2,1)S(1)}, u32[]{:S(2)}, u32[]{:S(2)}) collective-permute-start(bf16[384,768]{1,0:T(8,128)(2,1)S(1)} %get-tuple-element.98), channel_id=1, source_target_pairs={{0,16},{1,17},{2,18},{3,19},{4,20},{5,21},{6,22},{7,23},{8,24},{9,... | collective-permute-start | bytes 1769480 | tf_op jit(solution)/shard_map/ppermute | solution.py:785
  196.5 26.6 %collective-permute-start.29 = (bf16[384,768]{1,0:T(8,128)(2,1)S(1)}, bf16[384,768]{1,0:T(8,128)(2,1)S(1)}, u32[]{:S(2)}, u32[]{:S(2)}) collective-permute-start(bf16[384,768]{1,0:T(8,128)(2,1)S(1)} %get-tuple-element.119.refs_6_), channel_id=1, source_target_pairs={{16,0},{17,1},{18,2},{19,3},{20,4},{21,5},{22,6},{23,7},{24,8},{25... | collective-permute-start | bytes 1769480 | tf_op jit(solution)/shard_map/ppermute | solution.py:785
  237.1 24.9 %copy-start.26 = (bf16[384,768]{1,0:T(8,128)(2,1)}, bf16[384,768]{1,0:T(8,128)(2,1)S(1)}, u32[]{:S(2)}) copy-start(bf16[384,768]{1,0:T(8,128)(2,1)S(1)} %get-tuple-element.128) | copy-start | bytes 1769476
  237.1 24.9 %copy-start.36 = (bf16[384,2304]{1,0:T(8,128)(2,1)}, bf16[384,2304]{1,0:T(8,128)(2,1)S(1)}, u32[]{:S(2)}) copy-start(bf16[384,2304]{1,0:T(8,128)(2,1)S(1)} %get-tuple-element.148.refs_2_) | copy-start | bytes 5308420
  237.1 17.8 %collective-permute-start.30 = (bf16[384,768]{1,0:T(8,128)(2,1)S(1)}, bf16[384,768]{1,0:T(8,128)(2,1)S(1)}, u32[]{:S(2)}, u32[]{:S(2)}) collective-permute-start(bf16[384,768]{1,0:T(8,128)(2,1)S(1)} %get-tuple-element.128), channel_id=1, source_target_pairs={{16,0},{17,1},{18,2},{19,3},{20,4},{21,5},{22,6},{23,7},{24,8},{25... | collective-permute-start | bytes 1769480 | tf_op jit(solution)/shard_map/ppermute | solution.py:785
  271.2 15.9 %collective-permute-start.31 = (bf16[2,4,192,768]{3,2,0,1:T(8,128)(2,1)}, bf16[2,4,192,768]{3,2,0,1:T(8,128)(2,1)}, u32[]{:S(2)}, u32[]{:S(2)}) collective-permute-start(bf16[2,4,192,768]{3,2,0,1:T(8,128)(2,1)} %copy.91), channel_id=1, source_target_pairs={{0,1},{1,0},{2,3},{3,2},{4,5},{5,4},{6,7},{7,6},{8,9},{9,8},{10,11... | collective-permute-start | bytes 7077896 | tf_op jit(solution)/shard_map/ppermute | solution.py:675
  279.8 39.8 %collective-permute-start.36 = (bf16[2,4,48,3072]{3,2,1,0:T(8,128)(2,1)}, bf16[2,4,48,3072]{3,2,1,0:T(8,128)(2,1)}, u32[]{:S(2)}, u32[]{:S(2)}) collective-permute-start(bf16[2,4,48,3072]{3,2,1,0:T(8,128)(2,1)} %get-tuple-element.156), channel_id=1, source_target_pairs={{0,1},{1,0},{2,3},{3,2},{4,5},{5,4},{6,7},{7,6},{8,9},{9,8},{10,11... | collective-permute-start | bytes 7077896 | tf_op jit(solution)/shard_map/ppermute | solution.py:675
  286.1 17.4 %slice-start.2 = ((s8[4915200]{0:T(1024)(128)(4,1)}), s8[720896]{0:T(1024)(128)(4,1)S(1)}, s32[]{:S(2)}) async-start(s8[4915200]{0:T(1024)(128)(4,1)} %bitcast.231), calls=%async_computation.2 | async-start | bytes 1441792
  287.1 16.4 %slice-start.3 = ((s8[4915200]{0:T(1024)(128)(4,1)}), s8[4194304]{0:T(1024)(128)(4,1)S(1)}, s32[]{:S(2)}) async-start(s8[4915200]{0:T(1024)(128)(4,1)} %bitcast.231), calls=%async_computation.3 | async-start | bytes 8388608
  287.1 16.4 %copy-start.17 = (bf16[384,2304]{1,0:T(8,128)(2,1)S(1)}, bf16[384,2304]{1,0:T(8,128)(2,1)}, u32[]{:S(2)}) copy-start(bf16[384,2304]{1,0:T(8,128)(2,1)} %copy-done.16) | copy-start | bytes 5308420
  291.5 34.0 %collective-permute-start.35 = (bf16[2,192,768]{2,1,0:T(8,128)(2,1)}, bf16[2,192,768]{2,1,0:T(8,128)(2,1)}, u32[]{:S(2)}, u32[]{:S(2)}) collective-permute-start(bf16[2,192,768]{2,1,0:T(8,128)(2,1)} %get-tuple-element.189.refs_12_), channel_id=1, source_target_pairs={{12,4},{13,5},{14,6},{15,7},{28,20},{29,21},{30,22},{31,23}} | collective-permute-start | bytes 1769480 | tf_op jit(solution)/shard_map/ppermute | solution.py:681
  294.3 31.3 %collective-permute-start.34 = (bf16[2,192,768]{2,1,0:T(8,128)(2,1)}, bf16[2,192,768]{2,1,0:T(8,128)(2,1)}, u32[]{:S(2)}, u32[]{:S(2)}) collective-permute-start(bf16[2,192,768]{2,1,0:T(8,128)(2,1)} %get-tuple-element.175.refs_10_), channel_id=1, source_target_pairs={{8,4},{9,5},{10,6},{11,7},{12,8},{13,9},{14,10},{15,11},{24,20},{2... | collective-permute-start | bytes 1769480 | tf_op jit(solution)/shard_map/ppermute | solution.py:681
  295.9 29.7 %collective-permute-start.33 = (bf16[2,192,768]{2,1,0:T(8,128)(2,1)}, bf16[2,192,768]{2,1,0:T(8,128)(2,1)}, u32[]{:S(2)}, u32[]{:S(2)}) collective-permute-start(bf16[2,192,768]{2,1,0:T(8,128)(2,1)} %get-tuple-element.190.refs_11_), channel_id=1, source_target_pairs={{0,8},{1,9},{2,10},{3,11},{16,24},{17,25},{18,26},{19,27}} | collective-permute-start | bytes 1769480 | tf_op jit(solution)/shard_map/ppermute | solution.py:681
  301.4 24.7 %collective-permute-start.32 = (bf16[2,192,768]{2,1,0:T(8,128)(2,1)}, bf16[2,192,768]{2,1,0:T(8,128)(2,1)}, u32[]{:S(2)}, u32[]{:S(2)}) collective-permute-start(bf16[2,192,768]{2,1,0:T(8,128)(2,1)} %get-tuple-element.176.refs_9_), channel_id=1, source_target_pairs={{0,4},{1,5},{2,6},{3,7},{4,8},{5,9},{6,10},{7,11},{16,20},{17,21},... | collective-permute-start | bytes 1769480 | tf_op jit(solution)/shard_map/ppermute | solution.py:681
  337.4 30.4 %collective-permute-start.37 = (bf16[2,4,48,3200]{3,2,1,0:T(8,128)(2,1)}, bf16[2,4,48,3200]{3,2,1,0:T(8,128)(2,1)}, u32[]{:S(2)}, u32[]{:S(2)}) collective-permute-start(bf16[2,4,48,3200]{3,2,1,0:T(8,128)(2,1)} %get-tuple-element.158), channel_id=1, source_target_pairs={{0,1},{1,0},{2,3},{3,2},{4,5},{5,4},{6,7},{7,6},{8,9},{9,8},{10,11... | collective-permute-start | bytes 7372808 | tf_op jit(solution)/shard_map/ppermute | solution.py:675
  337.5 28.7 %collective-permute-start.45 = (bf16[4,48,3072]{2,1,0:T(8,128)(2,1)}, bf16[4,48,3072]{2,1,0:T(8,128)(2,1)}, u32[]{:S(2)}, u32[]{:S(2)}) collective-permute-start(bf16[4,48,3072]{2,1,0:T(8,128)(2,1)} %fusion.3.refs_11_), channel_id=1, source_target_pairs={{0,2},{1,3},{2,0},{3,1},{4,6},{5,7},{6,4},{7,5},{8,10},{9,11},{10,... | collective-permute-start | bytes 3538952 | tf_op jit(solution)/shard_map/ppermute | solution.py:678
  339.8 26.3 %copy-start.46 = (f32[2,4,48,3072]{3,2,1,0:T(8,128)S(1)}, f32[2,4,48,3072]{3,2,1,0:T(8,128)}, u32[]{:S(2)}) copy-start(f32[2,4,48,3072]{3,2,1,0:T(8,128)} %copy-done.45) | copy-start | bytes 14155780
  341.5 35.6 %collective-permute-start.53 = (bf16[2,192,768]{2,1,0:T(8,128)(2,1)S(1)}, bf16[2,192,768]{2,1,0:T(8,128)(2,1)S(1)}, u32[]{:S(2)}, u32[]{:S(2)}) collective-permute-start(bf16[2,192,768]{2,1,0:T(8,128)(2,1)S(1)} %copy-done.24), channel_id=1, source_target_pairs={{4,0},{5,1},{6,2},{7,3},{8,4},{9,5},{10,6},{11,7},{12,8},{13,9},{1... | collective-permute-start | bytes 1769480 | tf_op jit(solution)/shard_map/ppermute | solution.py:681
  343.1 34.8 %collective-permute-start.52 = (bf16[2,192,768]{2,1,0:T(8,128)(2,1)S(1)}, bf16[2,192,768]{2,1,0:T(8,128)(2,1)S(1)}, u32[]{:S(2)}, u32[]{:S(2)}) collective-permute-start(bf16[2,192,768]{2,1,0:T(8,128)(2,1)S(1)} %copy-done.22), channel_id=1, source_target_pairs={{0,4},{1,5},{2,6},{3,7},{4,8},{5,9},{6,10},{7,11},{8,12},{9,13},{1... | collective-permute-start | bytes 1769480 | tf_op jit(solution)/shard_map/ppermute | solution.py:681
  370.1 28.7 %collective-permute-start.38 = (bf16[4,48,3200]{2,1,0:T(8,128)(2,1)S(1)}, bf16[4,48,3200]{2,1,0:T(8,128)(2,1)S(1)}, u32[]{:S(2)}, u32[]{:S(2)}) collective-permute-start(bf16[4,48,3200]{2,1,0:T(8,128)(2,1)S(1)} %fusion.2), channel_id=1, source_target_pairs={{0,2},{1,3},{2,0},{3,1},{4,6},{5,7},{6,4},{7,5},{8,10},{9,11},{10,... | collective-permute-start | bytes 3686408 | tf_op jit(solution)/shard_map/ppermute | solution.py:678
  371.1 28.9 %collective-permute-start.47 = (bf16[1,48,3072]{2,1,0:T(8,128)(2,1)S(1)}, bf16[1,48,3072]{2,1,0:T(8,128)(2,1)S(1)}, u32[]{:S(2)}, u32[]{:S(2)}) collective-permute-start(bf16[1,48,3072]{2,1,0:T(8,128)(2,1)S(1)} %get-tuple-element.199), channel_id=1, source_target_pairs={{0,8},{1,9},{2,10},{3,11},{16,24},{17,25},{18,26},{19,27}} | collective-permute-start | bytes 884744 | tf_op jit(solution)/shard_map/ppermute | solution.py:681
  375.8 28.9 %collective-permute-start.46 = (bf16[1,48,3072]{2,1,0:T(8,128)(2,1)S(1)}, bf16[1,48,3072]{2,1,0:T(8,128)(2,1)S(1)}, u32[]{:S(2)}, u32[]{:S(2)}) collective-permute-start(bf16[1,48,3072]{2,1,0:T(8,128)(2,1)S(1)} %get-tuple-element.187), channel_id=1, source_target_pairs={{0,4},{1,5},{2,6},{3,7},{4,8},{5,9},{6,10},{7,11},{16,20},{17,21},... | collective-permute-start | bytes 884744 | tf_op jit(solution)/shard_map/ppermute | solution.py:681
  377.2 28.9 %collective-permute-start.50 = (bf16[1,48,3072]{2,1,0:T(8,128)(2,1)S(1)}, bf16[1,48,3072]{2,1,0:T(8,128)(2,1)S(1)}, u32[]{:S(2)}, u32[]{:S(2)}) collective-permute-start(bf16[1,48,3072]{2,1,0:T(8,128)(2,1)S(1)} %get-tuple-element.200), channel_id=1, source_target_pairs={{12,4},{13,5},{14,6},{15,7},{28,20},{29,21},{30,22},{31,23}} | collective-permute-start | bytes 884744 | tf_op jit(solution)/shard_map/ppermute | solution.py:681
  377.9 28.9 %collective-permute-start.49 = (bf16[1,48,3072]{2,1,0:T(8,128)(2,1)S(1)}, bf16[1,48,3072]{2,1,0:T(8,128)(2,1)S(1)}, u32[]{:S(2)}, u32[]{:S(2)}) collective-permute-start(bf16[1,48,3072]{2,1,0:T(8,128)(2,1)S(1)} %get-tuple-element.188), channel_id=1, source_target_pairs={{8,4},{9,5},{10,6},{11,7},{12,8},{13,9},{14,10},{15,11},{24,20},{2... | collective-permute-start | bytes 884744 | tf_op jit(solution)/shard_map/ppermute | solution.py:681
  398.8 8.9 %collective-permute-start.54 = (bf16[192,768]{1,0:T(8,128)(2,1)S(1)}, bf16[192,768]{1,0:T(8,128)(2,1)S(1)}, u32[]{:S(2)}, u32[]{:S(2)}) collective-permute-start(bf16[192,768]{1,0:T(8,128)(2,1)S(1)} %fusion.13), channel_id=1, source_target_pairs={{0,2},{1,3},{2,0},{3,1},{4,6},{5,7},{6,4},{7,5},{8,10},{9,11},{10,... | collective-permute-start | bytes 884744 | tf_op jit(solution)/shard_map/ppermute | solution.py:678
  400.0 12.4 %collective-permute-start.40 = (bf16[1,48,3200]{2,1,0:T(8,128)(2,1)S(1)}, bf16[1,48,3200]{2,1,0:T(8,128)(2,1)S(1)}, u32[]{:S(2)}, u32[]{:S(2)}) collective-permute-start(bf16[1,48,3200]{2,1,0:T(8,128)(2,1)S(1)} %get-tuple-element.197), channel_id=1, source_target_pairs={{0,8},{1,9},{2,10},{3,11},{16,24},{17,25},{18,26},{19,27}} | collective-permute-start | bytes 921608 | tf_op jit(solution)/shard_map/ppermute | solution.py:681
  404.7 14.3 %collective-permute-start.39 = (bf16[1,48,3200]{2,1,0:T(8,128)(2,1)S(1)}, bf16[1,48,3200]{2,1,0:T(8,128)(2,1)S(1)}, u32[]{:S(2)}, u32[]{:S(2)}) collective-permute-start(bf16[1,48,3200]{2,1,0:T(8,128)(2,1)S(1)} %get-tuple-element.179), channel_id=1, source_target_pairs={{0,4},{1,5},{2,6},{3,7},{4,8},{5,9},{6,10},{7,11},{16,20},{17,21},... | collective-permute-start | bytes 921608 | tf_op jit(solution)/shard_map/ppermute | solution.py:681
  406.1 12.9 %collective-permute-start.43 = (bf16[1,48,3200]{2,1,0:T(8,128)(2,1)S(1)}, bf16[1,48,3200]{2,1,0:T(8,128)(2,1)S(1)}, u32[]{:S(2)}, u32[]{:S(2)}) collective-permute-start(bf16[1,48,3200]{2,1,0:T(8,128)(2,1)S(1)} %get-tuple-element.198), channel_id=1, source_target_pairs={{12,4},{13,5},{14,6},{15,7},{28,20},{29,21},{30,22},{31,23}} | collective-permute-start | bytes 921608 | tf_op jit(solution)/shard_map/ppermute | solution.py:681
  406.8 12.2 %collective-permute-start.42 = (bf16[1,48,3200]{2,1,0:T(8,128)(2,1)S(1)}, bf16[1,48,3200]{2,1,0:T(8,128)(2,1)S(1)}, u32[]{:S(2)}, u32[]{:S(2)}) collective-permute-start(bf16[1,48,3200]{2,1,0:T(8,128)(2,1)S(1)} %get-tuple-element.180), channel_id=1, source_target_pairs={{8,4},{9,5},{10,6},{11,7},{12,8},{13,9},{14,10},{15,11},{24,20},{2... | collective-permute-start | bytes 921608 | tf_op jit(solution)/shard_map/ppermute | solution.py:681
  407.7 19.9 %collective-permute-start.51 = (bf16[1,48,3072]{2,1,0:T(8,128)(2,1)S(1)}, bf16[1,48,3072]{2,1,0:T(8,128)(2,1)S(1)}, u32[]{:S(2)}, u32[]{:S(2)}) collective-permute-start(bf16[1,48,3072]{2,1,0:T(8,128)(2,1)S(1)} %get-tuple-element.186), channel_id=1, source_target_pairs={{4,0},{5,1},{6,2},{7,3},{8,4},{9,5},{10,6},{11,7},{12,8},{13,9},{1... | collective-permute-start | bytes 884744 | tf_op jit(solution)/shard_map/ppermute | solution.py:681
  412.4 15.1 %collective-permute-start.48 = (bf16[1,48,3072]{2,1,0:T(8,128)(2,1)S(1)}, bf16[1,48,3072]{2,1,0:T(8,128)(2,1)S(1)}, u32[]{:S(2)}, u32[]{:S(2)}) collective-permute-start(bf16[1,48,3072]{2,1,0:T(8,128)(2,1)S(1)} %get-tuple-element.185), channel_id=1, source_target_pairs={{0,4},{1,5},{2,6},{3,7},{4,8},{5,9},{6,10},{7,11},{8,12},{9,13},{1... | collective-permute-start | bytes 884744 | tf_op jit(solution)/shard_map/ppermute | solution.py:681
  419.2 13.7 %collective-permute-start.44 = (bf16[1,48,3200]{2,1,0:T(8,128)(2,1)S(1)}, bf16[1,48,3200]{2,1,0:T(8,128)(2,1)S(1)}, u32[]{:S(2)}, u32[]{:S(2)}) collective-permute-start(bf16[1,48,3200]{2,1,0:T(8,128)(2,1)S(1)} %get-tuple-element.178), channel_id=1, source_target_pairs={{4,0},{5,1},{6,2},{7,3},{8,4},{9,5},{10,6},{11,7},{12,8},{13,9},{1... | collective-permute-start | bytes 921608 | tf_op jit(solution)/shard_map/ppermute | solution.py:681
  420.5 13.6 %collective-permute-start.41 = (bf16[1,48,3200]{2,1,0:T(8,128)(2,1)S(1)}, bf16[1,48,3200]{2,1,0:T(8,128)(2,1)S(1)}, u32[]{:S(2)}, u32[]{:S(2)}) collective-permute-start(bf16[1,48,3200]{2,1,0:T(8,128)(2,1)S(1)} %get-tuple-element.177), channel_id=1, source_target_pairs={{0,4},{1,5},{2,6},{3,7},{4,8},{5,9},{6,10},{7,11},{8,12},{9,13},{1... | collective-permute-start | bytes 921608 | tf_op jit(solution)/shard_map/ppermute | solution.py:681
  (49 other events, 257.0 us)
